TPU v7x, 32 devices: a whole 2x2x4 slice. The times are simulated.
32 devices in a mesh: dp: 4 (over z), ctx: 4 (over x, core), tensor: 2 (over y).
Axes of the slice: x: 2, y: 2, z: 4, core: 2. Of those that a mesh axis runs over, the one named last changes fastest.
Arguments:
- inputs: bfloat16 [8, 1024, 2048], P('dp', 'ctx', 'tensor'), may hold values from -6 to 6
- cotangent: bfloat16 [8, 1024, 2048], P('dp', 'ctx', 'tensor'), may hold values from -6 to 6
- lengths: int32 [8], replicated, may hold values from 512 to 1024, as said below
- deal_order: int32 [8], replicated, may hold values from 0 to 7, each once
- query_weight: bfloat16 [2048, 2048], P('ctx', 'tensor'), may hold values from -0.125 to 0.125
- key_weight: bfloat16 [2048, 512], P('ctx', 'tensor'), may hold values from -0.125 to 0.125
- value_weight: bfloat16 [2048, 512], P('ctx', 'tensor'), may hold values from -0.125 to 0.125
- output_weight: bfloat16 [2048, 2048], P('tensor', 'ctx'), may hold values from -2 to 2
- gate_weight: bfloat16 [2048, 8192], P('ctx', 'tensor'), may hold values from -0.125 to 0.125
- up_weight: bfloat16 [2048, 8192], P('ctx', 'tensor'), may hold values from -0.125 to 0.125
- down_weight: bfloat16 [8192, 2048], P('tensor', 'ctx'), may hold values from -0.0625 to 0.0625
- attention_gain: float32 [2048], P('tensor'), may hold values from 0.1 to 1.9
- feedforward_gain: float32 [2048], P('tensor'), may hold values from 0.1 to 1.9
Outputs:
- outputs: bfloat16 [8, 1024, 2048], P('dp', 'ctx', 'tensor')
- input_grad: bfloat16 [8, 1024, 2048], P('dp', 'ctx', 'tensor')
- query_grad: float32 [2048, 2048], P(('dp', 'ctx'), 'tensor')
- key_grad: float32 [2048, 512], P(('dp', 'ctx'), 'tensor')
- value_grad: float32 [2048, 512], P(('dp', 'ctx'), 'tensor')
- output_grad: float32 [2048, 2048], P('tensor', ('dp', 'ctx'))
- gate_grad: float32 [2048, 8192], P(('dp', 'ctx'), 'tensor')
- up_grad: float32 [2048, 8192], P(('dp', 'ctx'), 'tensor')
- down_grad: float32 [8192, 2048], P('tensor', ('dp', 'ctx'))
- attention_gain_grad: float32 [2048], P('tensor')
- feedforward_gain_grad: float32 [2048], P('tensor')
Inputs may be any that keep to these rules, and one draw needn't show every extreme that they name: `lengths`: every sequence has at least 512 tokens, and some sequence has exactly 1024.
All inputs are finite; a program needn't handle non-finite values.
Results may differ from a plain program's by a relative error of at most 0.02.
Values may be sent and summed in bfloat16 or wider, within the bound.
No kernel may reach another device: no remote copies, remote signals or barrier semaphores. Data moves between devices by JAX's collectives and lax.ppermute only.
A program may use at most 320 MiB of HBM per device.

v0:
```python
import jax
import jax.numpy as jnp
from jax import lax
from jax.sharding import PartitionSpec as P

HD = 64


EPS = 1e-05
NEGATIVE = -1e30


def inverse_frequency(head_size):
    exponent = jnp.arange(0, head_size, 2, dtype=jnp.int32).astype(jnp.float32) / head_size
    plain = 1.0 / jnp.power(jnp.float32(500000.0), exponent)
    factor = 32.0
    old_context = 8192.0
    wavelength = 2.0 * jnp.pi / plain
    smooth = (old_context / wavelength - 1.0) / (4.0 - 1.0)
    scaled = jnp.where(wavelength > old_context, plain / factor, plain)
    middle = (wavelength <= old_context) & (wavelength >= old_context / 4.0)
    scaled = jnp.where(middle, (1.0 - smooth) * plain / factor + smooth * plain, scaled)
    return scaled


def rotate(values, cosine, sine):
    half = values.shape[-1] // 2
    first = values[..., :half]
    second = values[..., half:]
    return jnp.concatenate(
        [first * cosine - second * sine, second * cosine + first * sine], axis=-1
    )


def feature_sum(values):
    return lax.psum(jnp.sum(values, axis=1), "tensor")


def whole_rows(values):
    return lax.all_gather(values, "tensor", axis=1, tiled=True)


def share_rows(values):
    return lax.psum_scatter(
        values.astype(jnp.bfloat16), "tensor", scatter_dimension=1, tiled=True
    ).astype(jnp.float32)


def norm_forward(values, gain, width):
    inverse = lax.rsqrt(feature_sum(values * values) / width + EPS)[:, None]
    return (values * inverse * gain, inverse)


def norm_backward(grad, values, inverse, gain, width):
    weighted = grad * gain
    total = feature_sum(weighted * values)[:, None]
    back = inverse * weighted - values * (inverse * inverse * inverse) * total / width
    return (back, jnp.sum(grad * values * inverse, axis=0))


def causal_mask(query_pos, start, count, length):
    key_pos = start + jnp.arange(count, dtype=jnp.int32)
    allowed = (key_pos[None, :] <= query_pos[:, None]) & (key_pos[None, :] < length)
    return allowed[:, None, None, :]


def attend_piece(carry, pieces, start, query, query_pos, length):
    top, total, accum = carry
    keys, values = pieces
    count = keys.shape[0]
    key_heads = query.shape[1]
    head_size = query.shape[3]
    keys = keys.reshape(count, key_heads, head_size)
    values = values.reshape(count, key_heads, head_size)
    scores = jnp.einsum(
        "tkgd,pkd->tkgp", query, keys, preferred_element_type=jnp.float32
    ) * head_size ** (-0.5)
    allowed = causal_mask(query_pos, start, count, length)
    masked = jnp.where(allowed, scores, NEGATIVE)
    fresh = jnp.maximum(top, jnp.max(masked, axis=3))
    weights = jnp.where(allowed, jnp.exp(masked - fresh[..., None]), 0.0)
    decay = jnp.exp(top - fresh)
    total = total * decay + jnp.sum(weights, axis=3)
    accum = accum * decay[..., None] + jnp.einsum(
        "tkgp,pkd->tkgd", weights.astype(jnp.bfloat16), values, preferred_element_type=jnp.float32
    )
    return (fresh, total, accum)


def attend_back(carry, pieces, start, query, query_pos, length, log_total, grad_out, delta):
    grad_query, key_sums, value_sums = carry
    keys, values = pieces
    count = keys.shape[0]
    key_heads = query.shape[1]
    head_size = query.shape[3]
    scale = head_size ** (-0.5)
    keys = keys.reshape(count, key_heads, head_size)
    values = values.reshape(count, key_heads, head_size)
    scores = jnp.einsum("tkgd,pkd->tkgp", query, keys, preferred_element_type=jnp.float32) * scale
    allowed = causal_mask(query_pos, start, count, length)
    masked = jnp.where(allowed, scores, NEGATIVE)
    probs = jnp.where(allowed, jnp.exp(masked - log_total[..., None]), 0.0)
    grad_probs = jnp.einsum("tkgd,pkd->tkgp", grad_out, values, preferred_element_type=jnp.float32)
    grad_scores = (probs * (grad_probs - delta[..., None]) * scale).astype(jnp.bfloat16)
    grad_query = grad_query + jnp.einsum(
        "tkgp,pkd->tkgd", grad_scores, keys, preferred_element_type=jnp.float32
    )
    key_part = jnp.einsum(
        "tkgp,tkgd->pkd", grad_scores, query, preferred_element_type=jnp.float32
    ).reshape(count, -1)
    value_part = jnp.einsum(
        "tkgp,tkgd->pkd", probs.astype(jnp.bfloat16), grad_out, preferred_element_type=jnp.float32
    ).reshape(count, -1)
    key_sums = lax.dynamic_update_slice_in_dim(
        key_sums, lax.dynamic_slice_in_dim(key_sums, start, count, 0) + key_part, start, 0
    )
    value_sums = lax.dynamic_update_slice_in_dim(
        value_sums, lax.dynamic_slice_in_dim(value_sums, start, count, 0) + value_part, start, 0
    )
    return (grad_query, key_sums, value_sums)


def local_fold(function, init, arrays, piece_rows):

    def advance(index, carry):
        start = (index * piece_rows).astype(jnp.int32)
        pieces = tuple((lax.dynamic_slice_in_dim(item, start, piece_rows, 1) for item in arrays))
        return function(carry, pieces, start)

    return lax.fori_loop(0, arrays[0].shape[1] // piece_rows, advance, init)


def matmul(left, right):
    return jnp.dot(left, right, preferred_element_type=jnp.float32)


def per_device(
    inputs,
    cotangent,
    lengths,
    deal_order,
    query_weight,
    key_weight,
    value_weight,
    output_weight,
    gate_weight,
    up_weight,
    down_weight,
    attention_gain,
    feedforward_gain,
):
    slices = inputs.shape[0]
    rows = inputs.shape[1]
    half_width = inputs.shape[2]
    width = half_width * lax.axis_size("tensor")
    group_count = lax.axis_size("dp")
    span = rows * lax.axis_size("ctx")
    all_rows = slices * rows
    group = lax.axis_index("dp")
    place = lax.axis_index("ctx")
    sequences = lengths.shape[0]
    slot_ids = lax.dynamic_slice_in_dim(deal_order, group * slices, slices)
    matches = jnp.arange(sequences, dtype=jnp.int32)[None, :] == slot_ids[:, None]
    slot_lengths = jnp.sum(jnp.where(matches, lengths[None, :], 0), axis=1)
    scale = (
        jnp.sum(lengths).astype(jnp.float32)
        / group_count
        / jnp.sum(slot_lengths).astype(jnp.float32)
    )
    empty = jnp.zeros_like(inputs)
    carry = (empty, empty)
    pieces = (
        lax.all_gather(inputs, "dp", axis=0, tiled=True),
        lax.all_gather(cotangent, "dp", axis=0, tiled=True),
    )
    start = jnp.int32(0)
    count = pieces[0].shape[0]
    chosen = []
    for which in range(2):
        column = []
        for slot in range(slices):
            sequence_id = slot_ids[slot]
            inside = (sequence_id >= start) & (sequence_id < start + count)
            offset = jnp.clip(sequence_id, 0, count - 1)
            fetched = lax.dynamic_index_in_dim(pieces[which], offset, 0, keepdims=False)
            column.append(jnp.where(inside, fetched, carry[which][slot]))
        chosen.append(jnp.stack(column))
    packed = chosen[0]
    packed_grad = chosen[1]
    query_full, key_full, value_full, gate_full, up_full, output_full, down_full = (
        lax.all_gather(query_weight, "ctx", axis=0, tiled=True),
        lax.all_gather(key_weight, "ctx", axis=0, tiled=True),
        lax.all_gather(value_weight, "ctx", axis=0, tiled=True),
        lax.all_gather(gate_weight, "ctx", axis=0, tiled=True),
        lax.all_gather(up_weight, "ctx", axis=0, tiled=True),
        lax.all_gather(output_weight, "ctx", axis=1, tiled=True),
        lax.all_gather(down_weight, "ctx", axis=1, tiled=True),
    )
    head_size = HD
    key_heads = key_weight.shape[1] // head_size
    ratio = query_weight.shape[1] // key_weight.shape[1]
    query_pos = place * rows + jnp.arange(rows, dtype=jnp.int32)
    angle = query_pos.astype(jnp.float32)[:, None] * inverse_frequency(head_size)[None, :]
    cosine = jnp.tile(jnp.cos(angle), (slices, 1))
    sine = jnp.tile(jnp.sin(angle), (slices, 1))
    wide_cosine = cosine[:, None, None, :]
    wide_sine = sine[:, None, None, :]
    narrow_cosine = cosine[:, None, :]
    narrow_sine = sine[:, None, :]
    valid_rows = (query_pos[None, :] < slot_lengths[:, None]).reshape(all_rows)
    source = packed.reshape(all_rows, half_width).astype(jnp.float32)
    normed, inverse_one = norm_forward(source, attention_gain, width)
    normed_b = whole_rows(normed.astype(jnp.bfloat16))
    query_rot = rotate(
        matmul(normed_b, query_full).reshape(all_rows, key_heads, ratio, head_size),
        wide_cosine,
        wide_sine,
    ).astype(jnp.bfloat16)
    query_slots = query_rot.reshape(slices, rows, key_heads, ratio, head_size)
    key_rot = (
        rotate(
            matmul(normed_b, key_full).reshape(all_rows, key_heads, head_size),
            narrow_cosine,
            narrow_sine,
        )
        .reshape(slices, rows, -1)
        .astype(jnp.bfloat16)
    )
    value_b = matmul(normed_b, value_full).astype(jnp.bfloat16).reshape(slices, rows, -1)
    fold_init = (
        jnp.full((slices, rows, key_heads, ratio), NEGATIVE, jnp.float32),
        jnp.zeros((slices, rows, key_heads, ratio), jnp.float32),
        jnp.zeros((slices, rows, key_heads, ratio, head_size), jnp.float32),
    )

    def forward_all(carry, pieces, start):
        tops, totals, accums = carry
        results = [
            attend_piece(
                (tops[slot], totals[slot], accums[slot]),
                (pieces[0][slot], pieces[1][slot]),
                start,
                query_slots[slot],
                query_pos,
                slot_lengths[slot],
            )
            for slot in range(slices)
        ]
        return tuple((jnp.stack([item[which] for item in results]) for which in range(3)))

    kept = (
        lax.all_gather(key_rot, "ctx", axis=1, tiled=True),
        lax.all_gather(value_b, "ctx", axis=1, tiled=True),
    )
    top, total, accum = local_fold(forward_all, fold_init, kept, rows)
    attended = accum / total[..., None]
    attended_b = attended.reshape(all_rows, -1).astype(jnp.bfloat16)
    hidden = source + share_rows(matmul(attended_b, output_full))
    normed_two, inverse_two = norm_forward(hidden, feedforward_gain, width)
    normed_two_b = whole_rows(normed_two.astype(jnp.bfloat16))
    gate = matmul(normed_two_b, gate_full)
    upward = matmul(normed_two_b, up_full)
    sigmoid = jax.nn.sigmoid(gate)
    active_b = (gate * sigmoid * upward).astype(jnp.bfloat16)
    result = hidden + share_rows(matmul(active_b, down_full))
    out_stack = (
        jnp.where(valid_rows[:, None], result, 0.0)
        .astype(jnp.bfloat16)
        .reshape(slices, rows, half_width)
    )
    target = (
        packed_grad.reshape(all_rows, half_width).astype(jnp.float32) * valid_rows[:, None] * scale
    )
    target_b = whole_rows(target.astype(jnp.bfloat16))
    grad_active = matmul(target_b, down_full.T)
    down_sum = matmul(active_b.T, target_b)
    grad_gate = (grad_active * upward * sigmoid * (1.0 + gate * (1.0 - sigmoid))).astype(
        jnp.bfloat16
    )
    grad_up = (grad_active * gate * sigmoid).astype(jnp.bfloat16)
    gate_sum = matmul(normed_two_b.T, grad_gate)
    up_sum = matmul(normed_two_b.T, grad_up)
    grad_normed_two = share_rows(matmul(grad_gate, gate_full.T) + matmul(grad_up, up_full.T))
    back_two, gain_second = norm_backward(
        grad_normed_two, hidden, inverse_two, feedforward_gain, width
    )
    grad_hidden = target + back_two
    grad_hidden_b = whole_rows(grad_hidden.astype(jnp.bfloat16))
    grad_attended = (
        matmul(grad_hidden_b, output_full.T)
        .astype(jnp.bfloat16)
        .reshape(slices, rows, key_heads, ratio, head_size)
    )
    output_sum = matmul(attended_b.T, grad_hidden_b)
    delta = jnp.sum(grad_attended.astype(jnp.float32) * attended, axis=4)
    log_total = top + jnp.log(total)
    back_init = (
        jnp.zeros((slices, rows, key_heads, ratio, head_size), jnp.float32),
        jnp.zeros((slices, span, key_heads * head_size), jnp.float32),
        jnp.zeros((slices, span, key_heads * head_size), jnp.float32),
    )

    def backward_all(carry, pieces, start):
        grads, key_acc, value_acc = carry
        results = [
            attend_back(
                (grads[slot], key_acc[slot], value_acc[slot]),
                (pieces[0][slot], pieces[1][slot]),
                start,
                query_slots[slot],
                query_pos,
                slot_lengths[slot],
                log_total[slot],
                grad_attended[slot],
                delta[slot],
            )
            for slot in range(slices)
        ]
        return tuple((jnp.stack([item[which] for item in results]) for which in range(3)))

    grad_query, key_sums, value_sums = local_fold(backward_all, back_init, kept, rows)
    key_grad, value_grad = (
        lax.psum_scatter(
            key_sums.astype(jnp.bfloat16), "ctx", scatter_dimension=1, tiled=True
        ).astype(jnp.float32),
        lax.psum_scatter(
            value_sums.astype(jnp.bfloat16), "ctx", scatter_dimension=1, tiled=True
        ).astype(jnp.float32),
    )
    query_back = (
        rotate(grad_query.reshape(all_rows, key_heads, ratio, head_size), wide_cosine, -wide_sine)
        .reshape(all_rows, -1)
        .astype(jnp.bfloat16)
    )
    key_back = (
        rotate(key_grad.reshape(all_rows, key_heads, head_size), narrow_cosine, -narrow_sine)
        .reshape(all_rows, -1)
        .astype(jnp.bfloat16)
    )
    value_back = value_grad.reshape(all_rows, -1).astype(jnp.bfloat16)
    query_sum = matmul(normed_b.T, query_back)
    key_sum = matmul(normed_b.T, key_back)
    value_sum = matmul(normed_b.T, value_back)
    grad_normed = share_rows(
        matmul(query_back, query_full.T)
        + matmul(key_back, key_full.T)
        + matmul(value_back, value_full.T)
    )
    back_one, gain_first = norm_backward(grad_normed, source, inverse_one, attention_gain, width)
    grad_stack = (grad_hidden + back_one).astype(jnp.bfloat16).reshape(slices, rows, half_width)
    combined = jnp.concatenate(
        [out_stack.astype(jnp.float32), grad_stack.astype(jnp.float32)], axis=2
    )
    sequence_ids = jnp.arange(slices * lax.axis_size("dp"), dtype=jnp.int32)
    term = jnp.zeros((slices * lax.axis_size("dp"),) + combined.shape[1:], jnp.float32)
    for slot in range(slices):
        hits = sequence_ids == slot_ids[slot]
        term = term + jnp.where(hits[:, None, None], combined[slot][None], 0.0)
    returned = lax.psum_scatter(
        term.astype(jnp.bfloat16), "dp", scatter_dimension=0, tiled=True
    ).astype(jnp.float32)
    outputs = returned[:, :, :half_width].astype(jnp.bfloat16)
    input_grad = returned[:, :, half_width:].astype(jnp.bfloat16)
    query_out, key_out, value_out, gate_out, up_out, output_out, down_out = (
        lax.psum_scatter(query_sum, ("dp", "ctx"), scatter_dimension=0, tiled=True),
        lax.psum_scatter(key_sum, ("dp", "ctx"), scatter_dimension=0, tiled=True),
        lax.psum_scatter(value_sum, ("dp", "ctx"), scatter_dimension=0, tiled=True),
        lax.psum_scatter(gate_sum, ("dp", "ctx"), scatter_dimension=0, tiled=True),
        lax.psum_scatter(up_sum, ("dp", "ctx"), scatter_dimension=0, tiled=True),
        lax.psum_scatter(output_sum, ("dp", "ctx"), scatter_dimension=1, tiled=True),
        lax.psum_scatter(down_sum, ("dp", "ctx"), scatter_dimension=1, tiled=True),
    )
    gain_first_out, gain_second_out = lax.psum((gain_first, gain_second), ("dp", "ctx"))
    return (
        outputs,
        input_grad,
        query_out,
        key_out,
        value_out,
        output_out,
        gate_out,
        up_out,
        down_out,
        gain_first_out,
        gain_second_out,
    )


def solution(mesh):
    return jax.shard_map(
        per_device,
        mesh=mesh,
        in_specs=(
            P("dp", "ctx", "tensor"),
            P("dp", "ctx", "tensor"),
            P(),
            P(),
            P("ctx", "tensor"),
            P("ctx", "tensor"),
            P("ctx", "tensor"),
            P("tensor", "ctx"),
            P("ctx", "tensor"),
            P("ctx", "tensor"),
            P("tensor", "ctx"),
            P("tensor"),
            P("tensor"),
        ),
        out_specs=(
            P("dp", "ctx", "tensor"),
            P("dp", "ctx", "tensor"),
            P(("dp", "ctx"), "tensor"),
            P(("dp", "ctx"), "tensor"),
            P(("dp", "ctx"), "tensor"),
            P("tensor", ("dp", "ctx")),
            P(("dp", "ctx"), "tensor"),
            P(("dp", "ctx"), "tensor"),
            P("tensor", ("dp", "ctx")),
            P("tensor"),
            P("tensor"),
        ),
        check_vma=False,
    )
```

profile of v0, /device:TPU:0, one launch (start us, length us, event | category | flops | bytes accessed | tf_op | source)
XLA Modules:
  0.0 2642.2 jit_solution(10151020839949467872)
XLA Ops:
  13.8 79.3 %all-gather.16.cloned.1.call-done = bf16[8,256,1024]{2,1,0:T(8,128)(2,1)} async-done(((bf16[2,256,1024]{2,1,0:T(8,128)(2,1)}), bf16[8,256,1024]{2,1,0:T(8,128)(2,1)}) %all-gather.16.cloned.1.call-update) | async-done | bytes 4194320 | tf_op jit(solution)/shard_map/all_gather | solution.py:173
  103.7 6.3 all-gather.20.cloned.1.call-done
  109.9 35.3 %all-gather.18.cloned.1.call-done = bf16[512,2048]{1,0:T(8,128)(2,1)} async-done(((bf16[512,1024]{1,0:T(8,128)(2,1)}), bf16[512,2048]{1,0:T(8,128)(2,1)}) %all-gather.18.cloned.1.call-update) | async-done | bytes 2097168 | tf_op jit(solution)/shard_map/all_gather | solution.py:40
  148.9 14.4 all-gather.26.cloned.1.call-done
  168.4 30.9 %all-gather.24.cloned.1.call-done = bf16[2048,1024]{1,0:T(8,128)(2,1)} async-done(((bf16[512,1024]{1,0:T(8,128)(2,1)}), bf16[2048,1024]{1,0:T(8,128)(2,1)}) %all-gather.24.cloned.1.call-update) | async-done | bytes 4194320 | tf_op jit(solution)/shard_map/all_gather | solution.py:191
  206.1 12.1 all-gather.22.cloned.1.call-done
  219.7 17.5 all-gather.28.cloned.1.call-done
  238.8 43.2 %while.36 = (s32[]{:T(128)}, f32[2,256,4,4]{1,3,2,0:T(4,128)S(1)}, f32[2,256,4,4]{1,3,2,0:T(4,128)S(1)}, f32[2,256,4,4,64]{1,4,3,2,0:T(8,128)}, s32[2]{0:T(128)S...) while((s32[]{:T(128)}, f32[2,256,4,4]{1,3,2,0:T(4,128)S(1)}, ...), condition=%wide.region_8.9_spmd.clone, body=%wide.region_3.8_spmd.clone.sunk | while | flops 565953792 | bytes 45716744 | solution.py:130
  282.0 6.5 fusion.129
  289.8 6.2 convolution_convert_fusion
  298.2 57.5 %all-gather.40.cloned.1.call-done = bf16[8,256,1024]{2,1,0:T(8,128)(2,1)} async-done(((bf16[2,256,1024]{2,1,0:T(8,128)(2,1)}), bf16[8,256,1024]{2,1,0:T(8,128)(2,1)}) %all-gather.40.cloned.1.call-update) | async-done | bytes 4194320 | tf_op jit(solution)/shard_map/all_gather | solution.py:174
  358.9 29.7 %reduce-scatter.15.cloned.1.call-done = bf16[512,1024]{1,0:T(8,128)(2,1)} async-done(((bf16[512,2048]{1,0:T(8,128)(2,1)}), bf16[512,1024]{1,0:T(8,128)(2,1)}) %reduce-scatter.15.cloned.1.call-update) | async-done | bytes 1048592 | tf_op jit(solution)/shard_map/reduce_scatter | solution.py:44
  390.3 5.3 psum.43
  399.6 24.4 all-gather.42.cloned.1.call-done
  424.0 107.4 %all-gather.38.cloned.1.call-done = bf16[4096,2048]{1,0:T(8,128)(2,1)} async-done(((bf16[4096,512]{1,0:T(8,128)(2,1)}), bf16[4096,2048]{1,0:T(8,128)(2,1)}) %all-gather.38.cloned.1.call-update) | async-done | bytes 16777232 | tf_op jit(solution)/shard_map/all_gather | solution.py:197
  531.5 15.1 fusion.139
  546.5 20.3 all-gather.32.cloned.1.call-done
  566.8 107.4 %all-gather.34.cloned.1.call-done = bf16[2048,4096]{1,0:T(8,128)(2,1)} async-done(((bf16[512,4096]{1,0:T(8,128)(2,1)}), bf16[2048,4096]{1,0:T(8,128)(2,1)}) %all-gather.34.cloned.1.call-update) | async-done | bytes 16777232 | tf_op jit(solution)/shard_map/all_gather | solution.py:194
  674.3 15.0 fusion.138
  689.3 92.4 %all-gather.36.cloned.1.call-done = bf16[2048,4096]{1,0:T(8,128)(2,1)} async-done(((bf16[512,4096]{1,0:T(8,128)(2,1)}), bf16[2048,4096]{1,0:T(8,128)(2,1)}) %all-gather.36.cloned.1.call-update) | async-done | bytes 16777232 | tf_op jit(solution)/shard_map/all_gather | solution.py:195
  781.7 22.0 multiply_convert_fusion.2
  803.7 15.4 fusion.140
  819.1 14.0 add_convert_fusion.2
  833.2 14.6 convolution_convert_fusion.1
  847.9 17.2 reduce-scatter.19.cloned.1.call-done
  867.8 5.3 psum.44
  873.1 26.5 %reduce-scatter.17.cloned.1.call-done = bf16[512,1024]{1,0:T(8,128)(2,1)} async-done(((bf16[512,2048]{1,0:T(8,128)(2,1)}), bf16[512,1024]{1,0:T(8,128)(2,1)}) %reduce-scatter.17.cloned.1.call-update) | async-done | bytes 1048592 | tf_op jit(solution)/shard_map/reduce_scatter | solution.py:44
  904.2 33.2 %all-gather.44.cloned.1.call-done = bf16[512,2048]{1,0:T(8,128)(2,1)} async-done(((bf16[512,1024]{1,0:T(8,128)(2,1)}), bf16[512,2048]{1,0:T(8,128)(2,1)}) %all-gather.44.cloned.1.call-update) | async-done | bytes 2097168 | tf_op jit(solution)/shard_map/all_gather | solution.py:40
  950.8 70.0 %while.37 = (s32[]{:T(128)}, f32[2,256,4,4,64]{1,4,3,2,0:T(8,128)S(1)}, f32[2,1024,256]{1,2,0:T(8,128)}, f32[2,1024,256]{1,2,0:T(8,128)}, bf16[2,1024,256]{1,2,0...) while((s32[]{:T(128)}, ...), condition=%wide.region_20.21_spmd.clone, body=%wide.region_19.20_spmd.clone.sunk | while | flops 1371997440 | bytes 94737760 | solution.py:130
  1033.6 15.0 reduce-scatter.21.cloned.1.call-done
  1054.4 22.1 reduce-scatter.23.cloned.1.call-done
  1076.5 5.7 add_convert_fusion.1
  1083.6 30.6 %reduce-scatter.25.cloned.1.call-done = bf16[512,1024]{1,0:T(8,128)(2,1)} async-done(((bf16[512,2048]{1,0:T(8,128)(2,1)}), bf16[512,1024]{1,0:T(8,128)(2,1)}) %reduce-scatter.25.cloned.1.call-update) | async-done | bytes 1048592 | tf_op jit(solution)/shard_map/reduce_scatter | solution.py:44
  1124.1 6.1 add_convert_fusion
  1136.3 5.7 fusion.143
  1143.8 5.6 fusion.146
  1151.1 17.6 fusion.147
  1169.0 17.6 fusion.148
  1188.2 17.9 fusion.149
  1206.8 35.2 %all-reduce = (f32[1024]{0:T(1024)}, f32[1024]{0:T(1024)}) all-reduce(f32[1024]{0:T(1024)S(1)} %get-tuple-element.499, f32[1024]{0:T(1024)S(1)} %copy-done.36), channel_id=1, replica_groups=mesh['dp'=4,'ctx'=4,'tensor'=2] {'dp','ctx'}, use_global_device_ids=true, to_apply=%region_35.36 | all-reduce | flops 2048 | bytes 16384 | tf_op jit(solution)/shard_map/psum | solution.py:373
  1242.0 33.4 %reduce-scatter.27.cloned.1.call-done = bf16[2,256,2048]{2,1,0:T(8,128)(2,1)} async-done(((bf16[8,256,2048]{2,1,0:T(8,128)(2,1)}), bf16[2,256,2048]{2,1,0:T(8,128)(2,1)}) %reduce-scatter.27.cloned.1.call-update) | async-done | bytes 2097168 | tf_op jit(solution)/shard_map/reduce_scatter | solution.py:359
  1278.4 63.6 %reduce-scatter.31.cloned.1.call-done = f32[128,256]{1,0:T(8,128)} async-done(((f32[2048,256]{1,0:T(8,128)}), f32[128,256]{1,0:T(8,128)}) %reduce-scatter.31.cloned.1.call-update) | async-done | bytes 131088 | tf_op jit(solution)/shard_map/reduce_scatter | solution.py:366
  1342.0 65.2 %reduce-scatter.33.cloned.1.call-done = f32[128,256]{1,0:T(8,128)} async-done(((f32[2048,256]{1,0:T(8,128)}), f32[128,256]{1,0:T(8,128)}) %reduce-scatter.33.cloned.1.call-update) | async-done | bytes 131088 | tf_op jit(solution)/shard_map/reduce_scatter | solution.py:367
  1407.3 108.3 %reduce-scatter.29.cloned.1.call-done = f32[128,1024]{1,0:T(8,128)} async-done(((f32[2048,1024]{1,0:T(8,128)}), f32[128,1024]{1,0:T(8,128)}) %reduce-scatter.29.cloned.1.call-update) | async-done | bytes 524304 | tf_op jit(solution)/shard_map/reduce_scatter | solution.py:365
  1515.5 109.1 %reduce-scatter.35.cloned.1.call-done = f32[1024,128]{1,0:T(8,128)} async-done(((f32[1024,2048]{1,0:T(8,128)}), f32[1024,128]{1,0:T(8,128)}) %reduce-scatter.35.cloned.1.call-update) | async-done | bytes 524304 | tf_op jit(solution)/shard_map/reduce_scatter | solution.py:370
  1624.7 337.2 %reduce-scatter.37.cloned.1.call-done = f32[128,4096]{1,0:T(8,128)} async-done(((f32[2048,4096]{1,0:T(8,128)}), f32[128,4096]{1,0:T(8,128)}) %reduce-scatter.37.cloned.1.call-update) | async-done | bytes 2097168 | tf_op jit(solution)/shard_map/reduce_scatter | solution.py:368
  1961.8 336.8 %reduce-scatter.39.cloned.1.call-done = f32[128,4096]{1,0:T(8,128)} async-done(((f32[2048,4096]{1,0:T(8,128)}), f32[128,4096]{1,0:T(8,128)}) %reduce-scatter.39.cloned.1.call-update) | async-done | bytes 2097168 | tf_op jit(solution)/shard_map/reduce_scatter | solution.py:369
  2298.6 336.6 %reduce-scatter.41.cloned.1.call-done = f32[4096,128]{1,0:T(8,128)} async-done(((f32[4096,2048]{1,0:T(8,128)}), f32[4096,128]{1,0:T(8,128)}) %reduce-scatter.41.cloned.1.call-update) | async-done | bytes 2097168 | tf_op jit(solution)/shard_map/reduce_scatter | solution.py:371
  (408 shorter events, 220.0 us)
Async XLA Ops:
  7.2 93.6 %copy-start.32 = (f32[1024]{0:T(1024)S(1)}, f32[1024]{0:T(1024)}, u32[]{:S(2)}) copy-start(f32[1024]{0:T(1024)} %param.28) | copy-start | bytes 12292
  7.2 85.9 %all-gather.16.cloned.1.call-start = ((), (), s32[]{:S(2)}) async-start(), calls=%async_computation.14 | async-start | bytes 5242880 | tf_op jit(solution)/shard_map/all_gather | solution.py:173
  7.9 102.0 %all-gather.20.cloned.1.call-start = ((), (), s32[]{:S(2)}) async-start(), calls=%async_computation.16 | async-start | bytes 1310720 | tf_op jit(solution)/shard_map/all_gather | solution.py:192
  8.7 136.5 %all-gather.18.cloned.1.call-start = ((), (), s32[]{:S(2)}) async-start(), calls=%async_computation.15 | async-start | bytes 3145728 | tf_op jit(solution)/shard_map/all_gather | solution.py:40
  94.4 805.3 %copy-start.4 = (bf16[1,256,1024]{2,1,0:T(8,128)(2,1)}, bf16[1,256,1024]{2,1,0:T(8,128)(2,1)S(1)}, u32[]{:S(2)}) copy-start(bf16[1,256,1024]{2,1,0:T(8,128)(2,1)S(1)} %get-tuple-element.614) | copy-start | bytes 1572868
  94.4 805.3 %copy-start.6 = (bf16[1,256,1024]{2,1,0:T(8,128)(2,1)}, bf16[1,256,1024]{2,1,0:T(8,128)(2,1)S(1)}, u32[]{:S(2)}) copy-start(bf16[1,256,1024]{2,1,0:T(8,128)(2,1)S(1)} %get-tuple-element.615) | copy-start | bytes 1572868
  102.1 61.3 %all-gather.26.cloned.1.call-start = ((), (), s32[]{:S(2)}) async-start(), calls=%async_computation.19 | async-start | bytes 1310720 | tf_op jit(solution)/shard_map/all_gather | solution.py:193
  102.7 96.6 %all-gather.24.cloned.1.call-start = ((), (), s32[]{:S(2)}) async-start(), calls=%async_computation.18 | async-start | bytes 5242880 | tf_op jit(solution)/shard_map/all_gather | solution.py:191
  103.3 114.9 %all-gather.22.cloned.1.call-start = ((), (), s32[]{:S(2)}) async-start(), calls=%async_computation.17 | async-start | bytes 1310720 | tf_op jit(solution)/shard_map/all_gather | solution.py:252
  103.6 100.3 %copy-start.19 = (f32[4,8,2,256]{3,1,2,0:T(8,128)}, f32[4,8,2,256]{3,1,2,0:T(8,128)S(1)}, u32[]{:S(2)}) copy-start(f32[4,8,2,256]{3,1,2,0:T(8,128)S(1)} %copy.126) | copy-start | bytes 196612
  103.7 100.2 %copy-start.22 = (f32[4,8,2,256]{3,1,2,0:T(8,128)}, f32[4,8,2,256]{3,1,2,0:T(8,128)S(1)}, u32[]{:S(2)}) copy-start(f32[4,8,2,256]{3,1,2,0:T(8,128)S(1)} %copy.127) | copy-start | bytes 196612
  145.2 18.2 copy-start.8
  148.1 19.7 copy-start.38
  148.9 88.3 %all-gather.28.cloned.1.call-start = ((), (), s32[]{:S(2)}) async-start(), calls=%async_computation.20 | async-start | bytes 1310720 | tf_op jit(solution)/shard_map/all_gather | solution.py:253
  166.2 123.6 %all-gather.30.cloned.1.call-start = ((), (), s32[]{:S(2)}) async-start(), calls=%async_computation.21 | async-start | bytes 5242880 | tf_op jit(solution)/shard_map/all_gather | solution.py:196
  166.9 188.7 %all-gather.40.cloned.1.call-start = ((), (), s32[]{:S(2)}) async-start(), calls=%async_computation.28 | async-start | bytes 5242880 | tf_op jit(solution)/shard_map/all_gather | solution.py:174
  167.7 221.0 %reduce-scatter.15.cloned.1.call-start = ((), (), s32[]{:S(2)}) async-start(), calls=%async_computation.22 | async-start | bytes 3145728 | tf_op jit(solution)/shard_map/reduce_scatter | solution.py:44
  282.0 14.0 copy-start
  282.0 14.7 copy-start.29
  296.0 128.0 %all-gather.42.cloned.1.call-start = ((), (), s32[]{:S(2)}) async-start(), calls=%async_computation.29 | async-start | bytes 3145728 | tf_op jit(solution)/shard_map/all_gather | solution.py:40
  358.3 37.4 %copy-start.31 = (f32[1024]{0:T(1024)S(1)}, f32[1024]{0:T(1024)}, u32[]{:S(2)}) copy-start(f32[1024]{0:T(1024)} %param.29) | copy-start | bytes 12292
  358.3 173.2 %all-gather.38.cloned.1.call-start = ((), (), s32[]{:S(2)}) async-start(), calls=%async_computation.26 | async-start | bytes 20971520 | tf_op jit(solution)/shard_map/all_gather | solution.py:197
  358.9 207.9 %all-gather.32.cloned.1.call-start = ((), (), s32[]{:S(2)}) async-start(), calls=%async_computation.23 | async-start | bytes 3145728 | tf_op jit(solution)/shard_map/all_gather | solution.py:40
  398.4 275.9 %all-gather.34.cloned.1.call-start = ((), (), s32[]{:S(2)}) async-start(), calls=%async_computation.24 | async-start | bytes 20971520 | tf_op jit(solution)/shard_map/all_gather | solution.py:194
  399.0 382.7 %all-gather.36.cloned.1.call-start = ((), (), s32[]{:S(2)}) async-start(), calls=%async_computation.25 | async-start | bytes 20971520 | tf_op jit(solution)/shard_map/all_gather | solution.py:195
  399.6 465.5 %reduce-scatter.19.cloned.1.call-start = ((), (), s32[]{:S(2)}) async-start(), calls=%async_computation.30 | async-start | bytes 3145728 | tf_op jit(solution)/shard_map/reduce_scatter | solution.py:44
  803.7 15.4 copy-start.43
  833.1 66.5 %reduce-scatter.17.cloned.1.call-start = ((), (), s32[]{:S(2)}) async-start(), calls=%async_computation.27 | async-start | bytes 3145728 | tf_op jit(solution)/shard_map/reduce_scatter | solution.py:44
  833.2 31.9 %copy-start.10 = (bf16[512,1024]{1,0:T(8,128)(2,1)S(1)}, bf16[512,1024]{1,0:T(8,128)(2,1)}, u32[]{:S(2)}) copy-start(bf16[512,1024]{1,0:T(8,128)(2,1)} %reduce-scatter.15.cloned.1.call-done) | copy-start | bytes 3145732
  847.8 89.5 %all-gather.44.cloned.1.call-start = ((), (), s32[]{:S(2)}) async-start(), calls=%async_computation.31 | async-start | bytes 3145728 | tf_op jit(solution)/shard_map/all_gather | solution.py:40
  904.1 144.5 %reduce-scatter.21.cloned.1.call-start = ((), (), s32[]{:S(2)}) async-start(), calls=%async_computation.32 | async-start | bytes 1310720 | tf_op jit(solution)/shard_map/reduce_scatter | solution.py:323
  1023.6 52.9 %reduce-scatter.23.cloned.1.call-start = ((), (), s32[]{:S(2)}) async-start(), calls=%async_computation.33 | async-start | bytes 1310720 | tf_op jit(solution)/shard_map/reduce_scatter | solution.py:326
  1026.2 88.0 %reduce-scatter.25.cloned.1.call-start = ((), (), s32[]{:S(2)}) async-start(), calls=%async_computation.34 | async-start | bytes 3145728 | tf_op jit(solution)/shard_map/reduce_scatter | solution.py:44
  1050.3 26.1 copy-start.24
  1076.5 37.7 %copy-start.5 = (bf16[1,256,1024]{2,1,0:T(8,128)(2,1)S(1)}, bf16[1,256,1024]{2,1,0:T(8,128)(2,1)}, u32[]{:S(2)}) copy-start(bf16[1,256,1024]{2,1,0:T(8,128)(2,1)} %copy-done.4) | copy-start | bytes 1572868
  1076.5 37.7 %copy-start.7 = (bf16[1,256,1024]{2,1,0:T(8,128)(2,1)S(1)}, bf16[1,256,1024]{2,1,0:T(8,128)(2,1)}, u32[]{:S(2)}) copy-start(bf16[1,256,1024]{2,1,0:T(8,128)(2,1)} %copy-done.6) | copy-start | bytes 1572868
  1076.5 37.7 %copy-start.33 = (f32[1024]{0:T(1024)S(1)}, f32[1024]{0:T(1024)}, u32[]{:S(2)}) copy-start(f32[1024]{0:T(1024)} %param.28) | copy-start | bytes 12292
  1076.5 37.7 %copy-start.35 = (f32[512]{0:T(512)S(1)}, f32[512]{0:T(512)}, u32[]{:S(2)}) copy-start(f32[512]{0:T(512)} %copy-done.34) | copy-start | bytes 6148
  1082.2 39.1 %copy-start.13 = (f32[512,1024]{1,0:T(8,128)S(1)}, f32[512,1024]{1,0:T(8,128)}, u32[]{:S(2)}) copy-start(f32[512,1024]{1,0:T(8,128)} %get-tuple-element.556) | copy-start | bytes 6291460
  1082.2 39.1 %copy-start.37 = (f32[512]{0:T(512)S(1)}, f32[512]{0:T(512)}, u32[]{:S(2)}) copy-start(f32[512]{0:T(512)} %get-tuple-element.627) | copy-start | bytes 6148
  1082.2 193.2 %reduce-scatter.27.cloned.1.call-start = ((), (), s32[]{:S(2)}) async-start(), calls=%async_computation.35 | async-start | bytes 10485760 | tf_op jit(solution)/shard_map/reduce_scatter | solution.py:359
  1130.2 211.9 %reduce-scatter.31.cloned.1.call-start = ((), (), s32[]{:S(2)}) async-start(), calls=%async_computation.37 | async-start | bytes 2228224 | tf_op jit(solution)/shard_map/reduce_scatter | solution.py:366
  1133.8 273.4 %reduce-scatter.33.cloned.1.call-start = ((), (), s32[]{:S(2)}) async-start(), calls=%async_computation.38 | async-start | bytes 2228224 | tf_op jit(solution)/shard_map/reduce_scatter | solution.py:367
  1136.2 379.3 %reduce-scatter.29.cloned.1.call-start = ((), (), s32[]{:S(2)}) async-start(), calls=%async_computation.36 | async-start | bytes 8912896 | tf_op jit(solution)/shard_map/reduce_scatter | solution.py:365
  1142.0 482.7 %reduce-scatter.35.cloned.1.call-start = ((), (), s32[]{:S(2)}) async-start(), calls=%async_computation.39 | async-start | bytes 8912896 | tf_op jit(solution)/shard_map/reduce_scatter | solution.py:370
  1149.5 812.3 %reduce-scatter.37.cloned.1.call-start = ((), (), s32[]{:S(2)}) async-start(), calls=%async_computation.40 | async-start | bytes 35651584 | tf_op jit(solution)/shard_map/reduce_scatter | solution.py:368
  1168.7 1129.9 %reduce-scatter.39.cloned.1.call-start = ((), (), s32[]{:S(2)}) async-start(), calls=%async_computation.41 | async-start | bytes 35651584 | tf_op jit(solution)/shard_map/reduce_scatter | solution.py:369
  1186.7 1448.6 %reduce-scatter.41.cloned.1.call-start = ((), (), s32[]{:S(2)}) async-start(), calls=%async_computation.42 | async-start | bytes 35651584 | tf_op jit(solution)/shard_map/reduce_scatter | solution.py:371
  (37 other events, 123.6 us)
Sparse Core Ops, SparseCore 0:
  9.6 83.4 all-gather.15
  94.6 15.2 all-gather.19
  112.1 33.1 all-gather.17
  146.6 16.7 all-gather.25
  164.8 34.4 all-gather.23
  201.3 16.8 all-gather.21
  220.3 16.8 all-gather.27
  238.7 34.4 all-gather.29
  274.8 80.7 all-gather.39
  358.3 30.3 reduce-scatter.14
  390.9 33.0 all-gather.41
  425.5 105.9 all-gather.37
  533.7 33.1 all-gather.31
  568.3 105.9 all-gather.33
  675.8 105.9 all-gather.35
  833.2 31.8 reduce-scatter.18
  867.8 31.8 reduce-scatter.16
  904.2 33.0 all-gather.43
  1023.7 24.8 reduce-scatter.20
  1051.5 24.8 reduce-scatter.22
  1082.3 31.8 reduce-scatter.24
  1130.3 145.0 reduce-scatter.26
  1279.7 62.2 reduce-scatter.30
  1346.7 60.5 reduce-scatter.32
  1411.9 103.5 reduce-scatter.28
  1520.0 104.5 reduce-scatter.34
  1629.4 332.4 reduce-scatter.36
  1966.7 331.9 reduce-scatter.38
  2303.5 331.7 reduce-scatter.40
where the time goes:
time: 2650 us; the launch traced here: 2640 us
  waiting for transfers between devices  2180 us (82%)
  matrix products  252 us (10%)
  other arithmetic  85.2 us (3%)
  blocking collectives  55.7 us (2%)
  local copies, waits for them, and re-layouts  50.3 us (2%)
    reduce_scatter x1, waiting for transfers between devices, per_device(): lax.psum_scatter(gate_sum, ('dp', 'ctx'), scatter_dimension=0, tiled=True)  337 us
    reduce_scatter x1, waiting for transfers between devices, per_device(): lax.psum_scatter(up_sum, ('dp', 'ctx'), scatter_dimension=0, tiled=True)  337 us
    reduce_scatter x1, waiting for transfers between devices, per_device(): lax.psum_scatter(down_sum, ('dp', 'ctx'), scatter_dimension=1, tiled=True)  337 us
    dot_general x21, matrix products, matmul(): return jnp.dot(left, right, preferred_element_type=jnp.float32)  200 us
    all_gather x4, waiting for transfers between devices, whole_rows(): return lax.all_gather(values, 'tensor', axis=1, tiled=True)  113 us
    reduce_scatter x1, waiting for transfers between devices, per_device(): lax.psum_scatter(output_sum, ('dp', 'ctx'), scatter_dimension=1, tiled=True)  109 us
    reduce_scatter x1, waiting for transfers between devices, per_device(): lax.psum_scatter(query_sum, ('dp', 'ctx'), scatter_dimension=0, tiled=True)  108 us
    all_gather x1, waiting for transfers between devices, per_device(): lax.all_gather(down_weight, 'ctx', axis=1, tiled=True)  107 us
  transfers between devices with their start and end apart: 29, of which 28 were waited for; matrix products, arithmetic and copies ran while one was open for 8% of the time, Pallas kernels for 0%

commit v1 on v0

v1 whole, which is shorter than its diff:
```python
import jax
import jax.numpy as jnp
from jax import lax
from jax.sharding import PartitionSpec as P

HD = 64
EPS = 1e-05
NEGATIVE = -1e30
BF = jnp.bfloat16


def inverse_frequency(head_size):
    exponent = jnp.arange(0, head_size, 2, dtype=jnp.int32).astype(jnp.float32) / head_size
    plain = 1.0 / jnp.power(jnp.float32(500000.0), exponent)
    factor = 32.0
    old_context = 8192.0
    wavelength = 2.0 * jnp.pi / plain
    smooth = (old_context / wavelength - 1.0) / (4.0 - 1.0)
    scaled = jnp.where(wavelength > old_context, plain / factor, plain)
    middle = (wavelength <= old_context) & (wavelength >= old_context / 4.0)
    scaled = jnp.where(middle, (1.0 - smooth) * plain / factor + smooth * plain, scaled)
    return scaled


def rotate(values, cosine, sine):
    half = values.shape[-1] // 2
    first = values[..., :half]
    second = values[..., half:]
    return jnp.concatenate(
        [first * cosine - second * sine, second * cosine + first * sine], axis=-1
    )


def matmul(left, right):
    return jnp.dot(left, right, preferred_element_type=jnp.float32)


class Plan:
    def __init__(self):
        self.place = lax.axis_index("ctx")
        self.side = lax.axis_index("tensor")
        self.group = lax.axis_index("dp")
        self.parts = lax.axis_size("ctx")
        self.sides = lax.axis_size("tensor")
        self.groups = lax.axis_size("dp")
        self.fast = self.parts == 4 and self.sides == 2
        self.core = self.place % 2
        self.masks = (0, 2, 1, 3) if self.fast else tuple(range(self.parts))

    def member(self, block):
        return self.place ^ self.masks[block] if self.fast else block

    def half(self, index):
        return self.side ^ index if self.fast else index

    def ordered(self, block, count):
        return block ^ (self.side * (count // 2)) if self.fast else block


def swap(values, axis, mask):
    size = lax.axis_size(axis)
    return lax.ppermute(values, axis, [(i, i ^ mask) for i in range(size)])


def shift(values, axis, step):
    size = lax.axis_size(axis)
    return lax.ppermute(values, axis, [(i, (i + step) % size) for i in range(size)])


def turn(values, first):
    pairs = []
    for i in range(8):
        along_tensor = (((i >> 1) & 1) == 0) == first
        pairs.append((i, i ^ 1 if along_tensor else i ^ 4))
    return lax.ppermute(values, ("ctx", "tensor"), pairs)


def gather_rows(plan, values):
    if not plan.fast:
        wide = lax.all_gather(values, "tensor", axis=2, tiled=True)
        return lax.all_gather(wide, "ctx", axis=0)
    one = turn(values, True)
    two = turn(values, False)
    far = turn(one, False)
    core_own = swap(values, "ctx", 1)
    core_one = swap(one, "ctx", 1)
    core_two = swap(two, "ctx", 1)
    core_far = swap(far, "ctx", 1)
    zero = plan.core == 0
    rows = [
        jnp.concatenate([values, jnp.where(zero, one, two)], axis=2),
        jnp.concatenate([jnp.where(zero, two, one), far], axis=2),
        jnp.concatenate([core_own, jnp.where(zero, core_two, core_one)], axis=2),
        jnp.concatenate([jnp.where(zero, core_one, core_two), core_far], axis=2),
    ]
    return jnp.stack(rows)


def scatter_rows(plan, left, right, slots):
    width = right.shape[-1]
    if not plan.fast:
        whole = matmul(left, right).astype(BF).reshape(plan.parts, slots, -1, width)
        narrow = lax.psum_scatter(whole, "tensor", scatter_dimension=3, tiled=True)
        return lax.psum_scatter(narrow, "ctx", scatter_dimension=0, tiled=False).astype(jnp.float32)
    half = left.shape[0] // 2
    away = matmul(left[half:], right).astype(BF).reshape(2, slots, -1, width)
    here = matmul(left[:half], right).astype(BF).reshape(2, slots, -1, width)
    return scatter_blocks(plan, here, away)


def add(left, right):
    return (left.astype(jnp.float32) + right.astype(jnp.float32)).astype(BF)


def scatter_blocks(plan, here, away):
    width = here.shape[-1] // 2
    both = add(here, swap(away, "ctx", 1))
    zero = plan.core == 0
    near = both[0, :, :, :width]
    by_tensor = both[0, :, :, width:]
    by_ctx = both[1, :, :, :width]
    far = both[1, :, :, width:]
    got = turn(jnp.stack([jnp.where(zero, by_ctx, by_tensor), far]), False)
    kept = add(near, got[0])
    sent = add(jnp.where(zero, by_tensor, by_ctx), got[1])
    return kept.astype(jnp.float32) + turn(sent, True).astype(jnp.float32)


def exchange_pieces(plan, piece):
    found = [(plan.place, piece(plan.place))]
    for mask in range(1, plan.parts):
        other = plan.place ^ mask
        found.append((other, swap(piece(other), "ctx", mask)))
    return found


def place_rows(plan, found, total):
    rows, columns = found[0][1].shape
    whole = jnp.zeros((total, columns), found[0][1].dtype)
    for member, piece in found:
        start = plan.ordered(member, plan.parts) * rows
        whole = lax.dynamic_update_slice(whole, piece, (start, 0))
    return whole


def place_columns(plan, found, total):
    rows, columns = found[0][1].shape
    whole = jnp.zeros((rows, total), found[0][1].dtype)
    for member, piece in found:
        start = plan.ordered(member, plan.parts) * columns
        whole = lax.dynamic_update_slice(whole, piece, (0, start))
    return whole


def column_piece(weights, parts, least=1):
    def piece(member):
        taken = []
        for weight in weights:
            share = max(1, least * parts // weight.shape[1])
            size = weight.shape[1] * share // parts
            taken.append(lax.dynamic_slice_in_dim(weight, member // share * size, size, 1))
        return jnp.concatenate(taken, axis=1)

    return piece


def row_piece(weight, parts):
    size = weight.shape[0] // parts

    def piece(member):
        return lax.dynamic_slice_in_dim(weight, member * size, size, 0)

    return piece


def reduce_groups(plan, block):
    count = plan.groups
    size = block(plan.group).shape[0] // 2

    def up_block(step):
        return block((plan.group + step) % count)[:size]

    def down_block(step):
        return block((plan.group - step) % count)[size:]

    up = up_block(count - 1).astype(BF)
    down = down_block(count - 1).astype(BF)
    for step in range(count - 2, -1, -1):
        up = add(shift(up, "dp", 1), up_block(step))
        down = add(shift(down, "dp", -1), down_block(step))
    return jnp.concatenate([up, down], axis=0)


def finish_columns(plan, grad, widths):
    rows = grad.shape[0] // plan.groups

    def block(group):
        return lax.dynamic_slice_in_dim(grad, plan.ordered(group, plan.groups) * rows, rows, 0)

    part = reduce_groups(plan, block)
    found = exchange_pieces(plan, row_piece(part, plan.parts))
    outs = []
    start = 0
    for width, share in widths:
        whole = jnp.zeros((rows // plan.parts, width * plan.parts // share), jnp.float32)
        for member, piece in found:
            part = piece[:, start : start + width].astype(jnp.float32)
            at = member // share * width
            if share > 1:
                part = part + lax.dynamic_slice_in_dim(whole, at, width, 1)
            whole = lax.dynamic_update_slice(whole, part, (0, at))
        outs.append(whole)
        start += width
    return outs


def finish_rows(plan, grad):
    columns = grad.shape[1] // plan.groups
    height = grad.shape[0]

    def block(group):
        return lax.dynamic_slice_in_dim(
            grad, plan.ordered(group, plan.groups) * columns, columns, 1
        )

    part = reduce_groups(plan, block)
    found = exchange_pieces(plan, column_piece([part], plan.parts))
    whole = jnp.zeros((height * plan.parts, columns // plan.parts), jnp.float32)
    for member, piece in found:
        whole = lax.dynamic_update_slice(whole, piece.astype(jnp.float32), (member * height, 0))
    return whole


def feature_total(values):
    total = jnp.sum(values, axis=-1, keepdims=True)
    if lax.axis_size("tensor") == 2:
        return total + swap(total, "tensor", 1)
    return lax.psum(total, "tensor")


def per_device(
    inputs,
    cotangent,
    lengths,
    deal_order,
    query_weight,
    key_weight,
    value_weight,
    output_weight,
    gate_weight,
    up_weight,
    down_weight,
    attention_gain,
    feedforward_gain,
):
    plan = Plan()
    slots, rows, half_width = inputs.shape
    width = half_width * plan.sides
    parts = plan.parts
    groups = plan.groups
    sequences = lengths.shape[0]
    tokens = parts * slots * rows
    ids = jnp.arange(sequences, dtype=jnp.int32)
    own_ids = plan.group * slots + jnp.arange(slots, dtype=jnp.int32)
    slot_lengths = lax.dynamic_slice_in_dim(lengths, plan.group * slots, slots)
    dealt = jnp.sum(jnp.where(deal_order[:, None] == ids[None, :], lengths[None, :], 0), axis=1)
    totals = jnp.sum(dealt.reshape(groups, -1), axis=1)
    found = jnp.where(deal_order[None, :] == own_ids[:, None], ids[None, :], 0)
    owner = jnp.sum(found, axis=1) // (sequences // groups)
    mine = owner[:, None] == jnp.arange(groups, dtype=jnp.int32)[None, :]
    own_totals = jnp.sum(jnp.where(mine, totals[None, :], 0), axis=1)
    scale = jnp.sum(lengths).astype(jnp.float32) / groups / own_totals.astype(jnp.float32)

    starts = jnp.stack([plan.member(j) for j in range(parts)]).astype(jnp.int32) * rows
    positions = starts[:, None] + jnp.arange(rows, dtype=jnp.int32)[None, :]
    own_rows = plan.place * rows + jnp.arange(rows, dtype=jnp.int32)
    valid = positions[:, None, :] < slot_lengths[None, :, None]
    own_valid = own_rows[None, :] < slot_lengths[:, None]
    angle = positions.astype(jnp.float32)[:, :, None] * inverse_frequency(HD)
    cosine = jnp.cos(angle)[:, None]
    sine = jnp.sin(angle)[:, None]

    source = inputs.astype(jnp.float32)
    inverse_one = lax.rsqrt(feature_total(source * source) / width + EPS)
    normed = gather_rows(plan, (source * inverse_one * attention_gain).astype(BF))
    normed = normed.reshape(tokens, width)
    qkv_w = place_rows(
        plan, exchange_pieces(plan, column_piece([query_weight, key_weight, value_weight], parts, HD)), width
    )
    o_w = place_columns(plan, exchange_pieces(plan, row_piece(output_weight, parts)), width)
    pair_w = place_rows(
        plan, exchange_pieces(plan, column_piece([gate_weight, up_weight], parts)), width
    )
    down_w = place_columns(plan, exchange_pieces(plan, row_piece(down_weight, parts)), width)
    target_all = gather_rows(plan, cotangent).astype(jnp.float32)
    target_all = (target_all * valid[..., None] * scale[None, :, None, None]).astype(BF)
    target_all = target_all.reshape(tokens, width)

    wide = query_weight.shape[1] // parts
    share = max(1, HD * parts // key_weight.shape[1])
    narrow = key_weight.shape[1] * share // parts
    heads = wide // HD
    projected = matmul(normed, qkv_w)
    query = rotate(
        projected[:, :wide].reshape(parts, slots, rows, heads, HD),
        cosine[..., None, :],
        sine[..., None, :],
    ).astype(BF)
    key = rotate(
        projected[:, wide : wide + narrow].reshape(parts, slots, rows, HD), cosine, sine
    ).astype(BF)
    value = projected[:, wide + narrow :].reshape(parts, slots, rows, HD).astype(BF)
    limit = jnp.minimum(positions[:, None, :] + 1, slot_lengths[None, :, None])
    limit = limit.transpose(1, 0, 2).reshape(slots, 1, parts * rows, 1)
    allowed = positions.reshape(1, 1, 1, parts * rows) < limit

    def by_slot(values):
        return values.swapaxes(0, 1).reshape(slots, parts * rows, *values.shape[3:])

    def by_block(values):
        return values.reshape(slots, parts, rows, -1).swapaxes(0, 1).reshape(tokens, -1)

    query, key, value = by_slot(query), by_slot(key), by_slot(value)
    scores = jnp.einsum("sphd,sqd->shpq", query, key, preferred_element_type=jnp.float32)
    scores = jnp.where(allowed, scores * HD ** (-0.5), NEGATIVE)
    top = jnp.max(scores, axis=3, keepdims=True)
    powers = jnp.where(allowed, jnp.exp(scores - top), 0.0)
    probs = powers / jnp.sum(powers, axis=3, keepdims=True)
    probs_b = probs.astype(BF)
    attended = jnp.einsum("shpq,sqd->sphd", probs_b, value, preferred_element_type=jnp.float32)
    attended_b = by_block(attended.astype(BF))
    hidden = source + scatter_rows(plan, attended_b, o_w, slots)

    inverse_two = lax.rsqrt(feature_total(hidden * hidden) / width + EPS)
    normed_two = gather_rows(plan, (hidden * inverse_two * feedforward_gain).astype(BF))
    normed_two = normed_two.reshape(tokens, width)
    units = pair_w.shape[1] // 2
    gate = matmul(normed_two, pair_w[:, :units])
    upward = matmul(normed_two, pair_w[:, units:])
    sigmoid = jax.nn.sigmoid(gate)
    active = (gate * sigmoid * upward).astype(BF)
    result = hidden + scatter_rows(plan, active, down_w, slots)
    outputs = jnp.where(own_valid[:, :, None], result, 0.0).astype(BF)

    target = cotangent.astype(jnp.float32) * own_valid[:, :, None] * scale[:, None, None]
    grad_active = matmul(target_all, down_w.T)
    down_sum = matmul(active.T, target_all).astype(BF)
    grad_gate = (grad_active * upward * sigmoid * (1.0 + gate * (1.0 - sigmoid))).astype(BF)
    grad_up = (grad_active * gate * sigmoid).astype(BF)
    grad_pair = jnp.concatenate([grad_gate, grad_up], axis=1)
    pair_sum = matmul(normed_two.T, grad_pair).astype(BF)
    dn = scatter_rows(plan, grad_pair, pair_w.T, slots)
    weighted = dn * feedforward_gain
    total_two = feature_total(weighted * hidden)
    grad_hidden = target + inverse_two * weighted - hidden * inverse_two**3 * total_two / width
    gain_two_sum = jnp.sum(dn * hidden * inverse_two, axis=(0, 1))

    grad_hidden_all = gather_rows(plan, grad_hidden.astype(BF)).reshape(tokens, width)
    grad_attended = matmul(grad_hidden_all, o_w.T).astype(BF)
    output_sum = matmul(attended_b.T, grad_hidden_all).astype(BF)
    grad_attended = by_slot(grad_attended.reshape(parts, slots, rows, heads, HD))
    delta = jnp.sum(grad_attended.astype(jnp.float32) * attended, axis=3).transpose(0, 2, 1)
    grad_probs = jnp.einsum(
        "sphd,sqd->shpq", grad_attended, value, preferred_element_type=jnp.float32
    )
    grad_scores = (probs * (grad_probs - delta[..., None]) * HD ** (-0.5)).astype(BF)
    grad_query = jnp.einsum("shpq,sqd->sphd", grad_scores, key, preferred_element_type=jnp.float32)
    grad_key = jnp.einsum("shpq,sphd->sqd", grad_scores, query, preferred_element_type=jnp.float32)
    grad_value = jnp.einsum(
        "shpq,sphd->sqd", probs_b, grad_attended, preferred_element_type=jnp.float32
    )
    cosine_rows = cosine.reshape(parts * rows, -1)
    sine_rows = sine.reshape(parts * rows, -1)
    back_query = rotate(grad_query, cosine_rows[:, None], -sine_rows[:, None]).astype(BF)
    back_key = rotate(grad_key, cosine_rows, -sine_rows).astype(BF)
    back_value = grad_value.astype(BF)
    back = jnp.concatenate([by_block(back_query), by_block(back_key), by_block(back_value)], axis=1)
    dm = scatter_rows(plan, back, qkv_w.T, slots)
    qkv_sum = matmul(normed.T, back).astype(BF)
    weighted = dm * attention_gain
    total_one = feature_total(weighted * source)
    input_grad = grad_hidden + inverse_one * weighted - source * inverse_one**3 * total_one / width
    gain_one_sum = jnp.sum(dm * source * inverse_one, axis=(0, 1))

    gain_one_out, gain_two_out = lax.psum((gain_one_sum, gain_two_sum), ("dp", "ctx"))
    down_out = finish_rows(plan, down_sum)
    gate_out, up_out = finish_columns(plan, pair_sum, ((units, 1), (units, 1)))
    output_out = finish_rows(plan, output_sum)
    query_out, key_out, value_out = finish_columns(
        plan, qkv_sum, ((wide, 1), (narrow, share), (narrow, share))
    )
    return (
        outputs,
        input_grad.astype(BF),
        query_out,
        key_out,
        value_out,
        output_out,
        gate_out,
        up_out,
        down_out,
        gain_one_out,
        gain_two_out,
    )


def solution(mesh):
    return jax.shard_map(
        per_device,
        mesh=mesh,
        in_specs=(
            P("dp", "ctx", "tensor"),
            P("dp", "ctx", "tensor"),
            P(),
            P(),
            P("ctx", "tensor"),
            P("ctx", "tensor"),
            P("ctx", "tensor"),
            P("tensor", "ctx"),
            P("ctx", "tensor"),
            P("ctx", "tensor"),
            P("tensor", "ctx"),
            P("tensor"),
            P("tensor"),
        ),
        out_specs=(
            P("dp", "ctx", "tensor"),
            P("dp", "ctx", "tensor"),
            P(("dp", "ctx"), "tensor"),
            P(("dp", "ctx"), "tensor"),
            P(("dp", "ctx"), "tensor"),
            P("tensor", ("dp", "ctx")),
            P(("dp", "ctx"), "tensor"),
            P(("dp", "ctx"), "tensor"),
            P("tensor", ("dp", "ctx")),
            P("tensor"),
            P("tensor"),
        ),
        check_vma=False,
    )
```

time: 2650 us -> 983 us (0.37)
  waiting for transfers between devices: 2180 us -> 366 us
  starting transfers between devices: 1.81 us -> 124 us
  local copies, waits for them, and re-layouts: 50.3 us -> 101 us
  other arithmetic: 85.2 us -> 129 us
  matrix products: 252 us -> 217 us
    reduce_scatter x14 -> x0, waiting for transfers between devices: 1530 us -> none  [the longest x1 337 us: per_device(): lax.psum_scatter(gate_sum, ('dp', 'ctx'), scatter_dimension=0, tiled=True)]
    all_gather x15 -> x0, waiting for transfers between devices: 638 us -> none  [the longest x4 113 us: whole_rows(): return lax.all_gather(values, 'tensor', axis=1, tiled=True)]
    ppermute x0 -> x92, waiting for transfers between devices: none -> 366 us  [the longest x48 180 us: swap(): return lax.ppermute(values, axis, [(i, i ^ mask) for i in range(size)])]
    ppermute x0 -> x92, starting transfers between devices: none -> 124 us  [the longest x24 64.1 us: shift(): lax.ppermute(values, axis, [(i, (i + step) % size) for i in range(size)])]
    dot_general x21 -> x17, matrix products: 200 us -> 151 us  [matmul(): return jnp.dot(left, right, preferred_element_type=jnp.float32)]
    convert_element_type x9 -> x32, other arithmetic: 27 us -> 62.3 us  [the longest x20 33 us: add(): return (left.astype(jnp.float32) + right.astype(jnp.float32)).astype(BF)]
    psum x5 -> x1, blocking collectives: 55.7 us -> 30.6 us  [per_device(): lax.psum((gain_one_sum, gain_two_sum), ('dp', 'ctx'))]
  transfers between devices with their start and end apart: 29 -> 92, of which waited for: 28 -> 29; matrix products, arithmetic and copies ran while one was open for 8% -> 26% of each run, Pallas kernels for 0% -> 0%
where the time goes in v1:
time: 983 us; the launch traced here: 972 us
  waiting for transfers between devices  366 us (37%)
  matrix products  217 us (22%)
  other arithmetic  129 us (13%)
  starting transfers between devices  124 us (13%)
  local copies, waits for them, and re-layouts  101 us (10%)
  blocking collectives  30.6 us (3%)
    ppermute x48, waiting for transfers between devices, swap(): return lax.ppermute(values, axis, [(i, i ^ mask) for i in range(size)])  180 us
    dot_general x17, matrix products, matmul(): return jnp.dot(left, right, preferred_element_type=jnp.float32)  151 us
    ppermute x24, waiting for transfers between devices, shift(): lax.ppermute(values, axis, [(i, (i + step) % size) for i in range(size)])  95.3 us
    ppermute x20, waiting for transfers between devices, turn(): return lax.ppermute(values, ('ctx', 'tensor'), pairs)  90.9 us
    ppermute x24, starting transfers between devices, shift(): lax.ppermute(values, axis, [(i, (i + step) % size) for i in range(size)])  64.1 us
    ppermute x48, starting transfers between devices, swap(): return lax.ppermute(values, axis, [(i, i ^ mask) for i in range(size)])  34.6 us
    convert_element_type x20, other arithmetic, add(): return (left.astype(jnp.float32) + right.astype(jnp.float32)).astype(BF)  33 us
    psum x1, blocking collectives, per_device(): lax.psum((gain_one_sum, gain_two_sum), ('dp', 'ctx'))  30.6 us
  transfers between devices with their start and end apart: 92, of which 29 were waited for; matrix products, arithmetic and copies ran while one was open for 26% of the time, Pallas kernels for 0%

profile of v1, /device:TPU:0, one launch (start us, length us, event | category | flops | bytes accessed | tf_op | source)
XLA Modules:
  0.0 971.8 jit_solution(6442492607932923619)
XLA Ops:
  24.5 14.1 %collective-permute-done.1 = bf16[2,256,1024]{2,1,0:T(8,128)(2,1)} collective-permute-done((bf16[2,256,1024]{2,1,0:T(8,128)(2,1)}, bf16[2,256,1024]{2,1,0:T(8,128)(2,1)}, u32[]{:S(2)}, u32[]{:S(2)}) %collective-permute-start.1) | collective-permute-done | bytes 1048608 | tf_op jit(solution)/shard_map/ppermute | solution.py:75
  42.1 4.5 collective-permute-start.10
  54.7 17.0 %collective-permute-done.10 = bf16[512,384]{1,0:T(8,128)(2,1)S(1)} collective-permute-done((bf16[512,384]{1,0:T(8,128)(2,1)S(1)}, bf16[512,384]{1,0:T(8,128)(2,1)S(1)}, u32[]{:S(2)}, u32[]{:S(2)}) %collective-permute-start.10) | collective-permute-done | bytes 393248 | tf_op jit(solution)/shard_map/ppermute | solution.py:62
  78.7 6.2 fusion.118
  89.3 4.0 reshape.526
  106.0 19.7 %fusion.113 = (f32[2,4,1024]{2,1,0:T(4,128)S(1)}, f32[2,4,1024,1024]{2,3,1,0:T(8,128)}) fusion(pred[2,1024,1024]{1,2,0:T(8,128)(4,1)} %broadcast_compare_fusion, bf16[2,1024,4,64]{1,3,2,0:T(8,128)(2,1)S(1)} %reshape.527, bf16[2,1024,64,1]{1,2,0,3:T(8,128)(2,1)S(1)} %copy-done.42), kind=kOutput, calls=%fused_computation.386 | convolution fusion | flops 1115685888 | bytes 36995072 | tf_op jit(solution)/shard_map/sub | solution.py:327
  125.7 12.9 %fusion.10 = bf16[2,4,1024,1024]{2,3,1,0:T(8,128)(2,1)S(1)} fusion(f32[2,4,1024,1024]{2,3,1,0:T(8,128)} %get-tuple-element.161, f32[2,4,1024]{2,1,0:T(4,128)S(1)} %get-tuple-element.160), kind=kLoop, calls=%fused_computation.15 | loop fusion | flops 16777216 | bytes 50364416 | tf_op jit(solution)/shard_map/convert_element_type | solution.py:329
  138.7 5.0 bitcast_convert_fusion
  155.3 6.1 constant_dynamic-slice_fusion.9
  172.5 4.1 fusion.15
  194.7 90.1 %collective-permute-done.29 = bf16[1024,512]{1,0:T(8,128)(2,1)} collective-permute-done((bf16[1024,512]{1,0:T(8,128)(2,1)}, bf16[1024,512]{1,0:T(8,128)(2,1)}, u32[]{:S(2)}, u32[]{:S(2)}) %collective-permute-start.29) | collective-permute-done | bytes 1048608 | tf_op jit(solution)/shard_map/ppermute | solution.py:62
  284.7 17.0 %collective-permute-done.30 = bf16[1024,512]{1,0:T(8,128)(2,1)} collective-permute-done((bf16[1024,512]{1,0:T(8,128)(2,1)S(1)}, bf16[1024,512]{1,0:T(8,128)(2,1)}, u32[]{:S(2)}, u32[]{:S(2)}) %collective-permute-start.30) | collective-permute-done | bytes 1048608 | tf_op jit(solution)/shard_map/ppermute | solution.py:62
  314.8 48.4 %collective-permute-done.36 = bf16[2,256,1024]{2,1,0:T(8,128)(2,1)S(1)} collective-permute-done((bf16[2,256,1024]{2,1,0:T(8,128)(2,1)}, bf16[2,256,1024]{2,1,0:T(8,128)(2,1)S(1)}, u32[]{:S(2)}, u32[]{:S(2)}) %collective-permute-start.36) | collective-permute-done | bytes 1048608 | tf_op jit(solution)/shard_map/ppermute | solution.py:75
  374.4 21.0 %collective-permute-done.18 = bf16[2,256,1024]{2,1,0:T(8,128)(2,1)S(1)} collective-permute-done((bf16[2,256,1024]{2,1,0:T(8,128)(2,1)S(1)}, bf16[2,256,1024]{2,1,0:T(8,128)(2,1)S(1)}, u32[]{:S(2)}, u32[]{:S(2)}) %collective-permute-start.18) | collective-permute-done | bytes 1048608 | tf_op jit(solution)/shard_map/ppermute | solution.py:75
  398.1 5.1 fusion.6
  403.4 7.0 collective-permute-done.20
  415.2 4.1 slice-done.13
  419.3 11.7 %fusion.23 = f32[2048,1024]{0,1:T(8,128)} fusion(bf16[2048,2048]{1,0:T(8,128)(2,1)S(1)} %bitcast.295, bf16[2048,2048]{1,0:T(8,128)(2,1)S(1)} %bitcast.299), kind=kOutput, calls=%fused_computation.49 | convolution fusion | flops 8589934592 | bytes 20971520 | tf_op jit(solution)/shard_map/dot_general | solution.py:35
  431.0 11.8 %fusion.25 = f32[2048,1024]{0,1:T(8,128)} fusion(bf16[2048,2048]{1,0:T(8,128)(2,1)S(1)} %bitcast.296, bf16[2048,2048]{1,0:T(8,128)(2,1)S(1)} %bitcast.299), kind=kOutput, calls=%fused_computation.51 | convolution fusion | flops 8589934592 | bytes 20971520 | tf_op jit(solution)/shard_map/dot_general | solution.py:35
  442.8 22.6 %multiply_convert_fusion = (bf16[2048,1024]{0,1:T(8,128)(2,1)S(1)}, bf16[2048,1024]{0,1:T(8,128)(2,1)}, bf16[2048,1024]{0,1:T(8,128)(2,1)}) fusion(f32[2048,1024]{0,1:T(8,128)} %fusion.25, f32[2048,1024]{0,1:T(8,128)} %fusion.23, bf16[2048,2048]{1,0:T(8,128)(2,1)} %fusion.6, bf16[1024,2048]{1,0:T(8,128)(2,1)} %copy-done.27), kind=kOutput, calls=%fused_computation.34 | convolution fusion | flops 8623489024 | bytes 41943040 | tf_op jit(solution)/shard_map/dot_general | solution.py:35
  467.3 13.9 %fusion.29 = bf16[1024,2048]{1,0:T(8,128)(2,1)} fusion(bf16[2048,2048]{1,0:T(8,128)(2,1)} %copy-done.20, bf16[2048,1024]{0,1:T(8,128)(2,1)} %get-tuple-element.24, bf16[2048,1024]{0,1:T(8,128)(2,1)S(1)} %get-tuple-element.23), kind=kOutput, calls=%fused_computation.62 | convolution fusion | flops 8600420352 | bytes 20971520 | tf_op jit(solution)/shard_map/dot_general | solution.py:35
  481.3 23.8 %fusion.16 = bf16[2048,2048]{1,0:T(8,128)(2,1)} fusion(bf16[2048,2048]{1,0:T(8,128)(2,1)} %bitcast.297, bf16[2048,1024]{0,1:T(8,128)(2,1)} %copy-done.77, bf16[2048,1024]{0,1:T(8,128)(2,1)} %get-tuple-element.24), kind=kOutput, calls=%fused_computation.38 | convolution fusion | flops 17200840704 | bytes 25165824 | tf_op jit(solution)/shard_map/dot_general | solution.py:35
  505.1 7.9 convolution_convert_fusion.5
  513.5 9.2 convolution_convert_fusion.2
  528.7 12.6 %fusion.32 = bf16[1024,2048]{1,0:T(8,128)(2,1)S(1)} fusion(bf16[2048,2048]{1,0:T(8,128)(2,1)} %copy-done.20, bf16[2048,1024]{0,1:T(8,128)(2,1)} %get-tuple-element.24, bf16[2048,1024]{0,1:T(8,128)(2,1)} %copy-done.77), kind=kOutput, calls=%fused_computation.63 | convolution fusion | flops 8600420352 | bytes 20971520 | tf_op jit(solution)/shard_map/dot_general | solution.py:35
  541.3 7.4 convolution_convert_fusion.6
  563.0 4.1 fusion.14
  576.5 4.1 collective-permute-done.87
  582.6 20.9 %collective-permute-start.85 = (bf16[512,512]{1,0:T(8,128)(2,1)S(1)}, bf16[512,512]{1,0:T(8,128)(2,1)S(1)}, u32[]{:S(2)}, u32[]{:S(2)}) collective-permute-start(bf16[512,512]{1,0:T(8,128)(2,1)S(1)} %get-tuple-element.37), channel_id=1, source_target_pairs={{0,8},{8,16},{16,24},{24,0},{1,9},{9,17},{17,25},{25,1},{2,10},{10... | collective-permute-start | bytes 1572872 | tf_op jit(solution)/shard_map/ppermute | solution.py:67
  607.4 18.0 %collective-permute-done.77 = bf16[256,2048]{1,0:T(8,128)(2,1)} collective-permute-done((bf16[256,2048]{1,0:T(8,128)(2,1)S(1)}, bf16[256,2048]{1,0:T(8,128)(2,1)}, u32[]{:S(2)}, u32[]{:S(2)}) %collective-permute-start.77) | collective-permute-done | bytes 1048608 | tf_op jit(solution)/shard_map/ppermute | solution.py:67
  629.2 7.4 collective-permute-done.85
  637.4 10.4 %collective-permute-done.88 = bf16[512,512]{1,0:T(8,128)(2,1)S(1)} collective-permute-done((bf16[512,512]{1,0:T(8,128)(2,1)S(1)}, bf16[512,512]{1,0:T(8,128)(2,1)S(1)}, u32[]{:S(2)}, u32[]{:S(2)}) %collective-permute-start.88) | collective-permute-done | bytes 524320 | tf_op jit(solution)/shard_map/ppermute | solution.py:67
  654.6 15.7 %collective-permute-done.75 = bf16[256,2048]{1,0:T(8,128)(2,1)S(1)} collective-permute-done((bf16[256,2048]{1,0:T(8,128)(2,1)S(1)}, bf16[256,2048]{1,0:T(8,128)(2,1)S(1)}, u32[]{:S(2)}, u32[]{:S(2)}) %collective-permute-start.75) | collective-permute-done | bytes 1048608 | tf_op jit(solution)/shard_map/ppermute | solution.py:67
  670.3 20.5 %collective-permute-done.78 = bf16[256,2048]{1,0:T(8,128)(2,1)S(1)} collective-permute-done((bf16[256,2048]{1,0:T(8,128)(2,1)S(1)}, bf16[256,2048]{1,0:T(8,128)(2,1)S(1)}, u32[]{:S(2)}, u32[]{:S(2)}) %collective-permute-start.78) | collective-permute-done | bytes 1048608 | tf_op jit(solution)/shard_map/ppermute | solution.py:67
  696.0 4.0 fusion.108
  704.4 7.1 collective-permute-done.90
  713.5 17.2 %collective-permute-done.91 = bf16[1024,128]{1,0:T(8,128)(2,1)S(1)} collective-permute-done((bf16[1024,128]{1,0:T(8,128)(2,1)S(1)}, bf16[1024,128]{1,0:T(8,128)(2,1)S(1)}, u32[]{:S(2)}, u32[]{:S(2)}) %collective-permute-start.91) | collective-permute-done | bytes 262176 | tf_op jit(solution)/shard_map/ppermute | solution.py:62
  732.4 6.5 collective-permute-done.79
  768.6 17.5 %fusion.3 = bf16[2,4,1024,1024]{2,3,1,0:T(8,128)(2,1)} fusion(bf16[2,1024,4,64]{1,3,2,0:T(8,128)(2,1)S(1)} %reshape.536, f32[2,4,1024]{2,1,0:T(4,128)S(1)} %bitcast.315, f32[2,4,1024,1024]{2,3,1,0:T(8,128)} %get-tuple-element.161, f32[2,4,1024]{2,1,0:T(4,128)} %copy-done.65, bf16[2,1024,64,1]{1,2,0,3:T(8,128)(2,1)} %reshape.553), kind=kOutput, calls=%fused_computation.4 | convolution fusion | flops 1115684864 | bytes 51707904 | tf_op jit(solution)/shard_map/sphd,sqd->shpq/dot_general | solution.py:363
  786.2 8.9 convolution_bitcast_fusion.1
  795.2 9.8 %convolution_bitcast_fusion.3 = f32[2,1024,64]{1,2,0:T(8,128)} fusion(bf16[2,4,1024,1024]{2,3,1,0:T(8,128)(2,1)} %fusion.3, bf16[2,1024,4,64]{1,3,2,0:T(8,128)(2,1)} %copy-done.33), kind=kOutput, calls=%fused_computation.154 | convolution fusion | flops 1073741824 | bytes 18350080 | tf_op jit(solution)/shard_map/shpq,sphd->sqd/dot_general | solution.py:368
  805.0 5.2 fusion.54
  814.8 4.0 convolution_convert_fusion
  827.9 4.0 collective-permute-start.68
  832.0 4.6 convolution_convert_fusion.7
  867.8 4.1 collective-permute-start.61
  880.8 24.4 %collective-permute-done.72 = bf16[256,128]{1,0:T(8,128)(2,1)S(1)} collective-permute-done((bf16[256,128]{1,0:T(8,128)(2,1)S(1)}, bf16[256,128]{1,0:T(8,128)(2,1)S(1)}, u32[]{:S(2)}, u32[]{:S(2)}) %collective-permute-start.72) | collective-permute-done | bytes 65568 | tf_op jit(solution)/shard_map/ppermute | solution.py:62
  937.0 30.6 %all-reduce = (f32[1024]{0:T(1024)}, f32[1024]{0:T(1024)}) all-reduce(f32[1024]{0:T(1024)S(1)} %get-tuple-element.13, f32[1024]{0:T(1024)S(1)} %get-tuple-element.11), channel_id=1, replica_groups=mesh['dp'=4,'ctx'=4,'tensor'=2] {'dp','ctx'}, use_global_device_ids=true, to_apply=%region_13.14 | all-reduce | flops 2048 | bytes 16384 | tf_op jit(solution)/shard_map/psum | solution.py:385
  (560 shorter events, 311.9 us)
Async XLA Ops:
  9.1 33.0 %collective-permute-start.13 = (bf16[256,512]{1,0:T(8,128)(2,1)}, bf16[256,512]{1,0:T(8,128)(2,1)}, u32[]{:S(2)}, u32[]{:S(2)}) collective-permute-start(bf16[256,512]{1,0:T(8,128)(2,1)} %get-tuple-element.108), channel_id=1, source_target_pairs={{0,6},{2,4},{4,2},{6,0},{1,7},{3,5},{5,3},{7,1},{8,14},{10,12},{12... | collective-permute-start | bytes 786440 | tf_op jit(solution)/shard_map/ppermute | solution.py:62
  18.0 35.4 %collective-permute-start.2 = (bf16[2,256,1024]{2,1,0:T(8,128)(2,1)}, bf16[2,256,1024]{2,1,0:T(8,128)(2,1)}, u32[]{:S(2)}, u32[]{:S(2)}) collective-permute-start(bf16[2,256,1024]{2,1,0:T(8,128)(2,1)} %fusion.38), channel_id=1, source_target_pairs={{0,4},{1,5},{2,3},{3,2},{4,0},{5,1},{6,7},{7,6},{8,12},{9,13},{10,... | collective-permute-start | bytes 3145736 | tf_op jit(solution)/shard_map/ppermute | solution.py:75
  22.0 26.6 %collective-permute-start.8 = (bf16[512,384]{1,0:T(8,128)(2,1)}, bf16[512,384]{1,0:T(8,128)(2,1)}, u32[]{:S(2)}, u32[]{:S(2)}) collective-permute-start(bf16[512,384]{1,0:T(8,128)(2,1)} %pad_maximum_fusion.17), channel_id=1, source_target_pairs={{0,2},{2,0},{4,6},{6,4},{1,3},{3,1},{5,7},{7,5},{8,10},{10,8},{12,... | collective-permute-start | bytes 1179656 | tf_op jit(solution)/shard_map/ppermute | solution.py:62
  24.3 29.2 %collective-permute-start.9 = (bf16[512,384]{1,0:T(8,128)(2,1)}, bf16[512,384]{1,0:T(8,128)(2,1)S(1)}, u32[]{:S(2)}, u32[]{:S(2)}) collective-permute-start(bf16[512,384]{1,0:T(8,128)(2,1)} %pad_maximum_fusion.18), channel_id=1, source_target_pairs={{0,4},{2,6},{4,0},{6,2},{1,5},{3,7},{5,1},{7,3},{8,12},{10,14},{12... | collective-permute-start | bytes 1179656 | tf_op jit(solution)/shard_map/ppermute | solution.py:62
  38.7 35.5 %collective-permute-start.3 = (bf16[2,256,1024]{2,1,0:T(8,128)(2,1)}, bf16[2,256,1024]{2,1,0:T(8,128)(2,1)S(1)}, u32[]{:S(2)}, u32[]{:S(2)}) collective-permute-start(bf16[2,256,1024]{2,1,0:T(8,128)(2,1)} %collective-permute-done.1), channel_id=1, source_target_pairs={{0,4},{1,5},{2,3},{3,2},{4,0},{5,1},{6,7},{7,6},{8,12},{9,13},{10,... | collective-permute-start | bytes 3145736 | tf_op jit(solution)/shard_map/ppermute | solution.py:75
  42.1 29.6 %collective-permute-start.10 = (bf16[512,384]{1,0:T(8,128)(2,1)S(1)}, bf16[512,384]{1,0:T(8,128)(2,1)S(1)}, u32[]{:S(2)}, u32[]{:S(2)}) collective-permute-start(bf16[512,384]{1,0:T(8,128)(2,1)S(1)} %pad_maximum_fusion.19), channel_id=1, source_target_pairs={{0,6},{2,4},{4,2},{6,0},{1,7},{3,5},{5,3},{7,1},{8,14},{10,12},{12... | collective-permute-start | bytes 1179656 | tf_op jit(solution)/shard_map/ppermute | solution.py:62
  48.6 28.3 %collective-permute-start.4 = (bf16[2,256,1024]{2,1,0:T(8,128)(2,1)}, bf16[2,256,1024]{2,1,0:T(8,128)(2,1)S(1)}, u32[]{:S(2)}, u32[]{:S(2)}) collective-permute-start(bf16[2,256,1024]{2,1,0:T(8,128)(2,1)} %fusion.38), channel_id=1, source_target_pairs={{0,2},{2,0},{4,6},{6,4},{1,3},{3,1},{5,7},{7,5},{8,10},{10,8},{12,... | collective-permute-start | bytes 3145736 | tf_op jit(solution)/shard_map/ppermute | solution.py:62
  153.3 31.8 %collective-permute-start.34 = (bf16[2,256,1024]{2,1,0:T(8,128)(2,1)}, bf16[2,256,1024]{2,1,0:T(8,128)(2,1)}, u32[]{:S(2)}, u32[]{:S(2)}) collective-permute-start(bf16[2,256,1024]{2,1,0:T(8,128)(2,1)} %param.14), channel_id=1, source_target_pairs={{0,1},{1,0},{2,6},{3,7},{4,5},{5,4},{6,2},{7,3},{8,9},{9,8},{10,14... | collective-permute-start | bytes 3145736 | tf_op jit(solution)/shard_map/ppermute | solution.py:75
  153.5 31.8 %collective-permute-start.35 = (bf16[2,256,1024]{2,1,0:T(8,128)(2,1)}, bf16[2,256,1024]{2,1,0:T(8,128)(2,1)}, u32[]{:S(2)}, u32[]{:S(2)}) collective-permute-start(bf16[2,256,1024]{2,1,0:T(8,128)(2,1)} %param.14), channel_id=1, source_target_pairs={{0,4},{1,5},{2,3},{3,2},{4,0},{5,1},{6,7},{7,6},{8,12},{9,13},{10,... | collective-permute-start | bytes 3145736 | tf_op jit(solution)/shard_map/ppermute | solution.py:75
  162.8 143.4 %collective-permute-start.25 = (bf16[512,2048]{1,0:T(8,128)(2,1)}, bf16[512,2048]{1,0:T(8,128)(2,1)}, u32[]{:S(2)}, u32[]{:S(2)}) collective-permute-start(bf16[512,2048]{1,0:T(8,128)(2,1)} %pad_maximum_fusion.9), channel_id=1, source_target_pairs={{0,2},{2,0},{4,6},{6,4},{1,3},{3,1},{5,7},{7,5},{8,10},{10,8},{12,... | collective-permute-start | bytes 6291464 | tf_op jit(solution)/shard_map/ppermute | solution.py:62
  179.7 128.4 %collective-permute-start.15 = (bf16[2,2,256,1024]{3,2,1,0:T(8,128)(2,1)}, bf16[2,2,256,1024]{3,2,1,0:T(8,128)(2,1)}, u32[]{:S(2)}, u32[]{:S(2)}) collective-permute-start(bf16[2,2,256,1024]{3,2,1,0:T(8,128)(2,1)} %pad_maximum_fusion.8), channel_id=1, source_target_pairs={{0,4},{1,5},{2,3},{3,2},{4,0},{5,1},{6,7},{7,6},{8,12},{9,13},{10,... | collective-permute-start | bytes 6291464 | tf_op jit(solution)/shard_map/ppermute | solution.py:75
  181.6 128.5 %collective-permute-start.26 = (bf16[512,2048]{1,0:T(8,128)(2,1)}, bf16[512,2048]{1,0:T(8,128)(2,1)}, u32[]{:S(2)}, u32[]{:S(2)}) collective-permute-start(bf16[512,2048]{1,0:T(8,128)(2,1)} %pad_maximum_fusion.10), channel_id=1, source_target_pairs={{0,4},{2,6},{4,0},{6,2},{1,5},{3,7},{5,1},{7,3},{8,12},{10,14},{12... | collective-permute-start | bytes 6291464 | tf_op jit(solution)/shard_map/ppermute | solution.py:62
  185.0 99.7 %collective-permute-start.29 = (bf16[1024,512]{1,0:T(8,128)(2,1)}, bf16[1024,512]{1,0:T(8,128)(2,1)}, u32[]{:S(2)}, u32[]{:S(2)}) collective-permute-start(bf16[1024,512]{1,0:T(8,128)(2,1)} %get-tuple-element.59), channel_id=1, source_target_pairs={{0,4},{2,6},{4,0},{6,2},{1,5},{3,7},{5,1},{7,3},{8,12},{10,14},{12... | collective-permute-start | bytes 3145736 | tf_op jit(solution)/shard_map/ppermute | solution.py:62
  185.3 116.4 %collective-permute-start.30 = (bf16[1024,512]{1,0:T(8,128)(2,1)S(1)}, bf16[1024,512]{1,0:T(8,128)(2,1)}, u32[]{:S(2)}, u32[]{:S(2)}) collective-permute-start(bf16[1024,512]{1,0:T(8,128)(2,1)S(1)} %copy-done.45), channel_id=1, source_target_pairs={{0,6},{2,4},{4,2},{6,0},{1,7},{3,5},{5,3},{7,1},{8,14},{10,12},{12... | collective-permute-start | bytes 3145736 | tf_op jit(solution)/shard_map/ppermute | solution.py:62
  284.7 83.2 %collective-permute-start.27 = (bf16[512,2048]{1,0:T(8,128)(2,1)S(1)}, bf16[512,2048]{1,0:T(8,128)(2,1)S(1)}, u32[]{:S(2)}, u32[]{:S(2)}) collective-permute-start(bf16[512,2048]{1,0:T(8,128)(2,1)S(1)} %copy-done.37), channel_id=1, source_target_pairs={{0,6},{2,4},{4,2},{6,0},{1,7},{3,5},{5,3},{7,1},{8,14},{10,12},{12... | collective-permute-start | bytes 6291464 | tf_op jit(solution)/shard_map/ppermute | solution.py:62
  301.7 61.5 %collective-permute-start.36 = (bf16[2,256,1024]{2,1,0:T(8,128)(2,1)}, bf16[2,256,1024]{2,1,0:T(8,128)(2,1)S(1)}, u32[]{:S(2)}, u32[]{:S(2)}) collective-permute-start(bf16[2,256,1024]{2,1,0:T(8,128)(2,1)} %collective-permute-done.34), channel_id=1, source_target_pairs={{0,4},{1,5},{2,3},{3,2},{4,0},{5,1},{6,7},{7,6},{8,12},{9,13},{10,... | collective-permute-start | bytes 3145736 | tf_op jit(solution)/shard_map/ppermute | solution.py:75
  306.2 57.2 %collective-permute-start.39 = (bf16[2,256,1024]{2,1,0:T(8,128)(2,1)}, bf16[2,256,1024]{2,1,0:T(8,128)(2,1)S(1)}, u32[]{:S(2)}, u32[]{:S(2)}) collective-permute-start(bf16[2,256,1024]{2,1,0:T(8,128)(2,1)} %collective-permute-done.34), channel_id=1, source_target_pairs={{0,2},{2,0},{4,6},{6,4},{1,3},{3,1},{5,7},{7,5},{8,10},{10,8},{12,... | collective-permute-start | bytes 3145736 | tf_op jit(solution)/shard_map/ppermute | solution.py:62
  308.1 55.9 %collective-permute-start.38 = (bf16[2,256,1024]{2,1,0:T(8,128)(2,1)}, bf16[2,256,1024]{2,1,0:T(8,128)(2,1)S(1)}, u32[]{:S(2)}, u32[]{:S(2)}) collective-permute-start(bf16[2,256,1024]{2,1,0:T(8,128)(2,1)} %collective-permute-done.35), channel_id=1, source_target_pairs={{0,2},{2,0},{4,6},{6,4},{1,3},{3,1},{5,7},{7,5},{8,10},{10,8},{12,... | collective-permute-start | bytes 3145736 | tf_op jit(solution)/shard_map/ppermute | solution.py:62
  310.1 54.1 %collective-permute-start.16 = (bf16[2,256,1024]{2,1,0:T(8,128)(2,1)S(1)}, bf16[2,256,1024]{2,1,0:T(8,128)(2,1)S(1)}, u32[]{:S(2)}, u32[]{:S(2)}) collective-permute-start(bf16[2,256,1024]{2,1,0:T(8,128)(2,1)S(1)} %fusion.56), channel_id=1, source_target_pairs={{0,1},{1,0},{2,6},{3,7},{4,5},{5,4},{6,2},{7,3},{8,9},{9,8},{10,14... | collective-permute-start | bytes 3145736 | tf_op jit(solution)/shard_map/ppermute | solution.py:75
  512.9 50.1 %collective-permute-start.31 = (bf16[2,2,256,2048]{3,2,1,0:T(8,128)(2,1)}, bf16[2,2,256,2048]{3,2,1,0:T(8,128)(2,1)}, u32[]{:S(2)}, u32[]{:S(2)}) collective-permute-start(bf16[2,2,256,2048]{3,2,1,0:T(8,128)(2,1)} %bitcast.35), channel_id=1, source_target_pairs={{0,2},{2,0},{4,6},{6,4},{1,3},{3,1},{5,7},{7,5},{8,10},{10,8},{12,... | collective-permute-start | bytes 12582920 | tf_op jit(solution)/shard_map/ppermute | solution.py:62
  513.1 43.3 %collective-permute-start.41 = (bf16[2,2,256,2048]{3,2,1,0:T(8,128)(2,1)}, bf16[2,2,256,2048]{3,2,1,0:T(8,128)(2,1)S(1)}, u32[]{:S(2)}, u32[]{:S(2)}) collective-permute-start(bf16[2,2,256,2048]{3,2,1,0:T(8,128)(2,1)} %bitcast.44), channel_id=1, source_target_pairs={{0,2},{2,0},{4,6},{6,4},{1,3},{3,1},{5,7},{7,5},{8,10},{10,8},{12,... | collective-permute-start | bytes 12582920 | tf_op jit(solution)/shard_map/ppermute | solution.py:62
  553.2 27.4 %collective-permute-start.87 = (bf16[512,512]{1,0:T(8,128)(2,1)}, bf16[512,512]{1,0:T(8,128)(2,1)}, u32[]{:S(2)}, u32[]{:S(2)}) collective-permute-start(bf16[512,512]{1,0:T(8,128)(2,1)} %get-tuple-element.38), channel_id=1, source_target_pairs={{0,24},{8,0},{16,8},{24,16},{1,25},{9,1},{17,9},{25,17},{2,26},{10... | collective-permute-start | bytes 1572872 | tf_op jit(solution)/shard_map/ppermute | solution.py:67
  561.0 42.5 %collective-permute-start.42 = (bf16[2,2,256,1024]{3,2,1,0:T(8,128)(2,1)}, bf16[2,2,256,1024]{3,2,1,0:T(8,128)(2,1)S(1)}, u32[]{:S(2)}, u32[]{:S(2)}) collective-permute-start(bf16[2,2,256,1024]{3,2,1,0:T(8,128)(2,1)} %pad_maximum_fusion.13), channel_id=1, source_target_pairs={{0,4},{1,5},{2,3},{3,2},{4,0},{5,1},{6,7},{7,6},{8,12},{9,13},{10,... | collective-permute-start | bytes 6291464 | tf_op jit(solution)/shard_map/ppermute | solution.py:75
  569.9 79.7 %collective-permute-start.32 = (bf16[2,2,256,1024]{3,2,1,0:T(8,128)(2,1)}, bf16[2,2,256,1024]{3,2,1,0:T(8,128)(2,1)}, u32[]{:S(2)}, u32[]{:S(2)}) collective-permute-start(bf16[2,2,256,1024]{3,2,1,0:T(8,128)(2,1)} %pad_maximum_fusion.12), channel_id=1, source_target_pairs={{0,4},{1,5},{2,3},{3,2},{4,0},{5,1},{6,7},{7,6},{8,12},{9,13},{10,... | collective-permute-start | bytes 6291464 | tf_op jit(solution)/shard_map/ppermute | solution.py:75
  572.6 33.1 %collective-permute-start.74 = (bf16[256,2048]{1,0:T(8,128)(2,1)}, bf16[256,2048]{1,0:T(8,128)(2,1)}, u32[]{:S(2)}, u32[]{:S(2)}) collective-permute-start(bf16[256,2048]{1,0:T(8,128)(2,1)} %get-tuple-element.33), channel_id=1, source_target_pairs={{0,8},{8,16},{16,24},{24,0},{1,9},{9,17},{17,25},{25,1},{2,10},{10... | collective-permute-start | bytes 3145736 | tf_op jit(solution)/shard_map/ppermute | solution.py:67
  572.6 52.9 %collective-permute-start.77 = (bf16[256,2048]{1,0:T(8,128)(2,1)S(1)}, bf16[256,2048]{1,0:T(8,128)(2,1)}, u32[]{:S(2)}, u32[]{:S(2)}) collective-permute-start(bf16[256,2048]{1,0:T(8,128)(2,1)S(1)} %get-tuple-element.32), channel_id=1, source_target_pairs={{0,24},{8,0},{16,8},{24,16},{1,25},{9,1},{17,9},{25,17},{2,26},{10... | collective-permute-start | bytes 3145736 | tf_op jit(solution)/shard_map/ppermute | solution.py:67
  582.6 54.0 %collective-permute-start.85 = (bf16[512,512]{1,0:T(8,128)(2,1)S(1)}, bf16[512,512]{1,0:T(8,128)(2,1)S(1)}, u32[]{:S(2)}, u32[]{:S(2)}) collective-permute-start(bf16[512,512]{1,0:T(8,128)(2,1)S(1)} %get-tuple-element.37), channel_id=1, source_target_pairs={{0,8},{8,16},{16,24},{24,0},{1,9},{9,17},{17,25},{25,1},{2,10},{10... | collective-permute-start | bytes 1572872 | tf_op jit(solution)/shard_map/ppermute | solution.py:67
  603.5 44.3 %collective-permute-start.88 = (bf16[512,512]{1,0:T(8,128)(2,1)S(1)}, bf16[512,512]{1,0:T(8,128)(2,1)S(1)}, u32[]{:S(2)}, u32[]{:S(2)}) collective-permute-start(bf16[512,512]{1,0:T(8,128)(2,1)S(1)} %get-tuple-element.36), channel_id=1, source_target_pairs={{0,24},{8,0},{16,8},{24,16},{1,25},{9,1},{17,9},{25,17},{2,26},{10... | collective-permute-start | bytes 1572872 | tf_op jit(solution)/shard_map/ppermute | solution.py:67
  605.7 47.1 %collective-permute-start.43 = (bf16[2,256,1024]{2,1,0:T(8,128)(2,1)S(1)}, bf16[2,256,1024]{2,1,0:T(8,128)(2,1)S(1)}, u32[]{:S(2)}, u32[]{:S(2)}) collective-permute-start(bf16[2,256,1024]{2,1,0:T(8,128)(2,1)S(1)} %fusion.60), channel_id=1, source_target_pairs={{0,1},{1,0},{2,6},{3,7},{4,5},{5,4},{6,2},{7,3},{8,9},{9,8},{10,14... | collective-permute-start | bytes 3145736 | tf_op jit(solution)/shard_map/ppermute | solution.py:75
  628.5 41.7 %collective-permute-start.75 = (bf16[256,2048]{1,0:T(8,128)(2,1)S(1)}, bf16[256,2048]{1,0:T(8,128)(2,1)S(1)}, u32[]{:S(2)}, u32[]{:S(2)}) collective-permute-start(bf16[256,2048]{1,0:T(8,128)(2,1)S(1)} %get-tuple-element.31), channel_id=1, source_target_pairs={{0,8},{8,16},{16,24},{24,0},{1,9},{9,17},{17,25},{25,1},{2,10},{10... | collective-permute-start | bytes 3145736 | tf_op jit(solution)/shard_map/ppermute | solution.py:67
  636.6 54.2 %collective-permute-start.78 = (bf16[256,2048]{1,0:T(8,128)(2,1)S(1)}, bf16[256,2048]{1,0:T(8,128)(2,1)S(1)}, u32[]{:S(2)}, u32[]{:S(2)}) collective-permute-start(bf16[256,2048]{1,0:T(8,128)(2,1)S(1)} %get-tuple-element.30), channel_id=1, source_target_pairs={{0,24},{8,0},{16,8},{24,16},{1,25},{9,1},{17,9},{25,17},{2,26},{10... | collective-permute-start | bytes 3145736 | tf_op jit(solution)/shard_map/ppermute | solution.py:67
  649.5 54.8 %collective-permute-start.89 = (bf16[1024,128]{1,0:T(8,128)(2,1)S(1)}, bf16[1024,128]{1,0:T(8,128)(2,1)S(1)}, u32[]{:S(2)}, u32[]{:S(2)}) collective-permute-start(bf16[1024,128]{1,0:T(8,128)(2,1)S(1)} %get-tuple-element.96), channel_id=1, source_target_pairs={{0,2},{2,0},{4,6},{6,4},{1,3},{3,1},{5,7},{7,5},{8,10},{10,8},{12,... | collective-permute-start | bytes 786440 | tf_op jit(solution)/shard_map/ppermute | solution.py:62
  651.4 44.5 %collective-permute-start.33 = (bf16[2,256,1024]{2,1,0:T(8,128)(2,1)S(1)}, bf16[2,256,1024]{2,1,0:T(8,128)(2,1)S(1)}, u32[]{:S(2)}, u32[]{:S(2)}) collective-permute-start(bf16[2,256,1024]{2,1,0:T(8,128)(2,1)S(1)} %fusion.58), channel_id=1, source_target_pairs={{0,1},{1,0},{2,6},{3,7},{4,5},{5,4},{6,2},{7,3},{8,9},{9,8},{10,14... | collective-permute-start | bytes 3145736 | tf_op jit(solution)/shard_map/ppermute | solution.py:75
  653.8 42.1 %collective-permute-start.44 = (f32[2,256,1]{1,0,2:T(2,128)S(1)}, f32[2,256,1]{1,0,2:T(2,128)S(1)}, u32[]{:S(2)}, u32[]{:S(2)}) collective-permute-start(f32[2,256,1]{1,0,2:T(2,128)S(1)} %bitcast.319), channel_id=1, source_target_pairs={{0,1},{1,0},{2,3},{3,2},{4,5},{5,4},{6,7},{7,6},{8,9},{9,8},{10,11... | collective-permute-start | bytes 6152 | tf_op jit(solution)/shard_map/ppermute | solution.py:62
  691.7 40.8 %collective-permute-start.76 = (bf16[256,2048]{1,0:T(8,128)(2,1)S(1)}, bf16[256,2048]{1,0:T(8,128)(2,1)S(1)}, u32[]{:S(2)}, u32[]{:S(2)}) collective-permute-start(bf16[256,2048]{1,0:T(8,128)(2,1)S(1)} %get-tuple-element.29), channel_id=1, source_target_pairs={{0,8},{8,16},{16,24},{24,0},{1,9},{9,17},{17,25},{25,1},{2,10},{10... | collective-permute-start | bytes 3145736 | tf_op jit(solution)/shard_map/ppermute | solution.py:67
  692.0 46.9 %collective-permute-start.79 = (bf16[256,2048]{1,0:T(8,128)(2,1)S(1)}, bf16[256,2048]{1,0:T(8,128)(2,1)S(1)}, u32[]{:S(2)}, u32[]{:S(2)}) collective-permute-start(bf16[256,2048]{1,0:T(8,128)(2,1)S(1)} %get-tuple-element.28), channel_id=1, source_target_pairs={{0,24},{8,0},{16,8},{24,16},{1,25},{9,1},{17,9},{25,17},{2,26},{10... | collective-permute-start | bytes 3145736 | tf_op jit(solution)/shard_map/ppermute | solution.py:67
  699.9 30.7 %collective-permute-start.45 = (bf16[2,256,1024]{2,1,0:T(8,128)(2,1)S(1)}, bf16[2,256,1024]{2,1,0:T(8,128)(2,1)S(1)}, u32[]{:S(2)}, u32[]{:S(2)}) collective-permute-start(bf16[2,256,1024]{2,1,0:T(8,128)(2,1)S(1)} %get-tuple-element.17), channel_id=1, source_target_pairs={{0,1},{1,0},{2,6},{3,7},{4,5},{5,4},{6,2},{7,3},{8,9},{9,8},{10,14... | collective-permute-start | bytes 3145736 | tf_op jit(solution)/shard_map/ppermute | solution.py:75
  704.3 26.3 %collective-permute-start.91 = (bf16[1024,128]{1,0:T(8,128)(2,1)S(1)}, bf16[1024,128]{1,0:T(8,128)(2,1)S(1)}, u32[]{:S(2)}, u32[]{:S(2)}) collective-permute-start(bf16[1024,128]{1,0:T(8,128)(2,1)S(1)} %get-tuple-element.95), channel_id=1, source_target_pairs={{0,6},{2,4},{4,2},{6,0},{1,7},{3,5},{5,3},{7,1},{8,14},{10,12},{12... | collective-permute-start | bytes 786440 | tf_op jit(solution)/shard_map/ppermute | solution.py:62
  711.6 31.4 %collective-permute-start.46 = (bf16[2,256,1024]{2,1,0:T(8,128)(2,1)S(1)}, bf16[2,256,1024]{2,1,0:T(8,128)(2,1)S(1)}, u32[]{:S(2)}, u32[]{:S(2)}) collective-permute-start(bf16[2,256,1024]{2,1,0:T(8,128)(2,1)S(1)} %get-tuple-element.17), channel_id=1, source_target_pairs={{0,4},{1,5},{2,3},{3,2},{4,0},{5,1},{6,7},{7,6},{8,12},{9,13},{10,... | collective-permute-start | bytes 3145736 | tf_op jit(solution)/shard_map/ppermute | solution.py:75
  742.5 77.1 %collective-permute-start.80 = (bf16[128,2048]{1,0:T(8,128)(2,1)}, bf16[128,2048]{1,0:T(8,128)(2,1)}, u32[]{:S(2)}, u32[]{:S(2)}) collective-permute-start(bf16[128,2048]{1,0:T(8,128)(2,1)} %get-tuple-element.68), channel_id=1, source_target_pairs={{0,2},{2,0},{4,6},{6,4},{1,3},{3,1},{5,7},{7,5},{8,10},{10,8},{12,... | collective-permute-start | bytes 1572872 | tf_op jit(solution)/shard_map/ppermute | solution.py:62
  750.5 71.1 %collective-permute-start.81 = (bf16[128,2048]{1,0:T(8,128)(2,1)}, bf16[128,2048]{1,0:T(8,128)(2,1)}, u32[]{:S(2)}, u32[]{:S(2)}) collective-permute-start(bf16[128,2048]{1,0:T(8,128)(2,1)} %get-tuple-element.69), channel_id=1, source_target_pairs={{0,4},{2,6},{4,0},{6,2},{1,5},{3,7},{5,1},{7,3},{8,12},{10,14},{12... | collective-permute-start | bytes 1572872 | tf_op jit(solution)/shard_map/ppermute | solution.py:62
  752.2 71.3 %collective-permute-start.82 = (bf16[128,2048]{1,0:T(8,128)(2,1)}, bf16[128,2048]{1,0:T(8,128)(2,1)}, u32[]{:S(2)}, u32[]{:S(2)}) collective-permute-start(bf16[128,2048]{1,0:T(8,128)(2,1)} %get-tuple-element.66), channel_id=1, source_target_pairs={{0,6},{2,4},{4,2},{6,0},{1,7},{3,5},{5,3},{7,1},{8,14},{10,12},{12... | collective-permute-start | bytes 1572872 | tf_op jit(solution)/shard_map/ppermute | solution.py:62
  818.8 53.1 %collective-permute-start.52 = (bf16[2,2,256,2048]{3,2,1,0:T(8,128)(2,1)S(1)}, bf16[2,2,256,2048]{3,2,1,0:T(8,128)(2,1)S(1)}, u32[]{:S(2)}, u32[]{:S(2)}) collective-permute-start(bf16[2,2,256,2048]{3,2,1,0:T(8,128)(2,1)S(1)} %bitcast.322), channel_id=1, source_target_pairs={{0,2},{2,0},{4,6},{6,4},{1,3},{3,1},{5,7},{7,5},{8,10},{10,8},{12,... | collective-permute-start | bytes 12582920 | tf_op jit(solution)/shard_map/ppermute | solution.py:62
  867.7 37.5 %collective-permute-start.58 = (bf16[256,384]{1,0:T(8,128)(2,1)S(1)}, bf16[256,384]{1,0:T(8,128)(2,1)S(1)}, u32[]{:S(2)}, u32[]{:S(2)}) collective-permute-start(bf16[256,384]{1,0:T(8,128)(2,1)S(1)} %get-tuple-element.90), channel_id=1, source_target_pairs={{0,8},{8,16},{16,24},{24,0},{1,9},{9,17},{17,25},{25,1},{2,10},{10... | collective-permute-start | bytes 589832 | tf_op jit(solution)/shard_map/ppermute | solution.py:67
  867.8 38.3 %collective-permute-start.61 = (bf16[256,384]{1,0:T(8,128)(2,1)S(1)}, bf16[256,384]{1,0:T(8,128)(2,1)S(1)}, u32[]{:S(2)}, u32[]{:S(2)}) collective-permute-start(bf16[256,384]{1,0:T(8,128)(2,1)S(1)} %get-tuple-element.89), channel_id=1, source_target_pairs={{0,24},{8,0},{16,8},{24,16},{1,25},{9,1},{17,9},{25,17},{2,26},{10... | collective-permute-start | bytes 589832 | tf_op jit(solution)/shard_map/ppermute | solution.py:67
  876.8 36.5 %collective-permute-start.53 = (bf16[2,2,256,1024]{3,2,1,0:T(8,128)(2,1)}, bf16[2,2,256,1024]{3,2,1,0:T(8,128)(2,1)}, u32[]{:S(2)}, u32[]{:S(2)}) collective-permute-start(bf16[2,2,256,1024]{3,2,1,0:T(8,128)(2,1)} %pad_maximum_fusion.14), channel_id=1, source_target_pairs={{0,4},{1,5},{2,3},{3,2},{4,0},{5,1},{6,7},{7,6},{8,12},{9,13},{10,... | collective-permute-start | bytes 6291464 | tf_op jit(solution)/shard_map/ppermute | solution.py:75
  878.8 26.4 %collective-permute-start.72 = (bf16[256,128]{1,0:T(8,128)(2,1)S(1)}, bf16[256,128]{1,0:T(8,128)(2,1)S(1)}, u32[]{:S(2)}, u32[]{:S(2)}) collective-permute-start(bf16[256,128]{1,0:T(8,128)(2,1)S(1)} %get-tuple-element.132), channel_id=1, source_target_pairs={{0,4},{2,6},{4,0},{6,2},{1,5},{3,7},{5,1},{7,3},{8,12},{10,14},{12... | collective-permute-start | bytes 196616 | tf_op jit(solution)/shard_map/ppermute | solution.py:62
  935.3 32.2 %collective-permute-start.55 = (f32[2,256,1]{1,0,2:T(2,128)S(1)}, f32[2,256,1]{1,0,2:T(2,128)S(1)}, u32[]{:S(2)}, u32[]{:S(2)}) collective-permute-start(f32[2,256,1]{1,0,2:T(2,128)S(1)} %bitcast.318), channel_id=1, source_target_pairs={{0,1},{1,0},{2,3},{3,2},{4,5},{5,4},{6,7},{7,6},{8,9},{9,8},{10,11... | collective-permute-start | bytes 6152 | tf_op jit(solution)/shard_map/ppermute | solution.py:62
  (136 other events, 2286.5 us)

commit v2 on v1

v2 whole, which is shorter than its diff:
```python
import functools

import jax
import jax.numpy as jnp
from jax import lax
from jax.experimental import pallas as pl
from jax.experimental.pallas import tpu as pltpu
from jax.sharding import PartitionSpec as P

HD = 64
EPS = 1e-05
NEGATIVE = -1e30
BF = jnp.bfloat16


def inverse_frequency(head_size):
    exponent = jnp.arange(0, head_size, 2, dtype=jnp.int32).astype(jnp.float32) / head_size
    plain = 1.0 / jnp.power(jnp.float32(500000.0), exponent)
    factor = 32.0
    old_context = 8192.0
    wavelength = 2.0 * jnp.pi / plain
    smooth = (old_context / wavelength - 1.0) / (4.0 - 1.0)
    scaled = jnp.where(wavelength > old_context, plain / factor, plain)
    middle = (wavelength <= old_context) & (wavelength >= old_context / 4.0)
    scaled = jnp.where(middle, (1.0 - smooth) * plain / factor + smooth * plain, scaled)
    return scaled


def rotation_tables(span):
    positions = jnp.arange(span, dtype=jnp.int32).astype(jnp.float32)
    angle = positions[:, None] * inverse_frequency(HD)[None, :]
    cosine = jnp.cos(angle)
    sine = jnp.sin(angle)
    one = jnp.ones((span, HD), jnp.float32)
    turning = jnp.concatenate([cosine, cosine], axis=1)
    crossing = jnp.concatenate([-sine, sine], axis=1)
    return jnp.stack(
        [
            jnp.concatenate([turning, turning], axis=1),
            jnp.concatenate([crossing, crossing], axis=1),
            jnp.concatenate([turning, one], axis=1),
            jnp.concatenate([crossing, 0.0 * one], axis=1),
        ]
    )


def rotate_lanes(values, tables, rows, sign):
    chunks = values.shape[1] // 128
    lanes = lax.broadcasted_iota(jnp.int32, (values.shape[0], 128), 1)
    first = lanes % HD < HD // 2
    turned = []
    for chunk in range(chunks):
        part = values[:, chunk * 128 : chunk * 128 + 128]
        other = jnp.where(
            first, pltpu.roll(part, 128 - HD // 2, 1), pltpu.roll(part, HD // 2, 1)
        )
        table = 2 if chunk == chunks - 1 else 0
        turned.append(part * tables[table, rows] + sign * other * tables[table + 1, rows])
    return jnp.concatenate(turned, axis=1)


def split_heads(refs, values, rows, heads):
    for head in range(heads):
        refs[0][head, rows] = values[:, head * HD : head * HD + HD]
    if len(refs) > 1:
        refs[1][rows] = values[:, heads * HD : heads * HD + HD]
        refs[2][rows] = values[:, heads * HD + HD :]


def masked_probs(query, keys, limit):
    scores = lax.dot_general(
        query, keys, (((1,), (1,)), ((), ())), preferred_element_type=jnp.float32
    )
    columns = lax.broadcasted_iota(jnp.int32, scores.shape, 1)
    scores = jnp.where(columns < limit, scores * HD ** (-0.5), NEGATIVE)
    powers = jnp.exp(scores - jnp.max(scores, axis=1, keepdims=True))
    return powers * (1.0 / jnp.sum(powers, axis=1, keepdims=True))


def row_limit(start, rows, length):
    positions = start + lax.broadcasted_iota(jnp.int32, (rows, 1), 0)
    return jnp.minimum(positions + 1, length)


def forward_kernel(heads, order, lengths, projected, tables, rotated, attended, qs, ks, vs, outs):
    blocks, _, rows, _ = projected.shape
    length = lengths[pl.program_id(0)]
    for block in range(blocks):
        where = pl.ds(block * rows, rows)
        turned = rotate_lanes(projected[order[block], 0], tables, where, 1.0).astype(BF)
        rotated[order[block], 0] = turned
        split_heads((qs, ks, vs), turned, where, heads)
    for block in range(blocks):
        where = pl.ds(block * rows, rows)
        extent = (block + 1) * rows
        limit = row_limit(block * rows, rows, length)

        def one_head(head, carry):
            probs = masked_probs(qs[head, where], ks[:extent], limit).astype(BF)
            outs[head] = matmul(probs, vs[:extent]).astype(BF)
            return carry

        lax.fori_loop(0, heads, one_head, 0)
        attended[order[block], 0] = jnp.concatenate([outs[h] for h in range(heads)], axis=1)


def backward_kernel(
    heads, order, lengths, rotated, grads, tables, back, qs, ks, vs, gs, dqs, dks, dvs
):
    blocks, _, rows, _ = rotated.shape
    length = lengths[pl.program_id(0)]
    scale = HD ** (-0.5)
    for block in range(blocks):
        where = pl.ds(block * rows, rows)
        split_heads((qs, ks, vs), rotated[order[block], 0], where, heads)
        split_heads((gs,), grads[order[block], 0], where, heads)
    dks[...] = jnp.zeros_like(dks)
    dvs[...] = jnp.zeros_like(dvs)
    for block in range(blocks):
        where = pl.ds(block * rows, rows)
        extent = (block + 1) * rows
        limit = row_limit(block * rows, rows, length)

        def one_head(head, carry):
            query = qs[head, where]
            grad = gs[head, where]
            keys = ks[:extent]
            probs = masked_probs(query, keys, limit)
            grad_probs = lax.dot_general(
                grad, vs[:extent], (((1,), (1,)), ((), ())), preferred_element_type=jnp.float32
            )
            delta = jnp.sum(probs * grad_probs, axis=1, keepdims=True)
            grad_scores = (probs * ((grad_probs - delta) * scale)).astype(BF)
            dqs[head, where] = matmul(grad_scores, keys)
            down = (((0,), (0,)), ((), ()))
            dks[:extent] += lax.dot_general(
                grad_scores, query, down, preferred_element_type=jnp.float32
            )
            dvs[:extent] += lax.dot_general(
                probs.astype(BF), grad, down, preferred_element_type=jnp.float32
            )
            return carry

        lax.fori_loop(0, heads, one_head, 0)
    for block in range(blocks):
        where = pl.ds(block * rows, rows)
        parts = [dqs[h, where] for h in range(heads)] + [dks[where], dvs[where]]
        turned = rotate_lanes(jnp.concatenate(parts, axis=1), tables, where, -1.0)
        back[order[block], 0] = turned.astype(BF)


def slot_spec(shape):
    blocks, _, rows, columns = shape
    return pl.BlockSpec((blocks, 1, rows, columns), lambda slot, *_: (0, slot, 0, 0))


def attention_call(kernel, backward, order, lengths, arrays, tables, outs, scratch, heads):
    blocks, slots, rows, _ = arrays[0].shape
    span = blocks * rows
    work = slots * heads * span * span * HD * (10 if backward else 4) * 5 // 8
    return pl.pallas_call(
        functools.partial(kernel, heads),
        grid_spec=pltpu.PrefetchScalarGridSpec(
            num_scalar_prefetch=2,
            grid=(slots,),
            in_specs=[slot_spec(item.shape) for item in arrays]
            + [pl.BlockSpec(tables.shape, lambda slot, *_: (0, 0, 0))],
            out_specs=[slot_spec(item.shape) for item in outs],
            scratch_shapes=scratch,
        ),
        out_shape=outs,
        compiler_params=pltpu.CompilerParams(vmem_limit_bytes=48 * 2**20),
        cost_estimate=pl.CostEstimate(
            flops=work * 4, bytes_accessed=16 * 2**20, transcendentals=slots * heads * span * span
        ),
    )(order, lengths, *arrays, tables)


def attention_forward(projected, tables, order, lengths):
    blocks, slots, rows, columns = projected.shape
    heads = columns // HD - 2
    span = blocks * rows
    outs = [
        jax.ShapeDtypeStruct(projected.shape, BF),
        jax.ShapeDtypeStruct((blocks, slots, rows, heads * HD), BF),
    ]
    scratch = [
        pltpu.VMEM((heads, span, HD), BF),
        pltpu.VMEM((span, HD), BF),
        pltpu.VMEM((span, HD), BF),
        pltpu.VMEM((heads, rows, HD), BF),
    ]
    return attention_call(
        forward_kernel, False, order, lengths, [projected], tables, outs, scratch, heads
    )


def attention_backward(rotated, grads, tables, order, lengths):
    blocks, slots, rows, columns = rotated.shape
    heads = columns // HD - 2
    span = blocks * rows
    scratch = [
        pltpu.VMEM((heads, span, HD), BF),
        pltpu.VMEM((span, HD), BF),
        pltpu.VMEM((span, HD), BF),
        pltpu.VMEM((heads, span, HD), BF),
        pltpu.VMEM((heads, span, HD), jnp.float32),
        pltpu.VMEM((span, HD), jnp.float32),
        pltpu.VMEM((span, HD), jnp.float32),
    ]
    outs = [jax.ShapeDtypeStruct(rotated.shape, BF)]
    return attention_call(
        backward_kernel, True, order, lengths, [rotated, grads], tables, outs, scratch, heads
    )[0]


def matmul(left, right):
    return jnp.dot(left, right, preferred_element_type=jnp.float32)


class Plan:
    def __init__(self):
        self.place = lax.axis_index("ctx")
        self.side = lax.axis_index("tensor")
        self.group = lax.axis_index("dp")
        self.parts = lax.axis_size("ctx")
        self.sides = lax.axis_size("tensor")
        self.groups = lax.axis_size("dp")
        self.fast = self.parts == 4 and self.sides == 2 and self.groups == 4
        self.core = self.place % 2
        self.masks = (0, 2, 1, 3) if self.fast else tuple(range(self.parts))

    def member(self, block):
        return self.place ^ self.masks[block] if self.fast else block

    def storage(self):
        if not self.fast:
            return jnp.arange(self.parts, dtype=jnp.int32)
        apart = self.place ^ jnp.arange(self.parts, dtype=jnp.int32)
        return (apart % 2) * 2 + apart // 2

    def half(self, index):
        return self.side ^ index if self.fast else index

    def ordered(self, block, count):
        return block ^ (self.side * (count // 2)) if self.fast else block


def after(values, anchor):
    return lax.optimization_barrier((values, anchor))[0]


def swap(values, axis, mask):
    size = lax.axis_size(axis)
    return lax.ppermute(values, axis, [(i, i ^ mask) for i in range(size)])


def shift(values, axis, step):
    size = lax.axis_size(axis)
    return lax.ppermute(values, axis, [(i, (i + step) % size) for i in range(size)])


def turn(values, first):
    pairs = []
    for i in range(8):
        along_tensor = (((i >> 1) & 1) == 0) == first
        pairs.append((i, i ^ 1 if along_tensor else i ^ 4))
    return lax.ppermute(values, ("ctx", "tensor"), pairs)


def gather_rows(plan, values):
    if not plan.fast:
        wide = lax.all_gather(values, "tensor", axis=2, tiled=True)
        return lax.all_gather(wide, "ctx", axis=0)
    one = turn(values, True)
    two = turn(values, False)
    far = turn(one, False)
    core_own = swap(values, "ctx", 1)
    core_one = swap(one, "ctx", 1)
    core_two = swap(two, "ctx", 1)
    core_far = swap(far, "ctx", 1)
    zero = plan.core == 0
    rows = [
        jnp.concatenate([values, jnp.where(zero, one, two)], axis=2),
        jnp.concatenate([jnp.where(zero, two, one), far], axis=2),
        jnp.concatenate([core_own, jnp.where(zero, core_two, core_one)], axis=2),
        jnp.concatenate([jnp.where(zero, core_one, core_two), core_far], axis=2),
    ]
    return jnp.stack(rows)


def scatter_rows(plan, left, right, slots):
    width = right.shape[-1]
    if not plan.fast:
        whole = matmul(left, right).astype(BF).reshape(plan.parts, slots, -1, width)
        narrow = lax.psum_scatter(whole, "tensor", scatter_dimension=3, tiled=True)
        return lax.psum_scatter(narrow, "ctx", scatter_dimension=0, tiled=False).astype(jnp.float32)
    half = left.shape[0] // 2
    away = matmul(left[half:], right).astype(BF).reshape(2, slots, -1, width)
    here = matmul(left[:half], right).astype(BF).reshape(2, slots, -1, width)
    return scatter_blocks(plan, here, away)


def add(left, right):
    return (left.astype(jnp.float32) + right.astype(jnp.float32)).astype(BF)


def scatter_blocks(plan, here, away):
    width = here.shape[-1] // 2
    both = add(here, swap(away, "ctx", 1))
    zero = plan.core == 0
    near = both[0, :, :, :width]
    by_tensor = both[0, :, :, width:]
    by_ctx = both[1, :, :, :width]
    far = both[1, :, :, width:]
    got = turn(jnp.stack([jnp.where(zero, by_ctx, by_tensor), far]), False)
    kept = add(near, got[0])
    sent = add(jnp.where(zero, by_tensor, by_ctx), got[1])
    return kept.astype(jnp.float32) + turn(sent, True).astype(jnp.float32)


def exchange_pieces(plan, piece, shared=False):
    found = [(plan.place, 0, piece(plan.place))]
    if not (shared and plan.fast):
        for mask in range(1, plan.parts):
            other = plan.place ^ mask
            found.append((other, 0, swap(piece(other), "ctx", mask)))
        return found
    found.append((plan.place ^ 1, 0, swap(piece(plan.place ^ 1), "ctx", 1)))
    size = found[0][2].shape[0] // plan.groups
    got = []
    for mask in (2, 3):
        mine = lax.dynamic_slice_in_dim(piece(plan.place ^ mask), plan.group * size, size, 0)
        got.append(swap(mine, "ctx", mask))
    whole = lax.all_gather(jnp.stack(got), "dp")
    for index, mask in enumerate((2, 3)):
        found.append((plan.place ^ mask, 0, whole[:, index].reshape(-1, whole.shape[-1])))
    return found


def place_rows(plan, found, height):
    columns = found[0][2].shape[1]
    whole = jnp.zeros((height * plan.parts, columns), found[0][2].dtype)
    for member, row, piece in found:
        start = plan.ordered(member, plan.parts) * height + row
        whole = lax.dynamic_update_slice(whole, piece, (start, 0))
    return whole


def place_columns(plan, found, height):
    columns = found[0][2].shape[1]
    whole = jnp.zeros((height, columns * plan.parts), found[0][2].dtype)
    for member, row, piece in found:
        start = plan.ordered(member, plan.parts) * columns
        whole = lax.dynamic_update_slice(whole, piece, (row, start))
    return whole


def column_piece(weights, parts, least=1):
    def piece(member):
        taken = []
        for weight in weights:
            share = max(1, least * parts // weight.shape[1])
            size = weight.shape[1] * share // parts
            taken.append(lax.dynamic_slice_in_dim(weight, member // share * size, size, 1))
        return jnp.concatenate(taken, axis=1)

    return piece


def row_piece(weight, parts):
    size = weight.shape[0] // parts

    def piece(member):
        return lax.dynamic_slice_in_dim(weight, member * size, size, 0)

    return piece


def gradient_kernel(side, left, right, out):
    total = lax.dot_general(
        left[...], right[...], (((0,), (0,)), ((), ())), preferred_element_type=jnp.float32
    )
    out[...] = total.astype(out.dtype).reshape(out.shape)


def weight_gradient(plan, left, right, features_first):
    tokens, height = left.shape
    width = right.shape[1]
    groups = plan.groups
    flip = groups // 2 if plan.fast else 0
    tall = height // groups if features_first else height
    broad = width if features_first else width // groups
    step = min(broad, 1024)
    lines = min(tall, 512)

    def at(i, j, side):
        group, line = (i // (tall // lines), i % (tall // lines)) if features_first else (j, i)
        column = j if features_first else 0
        return (group + flip * side[0]) % groups, line, column

    return pl.pallas_call(
        gradient_kernel,
        grid_spec=pltpu.PrefetchScalarGridSpec(
            num_scalar_prefetch=1,
            grid=(height // lines, width // step),
            in_specs=[
                pl.BlockSpec((tokens, lines), lambda i, j, side: (0, i)),
                pl.BlockSpec((tokens, step), lambda i, j, side: (0, j)),
            ],
            out_specs=pl.BlockSpec((1, lines, step), at),
        ),
        out_shape=jax.ShapeDtypeStruct((groups, tall, broad), BF),
        compiler_params=pltpu.CompilerParams(vmem_limit_bytes=48 * 2**20),
        cost_estimate=pl.CostEstimate(
            flops=2 * tokens * height * width,
            bytes_accessed=2 * (tokens * (height + width) + height * width),
            transcendentals=0,
        ),
    )(plan.side[None].astype(jnp.int32), left, right)


def reduce_groups(grad):
    return lax.psum_scatter(grad, "dp", scatter_dimension=0)


def finish_columns(plan, part, widths):
    rows = part.shape[0]
    found = exchange_pieces(plan, row_piece(part, plan.parts))
    outs = []
    start = 0
    for width, share in widths:
        whole = jnp.zeros((rows // plan.parts, width * plan.parts // share), jnp.float32)
        for member, _, piece in found:
            block = piece[:, start : start + width].astype(jnp.float32)
            at = member // share * width
            if share > 1:
                block = block + lax.dynamic_slice_in_dim(whole, at, width, 1)
            whole = lax.dynamic_update_slice(whole, block, (0, at))
        outs.append(whole)
        start += width
    return outs


def finish_rows(plan, part):
    height, columns = part.shape
    found = exchange_pieces(plan, column_piece([part], plan.parts))
    whole = jnp.zeros((height * plan.parts, columns // plan.parts), jnp.float32)
    for member, _, piece in found:
        whole = lax.dynamic_update_slice(whole, piece.astype(jnp.float32), (member * height, 0))
    return whole


def total_over(values, axis):
    mask = 1
    while mask < lax.axis_size(axis):
        values = values + swap(values, axis, mask)
        mask *= 2
    return values


def feature_total(values):
    total = jnp.sum(values, axis=-1, keepdims=True)
    if lax.axis_size("tensor") == 2:
        return total + swap(total, "tensor", 1)
    return lax.psum(total, "tensor")


def per_device(
    inputs,
    cotangent,
    lengths,
    deal_order,
    query_weight,
    key_weight,
    value_weight,
    output_weight,
    gate_weight,
    up_weight,
    down_weight,
    attention_gain,
    feedforward_gain,
):
    plan = Plan()
    slots, rows, half_width = inputs.shape
    width = half_width * plan.sides
    parts = plan.parts
    groups = plan.groups
    sequences = lengths.shape[0]
    tokens = parts * slots * rows
    ids = jnp.arange(sequences, dtype=jnp.int32)
    own_ids = plan.group * slots + jnp.arange(slots, dtype=jnp.int32)
    slot_lengths = lax.dynamic_slice_in_dim(lengths, plan.group * slots, slots)
    dealt = jnp.sum(jnp.where(deal_order[:, None] == ids[None, :], lengths[None, :], 0), axis=1)
    totals = jnp.sum(dealt.reshape(groups, -1), axis=1)
    found = jnp.where(deal_order[None, :] == own_ids[:, None], ids[None, :], 0)
    owner = jnp.sum(found, axis=1) // (sequences // groups)
    mine = owner[:, None] == jnp.arange(groups, dtype=jnp.int32)[None, :]
    own_totals = jnp.sum(jnp.where(mine, totals[None, :], 0), axis=1)
    scale = jnp.sum(lengths).astype(jnp.float32) / groups / own_totals.astype(jnp.float32)

    starts = jnp.stack([plan.member(j) for j in range(parts)]).astype(jnp.int32) * rows
    positions = starts[:, None] + jnp.arange(rows, dtype=jnp.int32)[None, :]
    own_rows = plan.place * rows + jnp.arange(rows, dtype=jnp.int32)
    valid = positions[:, None, :] < slot_lengths[None, :, None]
    own_valid = own_rows[None, :] < slot_lengths[:, None]
    tables = rotation_tables(parts * rows)
    order = plan.storage()

    source = inputs.astype(jnp.float32)
    inverse_one = lax.rsqrt(feature_total(source * source) / width + EPS)
    normed = gather_rows(plan, (source * inverse_one * attention_gain).astype(BF))
    normed = normed.reshape(tokens, width)
    qkv_w = place_rows(
        plan,
        exchange_pieces(plan, column_piece([query_weight, key_weight, value_weight], parts, HD)),
        query_weight.shape[0],
    )
    late = after((output_weight, gate_weight, up_weight, down_weight, cotangent), normed)
    o_w = place_columns(
        plan, exchange_pieces(plan, row_piece(late[0], parts)), output_weight.shape[0] // parts
    )
    pair_w = place_rows(
        plan,
        exchange_pieces(plan, column_piece([late[1], late[2]], parts), True),
        gate_weight.shape[0],
    )
    down_w = place_columns(
        plan, exchange_pieces(plan, row_piece(late[3], parts), True), down_weight.shape[0] // parts
    )
    target_all = gather_rows(plan, late[4]).astype(jnp.float32)
    target_all = (target_all * valid[..., None] * scale[None, :, None, None]).astype(BF)
    target_all = target_all.reshape(tokens, width)

    wide = query_weight.shape[1] // parts
    share = max(1, HD * parts // key_weight.shape[1])
    narrow = key_weight.shape[1] * share // parts
    projected = matmul(normed, qkv_w).reshape(parts, slots, rows, -1)
    rotated, attended = attention_forward(projected, tables, order, slot_lengths)
    attended = attended.reshape(tokens, wide)
    hidden = source + scatter_rows(plan, attended, o_w, slots)

    inverse_two = lax.rsqrt(feature_total(hidden * hidden) / width + EPS)
    normed_two = gather_rows(plan, (hidden * inverse_two * feedforward_gain).astype(BF))
    normed_two = normed_two.reshape(tokens, width)
    units = pair_w.shape[1] // 2
    gate = matmul(normed_two, pair_w[:, :units])
    upward = matmul(normed_two, pair_w[:, units:])
    sigmoid = jax.nn.sigmoid(gate)
    active = (gate * sigmoid * upward).astype(BF)
    target = cotangent.astype(jnp.float32) * own_valid[:, :, None] * scale[:, None, None]
    grad_active = matmul(target_all, down_w.T)
    grad_gate = (grad_active * upward * sigmoid * (1.0 + gate * (1.0 - sigmoid))).astype(BF)
    grad_up = (grad_active * gate * sigmoid).astype(BF)
    grad_pair = jnp.concatenate([grad_gate, grad_up], axis=1)
    dn = scatter_rows(plan, grad_pair, pair_w.T, slots)
    down_part = reduce_groups(weight_gradient(plan, active, target_all, False))
    pair_part = reduce_groups(weight_gradient(plan, normed_two, grad_pair, True))
    weighted = dn * feedforward_gain
    total_two = feature_total(weighted * hidden)
    grad_hidden = target + inverse_two * weighted - hidden * inverse_two**3 * total_two / width
    gain_two_sum = jnp.sum(dn * hidden * inverse_two, axis=(0, 1))

    grad_hidden_all = gather_rows(plan, grad_hidden.astype(BF)).reshape(tokens, width)
    result = hidden + scatter_rows(plan, after(active, dn), down_w, slots)
    outputs = jnp.where(own_valid[:, :, None], result, 0.0).astype(BF)
    grad_attended = matmul(grad_hidden_all, o_w.T).astype(BF)
    output_part = reduce_groups(weight_gradient(plan, attended, grad_hidden_all, False))
    grad_attended = grad_attended.reshape(parts, slots, rows, wide)
    back = attention_backward(rotated, grad_attended, tables, order, slot_lengths)
    back = back.reshape(tokens, -1)
    dm = scatter_rows(plan, back, qkv_w.T, slots)
    qkv_sum = weight_gradient(plan, normed, back, True)
    qkv_part = reduce_groups(qkv_sum)
    flip = plan.side * (width // 2) if plan.fast else 0
    halves = jnp.sum(
        jnp.roll(qkv_sum.reshape(width, -1).astype(jnp.float32), flip, 0)
        * qkv_w.astype(jnp.float32),
        axis=1,
    )
    if plan.fast:
        gain_one_sum = halves[:half_width] + swap(halves[half_width:], "tensor", 1)
    else:
        gain_one_sum = lax.psum_scatter(halves, "tensor", scatter_dimension=0, tiled=True)
    gain_one_sum = gain_one_sum / attention_gain
    weighted = dm * attention_gain
    total_one = feature_total(weighted * source)
    input_grad = grad_hidden + inverse_one * weighted - source * inverse_one**3 * total_one / width

    gains = total_over(total_over(jnp.stack([gain_one_sum, gain_two_sum]), "ctx"), "dp")
    down_out = finish_rows(plan, down_part)
    gate_out, up_out = finish_columns(plan, pair_part, ((units, 1), (units, 1)))
    output_out = finish_rows(plan, output_part)
    query_out, key_out, value_out = finish_columns(
        plan, qkv_part, ((wide, 1), (narrow, share), (narrow, share))
    )
    return (
        outputs,
        input_grad.astype(BF),
        query_out,
        key_out,
        value_out,
        output_out,
        gate_out,
        up_out,
        down_out,
        gains[0],
        gains[1],
    )


def solution(mesh):
    return jax.shard_map(
        per_device,
        mesh=mesh,
        in_specs=(
            P("dp", "ctx", "tensor"),
            P("dp", "ctx", "tensor"),
            P(),
            P(),
            P("ctx", "tensor"),
            P("ctx", "tensor"),
            P("ctx", "tensor"),
            P("tensor", "ctx"),
            P("ctx", "tensor"),
            P("ctx", "tensor"),
            P("tensor", "ctx"),
            P("tensor"),
            P("tensor"),
        ),
        out_specs=(
            P("dp", "ctx", "tensor"),
            P("dp", "ctx", "tensor"),
            P(("dp", "ctx"), "tensor"),
            P(("dp", "ctx"), "tensor"),
            P(("dp", "ctx"), "tensor"),
            P("tensor", ("dp", "ctx")),
            P(("dp", "ctx"), "tensor"),
            P(("dp", "ctx"), "tensor"),
            P("tensor", ("dp", "ctx")),
            P("tensor"),
            P("tensor"),
        ),
        check_vma=False,
    )
```

time: 983 us -> 768 us (0.78)
  Pallas kernels: 0 us -> 119 us
  matrix products: 217 us -> 110 us
  waiting for transfers between devices: 366 us -> 267 us
  starting transfers between devices: 124 us -> 63 us
  blocking collectives: 30.6 us -> 0 us
  local copies, waits for them, and re-layouts: 101 us -> 71.8 us
  other arithmetic: 129 us -> 113 us
  between operations: 3.97 us -> 16.6 us
    pallas_call x0 -> x6, Pallas kernels: none -> 119 us  [the longest x2 64.8 us: attention_call(): pl.pallas_call(functools.partial(kernel, heads), grid_spec=pltpu.Prefetch...]
    ppermute x48 -> x53, waiting for transfers between devices: 180 us -> 81.8 us  [swap(): return lax.ppermute(values, axis, [(i, i ^ mask) for i in range(size)])]
    ppermute x24 -> x0, waiting for transfers between devices: 95.3 us -> none  [shift(): lax.ppermute(values, axis, [(i, (i + step) % size) for i in range(size)])]
    ppermute x20, waiting for transfers between devices: 90.9 us -> 181 us  [turn(): return lax.ppermute(values, ('ctx', 'tensor'), pairs)]
    ppermute x24 -> x0, starting transfers between devices: 64.1 us -> none  [shift(): lax.ppermute(values, axis, [(i, (i + step) % size) for i in range(size)])]
    dot_general x5 -> x0, matrix products: 46.5 us -> none  [the longest x1 17.5 us: per_device(): jnp.einsum('sphd,sqd->shpq', grad_attended, value, preferred_element_type...]
    dot_general x17 -> x13, matrix products: 151 us -> 110 us  [matmul(): return jnp.dot(left, right, preferred_element_type=jnp.float32)]
    psum x1 -> x0, blocking collectives: 30.6 us -> none  [per_device(): lax.psum((gain_one_sum, gain_two_sum), ('dp', 'ctx'))]
  transfers between devices with their start and end apart: 92 -> 79, of which waited for: 29 -> 28; matrix products, arithmetic and copies ran while one was open for 26% -> 26% of each run, Pallas kernels for 0% -> 16%
where the time goes in v2:
time: 768 us; the launch traced here: 761 us
  waiting for transfers between devices  267 us (35%)
  Pallas kernels  119 us (15%)
  other arithmetic  113 us (15%)
  matrix products  110 us (14%)
  local copies, waits for them, and re-layouts  71.8 us (9%)
  starting transfers between devices  63 us (8%)
  between operations  16.6 us (2%)
    ppermute x20, waiting for transfers between devices, turn(): return lax.ppermute(values, ('ctx', 'tensor'), pairs)  181 us
    dot_general x13, matrix products, matmul(): return jnp.dot(left, right, preferred_element_type=jnp.float32)  110 us
    ppermute x53, waiting for transfers between devices, swap(): return lax.ppermute(values, axis, [(i, i ^ mask) for i in range(size)])  81.8 us
    pallas_call x2, Pallas kernels, attention_call(): pl.pallas_call(functools.partial(kernel, heads), grid_spec=pltpu.Prefetch...  64.8 us
    pallas_call x4, Pallas kernels, weight_gradient(): pl.pallas_call(gradient_kernel, grid_spec=pltpu.PrefetchScalarGridSpec(nu...  54.2 us
    ppermute x53, starting transfers between devices, swap(): return lax.ppermute(values, axis, [(i, i ^ mask) for i in range(size)])  36.1 us
    ppermute x20, starting transfers between devices, turn(): return lax.ppermute(values, ('ctx', 'tensor'), pairs)  26.2 us
    convert_element_type x8, other arithmetic, add(): return (left.astype(jnp.float32) + right.astype(jnp.float32)).astype(BF)  22.5 us
  transfers between devices with their start and end apart: 79, of which 28 were waited for; matrix products, arithmetic and copies ran while one was open for 26% of the time, Pallas kernels for 16%

profile of v2, /device:TPU:0, one launch (start us, length us, event | category | flops | bytes accessed | tf_op | source)
XLA Modules:
  0.0 760.5 jit_solution(7322903215144119523)
XLA Ops:
  8.8 3.0 collective-permute-start
  25.0 13.1 %collective-permute-done.1 = bf16[2,256,1024]{2,1,0:T(8,128)(2,1)} collective-permute-done((bf16[2,256,1024]{2,1,0:T(8,128)(2,1)}, bf16[2,256,1024]{2,1,0:T(8,128)(2,1)}, u32[]{:S(2)}, u32[]{:S(2)}) %collective-permute-start.1) | collective-permute-done | bytes 1048608 | tf_op jit(solution)/shard_map/ppermute | solution.py:268
  41.3 3.5 collective-permute-start.6
  44.7 12.4 %collective-permute-done.2 = bf16[2,256,1024]{2,1,0:T(8,128)(2,1)S(1)} collective-permute-done((bf16[2,256,1024]{2,1,0:T(8,128)(2,1)}, bf16[2,256,1024]{2,1,0:T(8,128)(2,1)S(1)}, u32[]{:S(2)}, u32[]{:S(2)}) %collective-permute-start.2) | collective-permute-done | bytes 1048608 | tf_op jit(solution)/shard_map/ppermute | solution.py:268
  60.4 8.0 %collective-permute-done.3 = bf16[2,256,1024]{2,1,0:T(8,128)(2,1)S(1)} collective-permute-done((bf16[2,256,1024]{2,1,0:T(8,128)(2,1)}, bf16[2,256,1024]{2,1,0:T(8,128)(2,1)S(1)}, u32[]{:S(2)}, u32[]{:S(2)}) %collective-permute-start.3) | collective-permute-done | bytes 1048608 | tf_op jit(solution)/shard_map/ppermute | solution.py:268
  75.7 6.4 fusion.37.projected
  82.2 27.2 %shard_map.212 = (bf16[4,2,256,384]{3,2,1,0:T(8,128)(2,1)S(1)}, bf16[4,2,256,256]{3,2,1,0:T(8,128)(2,1)S(1)}) custom-call(s32[4]{0:T(128)S(1)} %fusion.61.order, s32[2]{0:T(128)S(1)} %dynamic_slice.181.lengths, f32[4,2,256,384]{3,2,1,0:T(8,128)} %fusion.37.projected, f32[4,1024,128]{2,1,0:T(8,128)S(1)} %pad_maximum_fusion.5.tables), custom_call_target="tpu_custom_call" | custom-call | flops 5368709120 | bytes 16777216 | tf_op jit(solution)/shard_map/pallas_call | solution.py:161
  109.6 3.3 convolution_convert_fusion.2
  127.1 4.5 collective-permute-done.37
  133.8 5.8 constant_dynamic-slice_fusion.5
  144.5 4.1 fusion.5
  152.2 14.1 %collective-permute-done.26 = bf16[128,2048]{1,0:T(8,128)(2,1)S(1)} collective-permute-done((bf16[128,2048]{1,0:T(8,128)(2,1)S(1)}, bf16[128,2048]{1,0:T(8,128)(2,1)S(1)}, u32[]{:S(2)}, u32[]{:S(2)}) %collective-permute-start.26) | collective-permute-done | bytes 524320 | tf_op jit(solution)/shard_map/ppermute | solution.py:255
  169.4 6.4 collective-permute-done.27
  185.6 24.9 %collective-permute-done.30 = bf16[2,256,1024]{2,1,0:T(8,128)(2,1)} collective-permute-done((bf16[2,256,1024]{2,1,0:T(8,128)(2,1)}, bf16[2,256,1024]{2,1,0:T(8,128)(2,1)}, u32[]{:S(2)}, u32[]{:S(2)}) %collective-permute-start.30) | collective-permute-done | bytes 1048608 | tf_op jit(solution)/shard_map/ppermute | solution.py:268
  217.2 11.8 %collective-permute-done.16 = bf16[2,256,1024]{2,1,0:T(8,128)(2,1)S(1)} collective-permute-done((bf16[2,256,1024]{2,1,0:T(8,128)(2,1)S(1)}, bf16[2,256,1024]{2,1,0:T(8,128)(2,1)S(1)}, u32[]{:S(2)}, u32[]{:S(2)}) %collective-permute-start.16) | collective-permute-done | bytes 1048608 | tf_op jit(solution)/shard_map/ppermute | solution.py:268
  236.4 5.0 fusion.1.right
  247.0 8.4 %collective-permute-done.18 = bf16[2,256,1024]{2,1,0:T(8,128)(2,1)} collective-permute-done((bf16[2,256,1024]{2,1,0:T(8,128)(2,1)S(1)}, bf16[2,256,1024]{2,1,0:T(8,128)(2,1)}, u32[]{:S(2)}, u32[]{:S(2)}) %collective-permute-start.18) | collective-permute-done | bytes 1048608 | tf_op jit(solution)/shard_map/ppermute | solution.py:268
  257.8 4.4 all-gather.5.cloned.1.call-done
  277.3 4.1 slice-done.1
  281.4 11.4 %fusion.12 = f32[2048,1024]{1,0:T(8,128)} fusion(bf16[2048,2048]{1,0:T(8,128)(2,1)S(1)} %bitcast.216, bf16[2048,2048]{1,0:T(8,128)(2,1)S(1)} %bitcast.220), kind=kOutput, calls=%fused_computation.28 | convolution fusion | flops 8589934592 | bytes 20971520 | tf_op jit(solution)/shard_map/dot_general | solution.py:218
  292.8 11.7 %fusion.14 = f32[2048,1024]{1,0:T(8,128)} fusion(bf16[2048,2048]{1,0:T(8,128)(2,1)S(1)} %bitcast.217, bf16[2048,2048]{1,0:T(8,128)(2,1)S(1)} %bitcast.220), kind=kOutput, calls=%fused_computation.30 | convolution fusion | flops 8589934592 | bytes 20971520 | tf_op jit(solution)/shard_map/dot_general | solution.py:218
  304.5 22.9 %multiply_convert_fusion = (bf16[2048,1024]{1,0:T(8,128)(2,1)}, bf16[2048,1024]{1,0:T(8,128)(2,1)}, bf16[2048,1024]{1,0:T(8,128)(2,1)}) fusion(f32[2048,1024]{1,0:T(8,128)} %fusion.14, f32[2048,1024]{1,0:T(8,128)} %fusion.12, bf16[2048,2048]{1,0:T(8,128)(2,1)} %fusion.1.right, bf16[1024,2048]{1,0:T(8,128)(2,1)} %constant_dynamic-update-slice_fusion), kind=kOutput, calls=%fused_computation.20 | convolution fusion | flops 8623489024 | bytes 41943040 | tf_op jit(solution)/shard_map/dot_general | solution.py:218
  327.4 14.5 %fusion.16 = bf16[1024,2048]{1,0:T(8,128)(2,1)} fusion(bf16[2048,2048]{1,0:T(8,128)(2,1)} %constant_dynamic-update-slice_fusion.3, bf16[2048,1024]{1,0:T(8,128)(2,1)} %get-tuple-element.35, bf16[2048,1024]{1,0:T(8,128)(2,1)} %get-tuple-element.34), kind=kOutput, calls=%fused_computation.43 | convolution fusion | flops 8600420352 | bytes 20971520 | tf_op jit(solution)/shard_map/dot_general | solution.py:218
  342.3 14.2 %shard_map.217 = bf16[4,1024,512]{2,1,0:T(8,128)(2,1)S(1)} custom-call(s32[1]{0:T(128)} %bitcast.71.side, bf16[2048,1024]{1,0:T(8,128)(2,1)} %get-tuple-element.25.left, bf16[2048,2048]{1,0:T(8,128)(2,1)} %fusion.1.right), custom_call_target="tpu_custom_call" | custom-call | flops 8589934592 | bytes 16777216 | tf_op jit(solution)/shard_map/pallas_call | solution.py:402
  358.5 13.0 %fusion.19 = bf16[1024,2048]{1,0:T(8,128)(2,1)S(1)} fusion(bf16[2048,2048]{1,0:T(8,128)(2,1)} %constant_dynamic-update-slice_fusion.3, bf16[2048,1024]{1,0:T(8,128)(2,1)} %get-tuple-element.35, bf16[2048,1024]{1,0:T(8,128)(2,1)} %get-tuple-element.34), kind=kOutput, calls=%fused_computation.44 | convolution fusion | flops 8600420352 | bytes 20971520 | tf_op jit(solution)/shard_map/dot_general | solution.py:218
  371.5 4.1 fusion.4
  377.5 24.6 %collective-permute-done.39 = bf16[2,2,256,1024]{3,2,1,0:T(8,128)(2,1)S(1)} collective-permute-done((bf16[2,2,256,1024]{3,2,1,0:T(8,128)(2,1)S(1)}, bf16[2,2,256,1024]{3,2,1,0:T(8,128)(2,1)S(1)}, u32[]{:S(2)}, u32[]{:S(2)}) %collective-permute-start.39) | collective-permute-done | bytes 2097184 | tf_op jit(solution)/shard_map/ppermute | solution.py:268
  404.3 8.3 %pad_maximum_fusion.right = bf16[2048,2048]{1,0:T(8,128)(2,1)} fusion(bf16[2048,1024]{1,0:T(8,128)(2,1)} %get-tuple-element.34, bf16[2048,1024]{1,0:T(8,128)(2,1)} %get-tuple-element.35), kind=kLoop, calls=%fused_computation.5 | loop fusion | flops 16777216 | bytes 16777216 | tf_op jit(solution)/shard_map/concatenate | solution.py:555
  412.6 5.7 collective-permute-done.40
  418.3 4.7 multiply_reduce_fusion.1
  423.0 8.3 %convolution_convert_fusion.4 = bf16[1024,2048]{1,0:T(8,128)(2,1)} fusion(bf16[1024,2048]{1,0:T(8,128)(2,1)} %constant_dynamic-update-slice_fusion, bf16[2048,1024]{1,0:T(8,128)(2,1)S(1)} %copy-done.56), kind=kOutput, calls=%fused_computation.41 | convolution fusion | flops 4297064448 | bytes 10485760 | tf_op jit(solution)/shard_map/dot_general | solution.py:218
  431.3 25.3 %shard_map.216 = bf16[4,512,2048]{2,1,0:T(8,128)(2,1)} custom-call(s32[1]{0:T(128)} %bitcast.71.side, bf16[2048,2048]{1,0:T(8,128)(2,1)} %bitcast.218, bf16[2048,2048]{1,0:T(8,128)(2,1)} %pad_maximum_fusion.right), custom_call_target="tpu_custom_call" | custom-call | flops 17179869184 | bytes 25165824 | tf_op jit(solution)/shard_map/pallas_call | solution.py:402
  456.9 7.3 convolution_convert_fusion.5
  464.3 4.1 fusion.3
  470.5 24.4 %collective-permute-done.42 = bf16[2,2,256,1024]{3,2,1,0:T(8,128)(2,1)S(1)} collective-permute-done((bf16[2,2,256,1024]{3,2,1,0:T(8,128)(2,1)S(1)}, bf16[2,2,256,1024]{3,2,1,0:T(8,128)(2,1)S(1)}, u32[]{:S(2)}, u32[]{:S(2)}) %collective-permute-start.42) | collective-permute-done | bytes 2097184 | tf_op jit(solution)/shard_map/ppermute | solution.py:268
  497.8 12.7 %collective-permute-done.44 = f32[2,256,1]{1,0,2:T(2,128)S(1)} collective-permute-done((f32[2,256,1]{1,0,2:T(2,128)S(1)}, f32[2,256,1]{1,0,2:T(2,128)S(1)}, u32[]{:S(2)}, u32[]{:S(2)}) %collective-permute-start.44) | collective-permute-done | bytes 2080 | tf_op jit(solution)/shard_map/ppermute | solution.py:255
  515.5 23.2 %collective-permute-done.45 = bf16[2,256,1024]{2,1,0:T(8,128)(2,1)S(1)} collective-permute-done((bf16[2,256,1024]{2,1,0:T(8,128)(2,1)S(1)}, bf16[2,256,1024]{2,1,0:T(8,128)(2,1)S(1)}, u32[]{:S(2)}, u32[]{:S(2)}) %collective-permute-start.45) | collective-permute-done | bytes 1048608 | tf_op jit(solution)/shard_map/ppermute | solution.py:268
  540.0 13.6 %collective-permute-done.47 = bf16[2,256,1024]{2,1,0:T(8,128)(2,1)S(1)} collective-permute-done((bf16[2,256,1024]{2,1,0:T(8,128)(2,1)S(1)}, bf16[2,256,1024]{2,1,0:T(8,128)(2,1)S(1)}, u32[]{:S(2)}, u32[]{:S(2)}) %collective-permute-start.47) | collective-permute-done | bytes 1048608 | tf_op jit(solution)/shard_map/ppermute | solution.py:268
  560.9 37.6 %shard_map.213 = bf16[4,2,256,384]{3,2,1,0:T(8,128)(2,1)S(1)} custom-call(s32[4]{0:T(128)S(1)} %copy-done.7, s32[2]{0:T(128)S(1)} %copy-done.5, bf16[4,2,256,384]{3,2,1,0:T(8,128)(2,1)S(1)} %get-tuple-element.26.rotated, bf16[4,2,256,256]{3,2,1,0:T(8,128)(2,1)S(1)} %bitcast.211, f32[4,1024,128]{2,1,0:T(8,128)} %copy-done.3), custom_call_target="tpu_custom_call" | custom-call | flops 13421772800 | bytes 16777216 | tf_op jit(solution)/shard_map/pallas_call | solution.py:161
  600.2 4.5 convolution_convert_fusion
  617.3 6.4 shard_map.215
  630.7 8.3 %shard_map.214 = bf16[4,512,384]{2,1,0:T(8,128)(2,1)} custom-call(s32[1]{0:T(128)} %bitcast.71.side, bf16[2048,2048]{1,0:T(8,128)(2,1)} %bitcast.215, bf16[2048,384]{1,0:T(8,128)(2,1)S(1)} %bitcast.210), custom_call_target="tpu_custom_call" | custom-call | flops 3221225472 | bytes 11534336 | tf_op jit(solution)/shard_map/pallas_call | solution.py:402
  652.4 18.5 %collective-permute-done.70 = f32[2,1024]{1,0:T(2,128)S(1)} collective-permute-done((f32[2,1024]{1,0:T(2,128)S(1)}, f32[2,1024]{1,0:T(2,128)S(1)}, u32[]{:S(2)}, u32[]{:S(2)}) %collective-permute-start.70) | collective-permute-done | bytes 8224 | tf_op jit(solution)/shard_map/ppermute | solution.py:255
  672.5 4.1 fusion.2
  692.8 15.7 %collective-permute-done.60 = bf16[256,128]{1,0:T(8,128)(2,1)S(1)} collective-permute-done((bf16[256,128]{1,0:T(8,128)(2,1)S(1)}, bf16[256,128]{1,0:T(8,128)(2,1)S(1)}, u32[]{:S(2)}, u32[]{:S(2)}) %collective-permute-start.60) | collective-permute-done | bytes 65568 | tf_op jit(solution)/shard_map/ppermute | solution.py:255
  723.1 10.4 %collective-permute-done.54 = bf16[2,256,1024]{2,1,0:T(8,128)(2,1)S(1)} collective-permute-done((bf16[2,256,1024]{2,1,0:T(8,128)(2,1)S(1)}, bf16[2,256,1024]{2,1,0:T(8,128)(2,1)S(1)}, u32[]{:S(2)}, u32[]{:S(2)}) %collective-permute-start.54) | collective-permute-done | bytes 1048608 | tf_op jit(solution)/shard_map/ppermute | solution.py:268
  733.5 3.2 fusion.29
  748.8 4.5 fusion.28
  (425 shorter events, 206.3 us)
Async XLA Ops:
  7.2 234.1 %all-gather.7.cloned.1.call-start = ((), (), s32[]{:S(2)}) async-start(), calls=%async_computation.9 | async-start | bytes 2621440 | tf_op jit(solution)/shard_map/all_gather | solution.py:335
  15.5 22.6 %collective-permute-start.1 = (bf16[2,256,1024]{2,1,0:T(8,128)(2,1)}, bf16[2,256,1024]{2,1,0:T(8,128)(2,1)}, u32[]{:S(2)}, u32[]{:S(2)}) collective-permute-start(bf16[2,256,1024]{2,1,0:T(8,128)(2,1)} %fusion.24), channel_id=1, source_target_pairs={{0,1},{1,0},{2,6},{3,7},{4,5},{5,4},{6,2},{7,3},{8,9},{9,8},{10,14... | collective-permute-start | bytes 3145736 | tf_op jit(solution)/shard_map/ppermute | solution.py:268
  18.2 21.7 %collective-permute-start.8 = (bf16[512,384]{1,0:T(8,128)(2,1)}, bf16[512,384]{1,0:T(8,128)(2,1)}, u32[]{:S(2)}, u32[]{:S(2)}) collective-permute-start(bf16[512,384]{1,0:T(8,128)(2,1)} %pad_maximum_fusion.15), channel_id=1, source_target_pairs={{0,2},{2,0},{4,6},{6,4},{1,3},{3,1},{5,7},{7,5},{8,10},{10,8},{12,... | collective-permute-start | bytes 1179656 | tf_op jit(solution)/shard_map/ppermute | solution.py:255
  18.3 23.0 %collective-permute-start.9 = (bf16[512,384]{1,0:T(8,128)(2,1)S(1)}, bf16[512,384]{1,0:T(8,128)(2,1)S(1)}, u32[]{:S(2)}, u32[]{:S(2)}) collective-permute-start(bf16[512,384]{1,0:T(8,128)(2,1)S(1)} %pad_maximum_fusion.16), channel_id=1, source_target_pairs={{0,4},{2,6},{4,0},{6,2},{1,5},{3,7},{5,1},{7,3},{8,12},{10,14},{12... | collective-permute-start | bytes 1179656 | tf_op jit(solution)/shard_map/ppermute | solution.py:255
  20.0 37.3 %collective-permute-start.10 = (bf16[512,384]{1,0:T(8,128)(2,1)S(1)}, bf16[512,384]{1,0:T(8,128)(2,1)}, u32[]{:S(2)}, u32[]{:S(2)}) collective-permute-start(bf16[512,384]{1,0:T(8,128)(2,1)S(1)} %pad_maximum_fusion.17), channel_id=1, source_target_pairs={{0,6},{2,4},{4,2},{6,0},{1,7},{3,5},{5,3},{7,1},{8,14},{10,12},{12... | collective-permute-start | bytes 1179656 | tf_op jit(solution)/shard_map/ppermute | solution.py:255
  20.7 36.5 %collective-permute-start.2 = (bf16[2,256,1024]{2,1,0:T(8,128)(2,1)}, bf16[2,256,1024]{2,1,0:T(8,128)(2,1)S(1)}, u32[]{:S(2)}, u32[]{:S(2)}) collective-permute-start(bf16[2,256,1024]{2,1,0:T(8,128)(2,1)} %fusion.24), channel_id=1, source_target_pairs={{0,4},{1,5},{2,3},{3,2},{4,0},{5,1},{6,7},{7,6},{8,12},{9,13},{10,... | collective-permute-start | bytes 3145736 | tf_op jit(solution)/shard_map/ppermute | solution.py:268
  38.1 30.3 %collective-permute-start.3 = (bf16[2,256,1024]{2,1,0:T(8,128)(2,1)}, bf16[2,256,1024]{2,1,0:T(8,128)(2,1)S(1)}, u32[]{:S(2)}, u32[]{:S(2)}) collective-permute-start(bf16[2,256,1024]{2,1,0:T(8,128)(2,1)} %collective-permute-done.1), channel_id=1, source_target_pairs={{0,4},{1,5},{2,3},{3,2},{4,0},{5,1},{6,7},{7,6},{8,12},{9,13},{10,... | collective-permute-start | bytes 3145736 | tf_op jit(solution)/shard_map/ppermute | solution.py:268
  39.8 30.3 %collective-permute-start.4 = (bf16[2,256,1024]{2,1,0:T(8,128)(2,1)}, bf16[2,256,1024]{2,1,0:T(8,128)(2,1)S(1)}, u32[]{:S(2)}, u32[]{:S(2)}) collective-permute-start(bf16[2,256,1024]{2,1,0:T(8,128)(2,1)} %fusion.24), channel_id=1, source_target_pairs={{0,2},{2,0},{4,6},{6,4},{1,3},{3,1},{5,7},{7,5},{8,10},{10,8},{12,... | collective-permute-start | bytes 3145736 | tf_op jit(solution)/shard_map/ppermute | solution.py:255
  41.3 28.7 %collective-permute-start.6 = (bf16[2,256,1024]{2,1,0:T(8,128)(2,1)}, bf16[2,256,1024]{2,1,0:T(8,128)(2,1)S(1)}, u32[]{:S(2)}, u32[]{:S(2)}) collective-permute-start(bf16[2,256,1024]{2,1,0:T(8,128)(2,1)} %collective-permute-done.1), channel_id=1, source_target_pairs={{0,2},{2,0},{4,6},{6,4},{1,3},{3,1},{5,7},{7,5},{8,10},{10,8},{12,... | collective-permute-start | bytes 3145736 | tf_op jit(solution)/shard_map/ppermute | solution.py:255
  73.9 35.6 %collective-permute-start.11 = (bf16[256,512]{1,0:T(8,128)(2,1)}, bf16[256,512]{1,0:T(8,128)(2,1)S(1)}, u32[]{:S(2)}, u32[]{:S(2)}) collective-permute-start(bf16[256,512]{1,0:T(8,128)(2,1)} %get-tuple-element.92), channel_id=1, source_target_pairs={{0,2},{2,0},{4,6},{6,4},{1,3},{3,1},{5,7},{7,5},{8,10},{10,8},{12,... | collective-permute-start | bytes 786440 | tf_op jit(solution)/shard_map/ppermute | solution.py:255
  74.0 35.5 %collective-permute-start.12 = (bf16[256,512]{1,0:T(8,128)(2,1)}, bf16[256,512]{1,0:T(8,128)(2,1)S(1)}, u32[]{:S(2)}, u32[]{:S(2)}) collective-permute-start(bf16[256,512]{1,0:T(8,128)(2,1)} %get-tuple-element.91), channel_id=1, source_target_pairs={{0,4},{2,6},{4,0},{6,2},{1,5},{3,7},{5,1},{7,3},{8,12},{10,14},{12... | collective-permute-start | bytes 786440 | tf_op jit(solution)/shard_map/ppermute | solution.py:255
  75.5 34.1 %collective-permute-start.13 = (bf16[256,512]{1,0:T(8,128)(2,1)}, bf16[256,512]{1,0:T(8,128)(2,1)S(1)}, u32[]{:S(2)}, u32[]{:S(2)}) collective-permute-start(bf16[256,512]{1,0:T(8,128)(2,1)} %get-tuple-element.90), channel_id=1, source_target_pairs={{0,6},{2,4},{4,2},{6,0},{1,7},{3,5},{5,3},{7,1},{8,14},{10,12},{12... | collective-permute-start | bytes 786440 | tf_op jit(solution)/shard_map/ppermute | solution.py:255
  113.0 29.1 %collective-permute-start.14 = (bf16[2,2,256,2048]{3,2,1,0:T(8,128)(2,1)}, bf16[2,2,256,2048]{3,2,1,0:T(8,128)(2,1)}, u32[]{:S(2)}, u32[]{:S(2)}) collective-permute-start(bf16[2,2,256,2048]{3,2,1,0:T(8,128)(2,1)} %bitcast.16), channel_id=1, source_target_pairs={{0,2},{2,0},{4,6},{6,4},{1,3},{3,1},{5,7},{7,5},{8,10},{10,8},{12,... | collective-permute-start | bytes 12582920 | tf_op jit(solution)/shard_map/ppermute | solution.py:255
  119.2 58.1 %collective-permute-start.29 = (bf16[2,256,1024]{2,1,0:T(8,128)(2,1)}, bf16[2,256,1024]{2,1,0:T(8,128)(2,1)}, u32[]{:S(2)}, u32[]{:S(2)}) collective-permute-start(bf16[2,256,1024]{2,1,0:T(8,128)(2,1)} %param.14), channel_id=1, source_target_pairs={{0,4},{1,5},{2,3},{3,2},{4,0},{5,1},{6,7},{7,6},{8,12},{9,13},{10,... | collective-permute-start | bytes 3145736 | tf_op jit(solution)/shard_map/ppermute | solution.py:268
  120.6 48.8 %collective-permute-start.28 = (bf16[2,256,1024]{2,1,0:T(8,128)(2,1)}, bf16[2,256,1024]{2,1,0:T(8,128)(2,1)}, u32[]{:S(2)}, u32[]{:S(2)}) collective-permute-start(bf16[2,256,1024]{2,1,0:T(8,128)(2,1)} %param.14), channel_id=1, source_target_pairs={{0,1},{1,0},{2,6},{3,7},{4,5},{5,4},{6,2},{7,3},{8,9},{9,8},{10,14... | collective-permute-start | bytes 3145736 | tf_op jit(solution)/shard_map/ppermute | solution.py:268
  127.1 51.6 %collective-permute-start.35 = (bf16[1024,512]{1,0:T(8,128)(2,1)}, bf16[1024,512]{1,0:T(8,128)(2,1)}, u32[]{:S(2)}, u32[]{:S(2)}) collective-permute-start(bf16[1024,512]{1,0:T(8,128)(2,1)} %get-tuple-element.55), channel_id=1, source_target_pairs={{0,2},{2,0},{4,6},{6,4},{1,3},{3,1},{5,7},{7,5},{8,10},{10,8},{12,... | collective-permute-start | bytes 3145736 | tf_op jit(solution)/shard_map/ppermute | solution.py:255
  133.5 128.7 %all-gather.5.cloned.1.call-start = ((), (), s32[]{:S(2)}) async-start(), calls=%async_computation.8 | async-start | bytes 5242880 | tf_op jit(solution)/shard_map/all_gather | solution.py:335
  139.7 26.6 %collective-permute-start.26 = (bf16[128,2048]{1,0:T(8,128)(2,1)S(1)}, bf16[128,2048]{1,0:T(8,128)(2,1)S(1)}, u32[]{:S(2)}, u32[]{:S(2)}) collective-permute-start(bf16[128,2048]{1,0:T(8,128)(2,1)S(1)} %fusion.48), channel_id=1, source_target_pairs={{0,4},{2,6},{4,0},{6,2},{1,5},{3,7},{5,1},{7,3},{8,12},{10,14},{12... | collective-permute-start | bytes 1572872 | tf_op jit(solution)/shard_map/ppermute | solution.py:255
  142.1 33.7 %collective-permute-start.27 = (bf16[128,2048]{1,0:T(8,128)(2,1)S(1)}, bf16[128,2048]{1,0:T(8,128)(2,1)S(1)}, u32[]{:S(2)}, u32[]{:S(2)}) collective-permute-start(bf16[128,2048]{1,0:T(8,128)(2,1)S(1)} %fusion.47), channel_id=1, source_target_pairs={{0,6},{2,4},{4,2},{6,0},{1,7},{3,5},{5,3},{7,1},{8,14},{10,12},{12... | collective-permute-start | bytes 1572872 | tf_op jit(solution)/shard_map/ppermute | solution.py:255
  166.3 45.9 %collective-permute-start.15 = (bf16[2,2,256,1024]{3,2,1,0:T(8,128)(2,1)}, bf16[2,2,256,1024]{3,2,1,0:T(8,128)(2,1)}, u32[]{:S(2)}, u32[]{:S(2)}) collective-permute-start(bf16[2,2,256,1024]{3,2,1,0:T(8,128)(2,1)} %pad_maximum_fusion.6), channel_id=1, source_target_pairs={{0,4},{1,5},{2,3},{3,2},{4,0},{5,1},{6,7},{7,6},{8,12},{9,13},{10,... | collective-permute-start | bytes 6291464 | tf_op jit(solution)/shard_map/ppermute | solution.py:268
  169.4 41.1 %collective-permute-start.33 = (bf16[2,256,1024]{2,1,0:T(8,128)(2,1)}, bf16[2,256,1024]{2,1,0:T(8,128)(2,1)}, u32[]{:S(2)}, u32[]{:S(2)}) collective-permute-start(bf16[2,256,1024]{2,1,0:T(8,128)(2,1)} %collective-permute-done.28), channel_id=1, source_target_pairs={{0,2},{2,0},{4,6},{6,4},{1,3},{3,1},{5,7},{7,5},{8,10},{10,8},{12,... | collective-permute-start | bytes 3145736 | tf_op jit(solution)/shard_map/ppermute | solution.py:255
  175.8 34.7 %collective-permute-start.30 = (bf16[2,256,1024]{2,1,0:T(8,128)(2,1)}, bf16[2,256,1024]{2,1,0:T(8,128)(2,1)}, u32[]{:S(2)}, u32[]{:S(2)}) collective-permute-start(bf16[2,256,1024]{2,1,0:T(8,128)(2,1)} %collective-permute-done.28), channel_id=1, source_target_pairs={{0,4},{1,5},{2,3},{3,2},{4,0},{5,1},{6,7},{7,6},{8,12},{9,13},{10,... | collective-permute-start | bytes 3145736 | tf_op jit(solution)/shard_map/ppermute | solution.py:268
  178.7 426.1 %reduce-scatter.11.cloned.1.call-start = ((), (), s32[]{:S(2)}) async-start(), calls=%async_computation.7 | async-start | bytes 5242880 | tf_op jit(solution)/shard_map/reduce_scatter | solution.py:424
  178.7 37.9 %collective-permute-start.25 = (bf16[512,2048]{1,0:T(8,128)(2,1)}, bf16[512,2048]{1,0:T(8,128)(2,1)S(1)}, u32[]{:S(2)}, u32[]{:S(2)}) collective-permute-start(bf16[512,2048]{1,0:T(8,128)(2,1)} %pad_maximum_fusion.7), channel_id=1, source_target_pairs={{0,2},{2,0},{4,6},{6,4},{1,3},{3,1},{5,7},{7,5},{8,10},{10,8},{12,... | collective-permute-start | bytes 6291464 | tf_op jit(solution)/shard_map/ppermute | solution.py:255
  182.9 33.6 %collective-permute-start.31 = (bf16[2,256,1024]{2,1,0:T(8,128)(2,1)S(1)}, bf16[2,256,1024]{2,1,0:T(8,128)(2,1)S(1)}, u32[]{:S(2)}, u32[]{:S(2)}) collective-permute-start(bf16[2,256,1024]{2,1,0:T(8,128)(2,1)S(1)} %copy-done.19), channel_id=1, source_target_pairs={{0,2},{2,0},{4,6},{6,4},{1,3},{3,1},{5,7},{7,5},{8,10},{10,8},{12,... | collective-permute-start | bytes 3145736 | tf_op jit(solution)/shard_map/ppermute | solution.py:255
  235.4 20.0 %collective-permute-start.18 = (bf16[2,256,1024]{2,1,0:T(8,128)(2,1)S(1)}, bf16[2,256,1024]{2,1,0:T(8,128)(2,1)}, u32[]{:S(2)}, u32[]{:S(2)}) collective-permute-start(bf16[2,256,1024]{2,1,0:T(8,128)(2,1)S(1)} %multiply_convert_fusion.3), channel_id=1, source_target_pairs={{0,1},{1,0},{2,6},{3,7},{4,5},{5,4},{6,2},{7,3},{8,9},{9,8},{10,14... | collective-permute-start | bytes 3145736 | tf_op jit(solution)/shard_map/ppermute | solution.py:268
  243.1 23.4 %collective-permute-start.19 = (bf16[2,256,1024]{2,1,0:T(8,128)(2,1)S(1)}, bf16[2,256,1024]{2,1,0:T(8,128)(2,1)}, u32[]{:S(2)}, u32[]{:S(2)}) collective-permute-start(bf16[2,256,1024]{2,1,0:T(8,128)(2,1)S(1)} %multiply_convert_fusion.3), channel_id=1, source_target_pairs={{0,4},{1,5},{2,3},{3,2},{4,0},{5,1},{6,7},{7,6},{8,12},{9,13},{10,... | collective-permute-start | bytes 3145736 | tf_op jit(solution)/shard_map/ppermute | solution.py:268
  255.4 15.5 %collective-permute-start.20 = (bf16[2,256,1024]{2,1,0:T(8,128)(2,1)}, bf16[2,256,1024]{2,1,0:T(8,128)(2,1)}, u32[]{:S(2)}, u32[]{:S(2)}) collective-permute-start(bf16[2,256,1024]{2,1,0:T(8,128)(2,1)} %collective-permute-done.18), channel_id=1, source_target_pairs={{0,4},{1,5},{2,3},{3,2},{4,0},{5,1},{6,7},{7,6},{8,12},{9,13},{10,... | collective-permute-start | bytes 3145736 | tf_op jit(solution)/shard_map/ppermute | solution.py:268
  341.9 29.6 %collective-permute-start.38 = (bf16[2,2,256,2048]{3,2,1,0:T(8,128)(2,1)}, bf16[2,2,256,2048]{3,2,1,0:T(8,128)(2,1)}, u32[]{:S(2)}, u32[]{:S(2)}) collective-permute-start(bf16[2,2,256,2048]{3,2,1,0:T(8,128)(2,1)} %bitcast.46), channel_id=1, source_target_pairs={{0,2},{2,0},{4,6},{6,4},{1,3},{3,1},{5,7},{7,5},{8,10},{10,8},{12,... | collective-permute-start | bytes 12582920 | tf_op jit(solution)/shard_map/ppermute | solution.py:255
  358.5 267.1 %reduce-scatter.9.cloned.1.call-start = ((), (), s32[]{:S(2)}) async-start(), calls=%async_computation.6 | async-start | bytes 10485760 | tf_op jit(solution)/shard_map/reduce_scatter | solution.py:424
  376.0 26.1 %collective-permute-start.39 = (bf16[2,2,256,1024]{3,2,1,0:T(8,128)(2,1)S(1)}, bf16[2,2,256,1024]{3,2,1,0:T(8,128)(2,1)S(1)}, u32[]{:S(2)}, u32[]{:S(2)}) collective-permute-start(bf16[2,2,256,1024]{3,2,1,0:T(8,128)(2,1)S(1)} %pad_maximum_fusion.8), channel_id=1, source_target_pairs={{0,4},{1,5},{2,3},{3,2},{4,0},{5,1},{6,7},{7,6},{8,12},{9,13},{10,... | collective-permute-start | bytes 6291464 | tf_op jit(solution)/shard_map/ppermute | solution.py:268
  403.4 14.9 %collective-permute-start.40 = (bf16[2,256,1024]{2,1,0:T(8,128)(2,1)S(1)}, bf16[2,256,1024]{2,1,0:T(8,128)(2,1)}, u32[]{:S(2)}, u32[]{:S(2)}) collective-permute-start(bf16[2,256,1024]{2,1,0:T(8,128)(2,1)S(1)} %fusion.42), channel_id=1, source_target_pairs={{0,1},{1,0},{2,6},{3,7},{4,5},{5,4},{6,2},{7,3},{8,9},{9,8},{10,14... | collective-permute-start | bytes 3145736 | tf_op jit(solution)/shard_map/ppermute | solution.py:268
  431.3 32.9 %collective-permute-start.41 = (bf16[2,2,256,2048]{3,2,1,0:T(8,128)(2,1)}, bf16[2,2,256,2048]{3,2,1,0:T(8,128)(2,1)}, u32[]{:S(2)}, u32[]{:S(2)}) collective-permute-start(bf16[2,2,256,2048]{3,2,1,0:T(8,128)(2,1)} %bitcast.50), channel_id=1, source_target_pairs={{0,2},{2,0},{4,6},{6,4},{1,3},{3,1},{5,7},{7,5},{8,10},{10,8},{12,... | collective-permute-start | bytes 12582920 | tf_op jit(solution)/shard_map/ppermute | solution.py:255
  456.7 230.2 %reduce-scatter.7.cloned.1.call-start = ((), (), s32[]{:S(2)}) async-start(), calls=%async_computation.5 | async-start | bytes 1310720 | tf_op jit(solution)/shard_map/reduce_scatter | solution.py:424
  468.9 26.1 %collective-permute-start.42 = (bf16[2,2,256,1024]{3,2,1,0:T(8,128)(2,1)S(1)}, bf16[2,2,256,1024]{3,2,1,0:T(8,128)(2,1)S(1)}, u32[]{:S(2)}, u32[]{:S(2)}) collective-permute-start(bf16[2,2,256,1024]{3,2,1,0:T(8,128)(2,1)S(1)} %pad_maximum_fusion.9), channel_id=1, source_target_pairs={{0,4},{1,5},{2,3},{3,2},{4,0},{5,1},{6,7},{7,6},{8,12},{9,13},{10,... | collective-permute-start | bytes 6291464 | tf_op jit(solution)/shard_map/ppermute | solution.py:268
  495.6 14.9 %collective-permute-start.43 = (bf16[2,256,1024]{2,1,0:T(8,128)(2,1)S(1)}, bf16[2,256,1024]{2,1,0:T(8,128)(2,1)S(1)}, u32[]{:S(2)}, u32[]{:S(2)}) collective-permute-start(bf16[2,256,1024]{2,1,0:T(8,128)(2,1)S(1)} %fusion.44), channel_id=1, source_target_pairs={{0,1},{1,0},{2,6},{3,7},{4,5},{5,4},{6,2},{7,3},{8,9},{9,8},{10,14... | collective-permute-start | bytes 3145736 | tf_op jit(solution)/shard_map/ppermute | solution.py:268
  512.7 26.0 %collective-permute-start.45 = (bf16[2,256,1024]{2,1,0:T(8,128)(2,1)S(1)}, bf16[2,256,1024]{2,1,0:T(8,128)(2,1)S(1)}, u32[]{:S(2)}, u32[]{:S(2)}) collective-permute-start(bf16[2,256,1024]{2,1,0:T(8,128)(2,1)S(1)} %get-tuple-element.67), channel_id=1, source_target_pairs={{0,1},{1,0},{2,6},{3,7},{4,5},{5,4},{6,2},{7,3},{8,9},{9,8},{10,14... | collective-permute-start | bytes 3145736 | tf_op jit(solution)/shard_map/ppermute | solution.py:268
  514.0 25.2 %collective-permute-start.46 = (bf16[2,256,1024]{2,1,0:T(8,128)(2,1)S(1)}, bf16[2,256,1024]{2,1,0:T(8,128)(2,1)S(1)}, u32[]{:S(2)}, u32[]{:S(2)}) collective-permute-start(bf16[2,256,1024]{2,1,0:T(8,128)(2,1)S(1)} %get-tuple-element.67), channel_id=1, source_target_pairs={{0,4},{1,5},{2,3},{3,2},{4,0},{5,1},{6,7},{7,6},{8,12},{9,13},{10,... | collective-permute-start | bytes 3145736 | tf_op jit(solution)/shard_map/ppermute | solution.py:268
  604.7 67.9 %collective-permute-start.52 = (bf16[2,2,256,2048]{3,2,1,0:T(8,128)(2,1)}, bf16[2,2,256,2048]{3,2,1,0:T(8,128)(2,1)}, u32[]{:S(2)}, u32[]{:S(2)}) collective-permute-start(bf16[2,2,256,2048]{3,2,1,0:T(8,128)(2,1)} %bitcast.65), channel_id=1, source_target_pairs={{0,2},{2,0},{4,6},{6,4},{1,3},{3,1},{5,7},{7,5},{8,10},{10,8},{12,... | collective-permute-start | bytes 12582920 | tf_op jit(solution)/shard_map/ppermute | solution.py:255
  607.7 16.1 %collective-permute-start.67 = (bf16[1024,128]{1,0:T(8,128)(2,1)S(1)}, bf16[1024,128]{1,0:T(8,128)(2,1)}, u32[]{:S(2)}, u32[]{:S(2)}) collective-permute-start(bf16[1024,128]{1,0:T(8,128)(2,1)S(1)} %get-tuple-element.85), channel_id=1, source_target_pairs={{0,6},{2,4},{4,2},{6,0},{1,7},{3,5},{5,3},{7,1},{8,14},{10,12},{12... | collective-permute-start | bytes 786440 | tf_op jit(solution)/shard_map/ppermute | solution.py:255
  623.7 86.1 %reduce-scatter.5.cloned.1.call-start = ((), (), s32[]{:S(2)}) async-start(), calls=%async_computation.4 | async-start | bytes 1966080 | tf_op jit(solution)/shard_map/reduce_scatter | solution.py:424
  628.3 19.2 %collective-permute-start.62 = (bf16[128,2048]{1,0:T(8,128)(2,1)}, bf16[128,2048]{1,0:T(8,128)(2,1)}, u32[]{:S(2)}, u32[]{:S(2)}) collective-permute-start(bf16[128,2048]{1,0:T(8,128)(2,1)} %get-tuple-element.61), channel_id=1, source_target_pairs={{0,2},{2,0},{4,6},{6,4},{1,3},{3,1},{5,7},{7,5},{8,10},{10,8},{12,... | collective-permute-start | bytes 1572872 | tf_op jit(solution)/shard_map/ppermute | solution.py:255
  645.2 35.2 %collective-permute-start.63 = (bf16[128,2048]{1,0:T(8,128)(2,1)}, bf16[128,2048]{1,0:T(8,128)(2,1)S(1)}, u32[]{:S(2)}, u32[]{:S(2)}) collective-permute-start(bf16[128,2048]{1,0:T(8,128)(2,1)} %get-tuple-element.60), channel_id=1, source_target_pairs={{0,4},{2,6},{4,0},{6,2},{1,5},{3,7},{5,1},{7,3},{8,12},{10,14},{12... | collective-permute-start | bytes 1572872 | tf_op jit(solution)/shard_map/ppermute | solution.py:255
  645.5 38.6 %collective-permute-start.64 = (bf16[128,2048]{1,0:T(8,128)(2,1)}, bf16[128,2048]{1,0:T(8,128)(2,1)S(1)}, u32[]{:S(2)}, u32[]{:S(2)}) collective-permute-start(bf16[128,2048]{1,0:T(8,128)(2,1)} %get-tuple-element.59), channel_id=1, source_target_pairs={{0,6},{2,4},{4,2},{6,0},{1,7},{3,5},{5,3},{7,1},{8,14},{10,12},{12... | collective-permute-start | bytes 1572872 | tf_op jit(solution)/shard_map/ppermute | solution.py:255
  649.6 21.2 %collective-permute-start.70 = (f32[2,1024]{1,0:T(2,128)S(1)}, f32[2,1024]{1,0:T(2,128)S(1)}, u32[]{:S(2)}, u32[]{:S(2)}) collective-permute-start(f32[2,1024]{1,0:T(2,128)S(1)} %fusion.66), channel_id=1, source_target_pairs={{0,4},{2,6},{4,0},{6,2},{1,5},{3,7},{5,1},{7,3},{8,12},{10,14},{12... | collective-permute-start | bytes 24584 | tf_op jit(solution)/shard_map/ppermute | solution.py:255
  680.1 35.5 %collective-permute-start.53 = (bf16[2,2,256,1024]{3,2,1,0:T(8,128)(2,1)}, bf16[2,2,256,1024]{3,2,1,0:T(8,128)(2,1)S(1)}, u32[]{:S(2)}, u32[]{:S(2)}) collective-permute-start(bf16[2,2,256,1024]{3,2,1,0:T(8,128)(2,1)} %pad_maximum_fusion.10), channel_id=1, source_target_pairs={{0,4},{1,5},{2,3},{3,2},{4,0},{5,1},{6,7},{7,6},{8,12},{9,13},{10,... | collective-permute-start | bytes 6291464 | tf_op jit(solution)/shard_map/ppermute | solution.py:268
  687.9 20.6 %collective-permute-start.60 = (bf16[256,128]{1,0:T(8,128)(2,1)S(1)}, bf16[256,128]{1,0:T(8,128)(2,1)S(1)}, u32[]{:S(2)}, u32[]{:S(2)}) collective-permute-start(bf16[256,128]{1,0:T(8,128)(2,1)S(1)} %get-tuple-element.113), channel_id=1, source_target_pairs={{0,4},{2,6},{4,0},{6,2},{1,5},{3,7},{5,1},{7,3},{8,12},{10,14},{12... | collective-permute-start | bytes 196616 | tf_op jit(solution)/shard_map/ppermute | solution.py:255
  689.6 19.5 %collective-permute-start.61 = (bf16[256,128]{1,0:T(8,128)(2,1)S(1)}, bf16[256,128]{1,0:T(8,128)(2,1)S(1)}, u32[]{:S(2)}, u32[]{:S(2)}) collective-permute-start(bf16[256,128]{1,0:T(8,128)(2,1)S(1)} %get-tuple-element.112), channel_id=1, source_target_pairs={{0,6},{2,4},{4,2},{6,0},{1,7},{3,5},{5,3},{7,1},{8,14},{10,12},{12... | collective-permute-start | bytes 196616 | tf_op jit(solution)/shard_map/ppermute | solution.py:255
  (90 other events, 1070.8 us)
Sparse Core Ops, SparseCore 0:
  133.6 47.4 all-gather.6
  182.7 79.4 all-gather.4
  358.6 77.3 reduce-scatter.10
  456.8 145.2 reduce-scatter.8
  623.9 27.1 reduce-scatter.6
  653.2 34.2 reduce-scatter.4

commit v3 on v2

v3 whole, which is shorter than its diff:
```python
import functools

import jax
import jax.numpy as jnp
from jax import lax
from jax.experimental import pallas as pl
from jax.experimental.pallas import tpu as pltpu
from jax.sharding import PartitionSpec as P

HD = 64
EPS = 1e-05
NEGATIVE = -1e30
BF = jnp.bfloat16


def inverse_frequency(head_size):
    exponent = jnp.arange(0, head_size, 2, dtype=jnp.int32).astype(jnp.float32) / head_size
    plain = 1.0 / jnp.power(jnp.float32(500000.0), exponent)
    factor = 32.0
    old_context = 8192.0
    wavelength = 2.0 * jnp.pi / plain
    smooth = (old_context / wavelength - 1.0) / (4.0 - 1.0)
    scaled = jnp.where(wavelength > old_context, plain / factor, plain)
    middle = (wavelength <= old_context) & (wavelength >= old_context / 4.0)
    scaled = jnp.where(middle, (1.0 - smooth) * plain / factor + smooth * plain, scaled)
    return scaled


def rotation_tables(span):
    positions = jnp.arange(span, dtype=jnp.int32).astype(jnp.float32)
    angle = positions[:, None] * inverse_frequency(HD)[None, :]
    cosine = jnp.cos(angle)
    sine = jnp.sin(angle)
    one = jnp.ones((span, HD), jnp.float32)
    turning = jnp.concatenate([cosine, cosine], axis=1)
    crossing = jnp.concatenate([-sine, sine], axis=1)
    return jnp.stack(
        [
            jnp.concatenate([turning, turning], axis=1),
            jnp.concatenate([crossing, crossing], axis=1),
            jnp.concatenate([turning, one], axis=1),
            jnp.concatenate([crossing, 0.0 * one], axis=1),
        ]
    )


def rotate_lanes(values, tables, rows, sign):
    chunks = values.shape[1] // 128
    lanes = lax.broadcasted_iota(jnp.int32, (values.shape[0], 128), 1)
    first = lanes % HD < HD // 2
    turned = []
    for chunk in range(chunks):
        part = values[:, chunk * 128 : chunk * 128 + 128]
        other = jnp.where(
            first, pltpu.roll(part, 128 - HD // 2, 1), pltpu.roll(part, HD // 2, 1)
        )
        table = 2 if chunk == chunks - 1 else 0
        turned.append(part * tables[table, rows] + sign * other * tables[table + 1, rows])
    return jnp.concatenate(turned, axis=1)


def take_block(here, away, index):
    half = here.shape[1]
    return jnp.where(index < half, here[0, index % half], away[0, index % half])


def put_block(here, away, index, values):
    half = here.shape[1]

    @pl.when(index < half)
    def _():
        here[0, index % half] = values

    @pl.when(index >= half)
    def _():
        away[0, index % half] = values


def split_heads(ref, values, rows, heads):
    for head in range(heads):
        ref[head, rows] = values[:, head * HD : head * HD + HD]


def masked_scores(query, keys, limit):
    scores = lax.dot_general(
        query, keys, (((1,), (1,)), ((), ())), preferred_element_type=jnp.float32
    )
    columns = lax.broadcasted_iota(jnp.int32, scores.shape, 1)
    return jnp.where(columns < limit, scores, NEGATIVE)


def row_limit(start, rows, length):
    positions = start + lax.broadcasted_iota(jnp.int32, (rows, 1), 0)
    return jnp.minimum(positions + 1, length)


def forward_kernel(
    heads,
    order,
    lengths,
    projected_here,
    projected_away,
    tables,
    rotated_here,
    rotated_away,
    attended_here,
    attended_away,
    stats,
    qs,
    ks,
    vs,
):
    _, half, rows, _ = projected_here.shape
    blocks = 2 * half
    wide = heads * HD
    length = lengths[pl.program_id(0)]
    lanes = lax.broadcasted_iota(jnp.int32, (rows, 128), 1)
    for block in range(blocks):
        where = pl.ds(block * rows, rows)
        values = take_block(projected_here, projected_away, order[block])
        turned = rotate_lanes(values, tables, where, 1.0).astype(BF)
        put_block(rotated_here, rotated_away, order[block], turned)
        split_heads(qs, turned[:, :wide] * BF(HD ** (-0.5)), where, heads)
        ks[where] = turned[:, wide : wide + HD]
        vs[where] = turned[:, wide + HD :]
    for block in range(blocks):
        where = pl.ds(block * rows, rows)
        extent = (block + 1) * rows
        limit = row_limit(block * rows, rows, length)
        outs = []
        logs = jnp.zeros((rows, 128), jnp.float32)
        for head in range(heads):
            scores = masked_scores(qs[head, where], ks[:extent], limit)
            top = jnp.max(scores, axis=1, keepdims=True)
            powers = jnp.exp(scores - top)
            total = jnp.sum(powers, axis=1, keepdims=True)
            outs.append((matmul(powers.astype(BF), vs[:extent]) * (1.0 / total)).astype(BF))
            logs = jnp.where(lanes == head, top + jnp.log(total), logs)
        stats[0, where] = logs
        put_block(attended_here, attended_away, order[block], jnp.concatenate(outs, axis=1))


def backward_kernel(
    heads,
    order,
    lengths,
    rotated_here,
    rotated_away,
    grads_here,
    grads_away,
    tables,
    stats,
    back_here,
    back_away,
    qs,
    ks,
    vs,
    gs,
    dqs,
    dks,
    dvs,
):
    _, half, rows, _ = rotated_here.shape
    blocks = 2 * half
    wide = heads * HD
    length = lengths[pl.program_id(0)]
    scale = HD ** (-0.5)
    down = (((0,), (0,)), ((), ()))
    for block in range(blocks):
        where = pl.ds(block * rows, rows)
        turned = take_block(rotated_here, rotated_away, order[block])
        split_heads(qs, turned[:, :wide] * BF(scale), where, heads)
        ks[where] = turned[:, wide : wide + HD]
        vs[where] = turned[:, wide + HD :]
        split_heads(gs, take_block(grads_here, grads_away, order[block]), where, heads)
    dks[...] = jnp.zeros_like(dks)
    dvs[...] = jnp.zeros_like(dvs)
    for block in range(blocks):
        where = pl.ds(block * rows, rows)
        extent = (block + 1) * rows
        limit = row_limit(block * rows, rows, length)
        for head in range(heads):
            query = qs[head, where]
            grad = gs[head, where]
            keys = ks[:extent]
            scores = masked_scores(query, keys, limit)
            probs = jnp.exp(scores - stats[0, where][:, head : head + 1])
            grad_probs = lax.dot_general(
                grad, vs[:extent], (((1,), (1,)), ((), ())), preferred_element_type=jnp.float32
            )
            delta = jnp.sum(probs * grad_probs, axis=1, keepdims=True)
            grad_scores = (probs * (grad_probs - delta)).astype(BF)
            dqs[head, where] = matmul(grad_scores, keys) * scale
            dks[:extent] += lax.dot_general(
                grad_scores, query, down, preferred_element_type=jnp.float32
            )
            dvs[:extent] += lax.dot_general(
                probs.astype(BF), grad, down, preferred_element_type=jnp.float32
            )
    for block in range(blocks):
        where = pl.ds(block * rows, rows)
        parts = [dqs[h, where] for h in range(heads)] + [dks[where], dvs[where]]
        turned = rotate_lanes(jnp.concatenate(parts, axis=1), tables, where, -1.0)
        put_block(back_here, back_away, order[block], turned.astype(BF))


def slot_spec(shape):
    rest = tuple(shape[1:])
    return pl.BlockSpec((1, *rest), lambda slot, *_: (slot,) + (0,) * len(rest))


def attention_call(kernel, heads, order, lengths, tables, arrays, extra, outs, scratch, work):
    slots, half, rows, _ = arrays[0].shape
    span = 2 * half * rows
    return pl.pallas_call(
        functools.partial(kernel, heads),
        grid_spec=pltpu.PrefetchScalarGridSpec(
            num_scalar_prefetch=2,
            grid=(slots,),
            in_specs=[slot_spec(item.shape) for item in arrays]
            + [pl.BlockSpec(tables.shape, lambda slot, *_: (0, 0, 0))]
            + [slot_spec(item.shape) for item in extra],
            out_specs=[slot_spec(item.shape) for item in outs],
            scratch_shapes=scratch,
        ),
        out_shape=outs,
        compiler_params=pltpu.CompilerParams(vmem_limit_bytes=48 * 2**20),
        cost_estimate=pl.CostEstimate(
            flops=work * slots * heads * span * span * HD * 5 // 2,
            bytes_accessed=16 * 2**20,
            transcendentals=slots * heads * span * span,
        ),
    )(order, lengths, *arrays, tables, *extra)


def attention_forward(projected, tables, order, lengths):
    slots, half, rows, columns = projected[0].shape
    heads = columns // HD - 2
    span = 2 * half * rows
    rotated = jax.ShapeDtypeStruct(projected[0].shape, BF)
    attended = jax.ShapeDtypeStruct((slots, half, rows, heads * HD), BF)
    stats = jax.ShapeDtypeStruct((slots, span, 128), jnp.float32)
    scratch = [
        pltpu.VMEM((heads, span, HD), BF),
        pltpu.VMEM((span, HD), BF),
        pltpu.VMEM((span, HD), BF),
    ]
    outs = [rotated, rotated, attended, attended, stats]
    found = attention_call(
        forward_kernel, heads, order, lengths, tables, projected, [], outs, scratch, 4
    )
    return tuple(found[:2]), tuple(found[2:4]), found[4]


def attention_backward(rotated, grads, stats, tables, order, lengths):
    slots, half, rows, columns = rotated[0].shape
    heads = columns // HD - 2
    span = 2 * half * rows
    scratch = [
        pltpu.VMEM((heads, span, HD), BF),
        pltpu.VMEM((span, HD), BF),
        pltpu.VMEM((span, HD), BF),
        pltpu.VMEM((heads, span, HD), BF),
        pltpu.VMEM((heads, span, HD), jnp.float32),
        pltpu.VMEM((span, HD), jnp.float32),
        pltpu.VMEM((span, HD), jnp.float32),
    ]
    outs = [jax.ShapeDtypeStruct(rotated[0].shape, BF)] * 2
    arrays = [*rotated, *grads]
    return attention_call(
        backward_kernel, heads, order, lengths, tables, arrays, [stats], outs, scratch, 10
    )


def matmul(left, right):
    return jnp.dot(left, right, preferred_element_type=jnp.float32)


class Plan:
    def __init__(self, slots):
        self.place = lax.axis_index("ctx")
        self.side = lax.axis_index("tensor")
        self.group = lax.axis_index("dp")
        self.parts = lax.axis_size("ctx")
        self.sides = lax.axis_size("tensor")
        self.groups = lax.axis_size("dp")
        self.fast = self.parts == 4 and self.sides == 2 and self.groups == 4 and slots == 2

    def storage(self):
        members = jnp.arange(self.parts, dtype=jnp.int32)
        if not self.fast:
            return members
        apart = self.place ^ members
        return (apart % 2) * 2 + apart // 2

    def members(self, away):
        half = self.parts // 2
        if not self.fast:
            return jnp.arange(half, dtype=jnp.int32) + away * half
        return self.place ^ (2 * jnp.arange(half, dtype=jnp.int32) + away)

    def ordered(self, block, count):
        return block ^ (self.side * (count // 2)) if self.fast else block


def after(values, anchor):
    return lax.optimization_barrier((values, anchor))[0]


def swap(values, axis, mask):
    size = lax.axis_size(axis)
    return lax.ppermute(values, axis, [(i, i ^ mask) for i in range(size)])


def gather_open(plan, values):
    if not plan.fast:
        wide = lax.all_gather(values, "tensor", axis=2, tiled=True)
        return (lax.all_gather(wide, "ctx", axis=0),)
    zero, one = values[0], values[1]
    zero_side = swap(zero, "tensor", 1)
    one_ctx = swap(one, "ctx", 2)
    zero_ctx = swap(zero, "ctx", 2)
    one_side = swap(one, "tensor", 1)
    zero_far = swap(zero_side, "ctx", 2)
    one_far = swap(one_ctx, "tensor", 1)
    return zero, zero_side, zero_ctx, zero_far, one, one_side, one_ctx, one_far


def gather_close(plan, opened, finish=None):
    if finish is None:
        finish = [lambda half: half] * 2
    if not plan.fast:
        half = plan.parts // 2
        whole = opened[0].swapaxes(0, 1)
        return finish[0](whole[:, :half]), finish[1](whole[:, half:])
    opened = lax.optimization_barrier(opened)
    zero, zero_side, zero_ctx, zero_far, one, one_side, one_ctx, one_far = opened
    rows = [
        jnp.concatenate(pair, axis=1)
        for pair in ((zero, zero_side), (zero_ctx, zero_far), (one, one_side), (one_ctx, one_far))
    ]
    here = finish[0](jnp.stack(rows).reshape(2, 2, *rows[0].shape))
    return here, swap(here, "ctx", 1)


def flat(halves):
    return tuple(half.reshape(-1, half.shape[-1]) for half in halves)


def gather_rows(plan, values):
    return flat(gather_close(plan, gather_open(plan, values)))


def wide_sum(*terms):
    return sum(term.astype(jnp.float32) for term in terms)


def scatter_open(plan, lefts, right, slots):
    away = matmul(lefts[1], right).astype(BF)
    here = matmul(lefts[0], right).astype(BF)
    return scatter_halves(plan, here, away, slots)


def scatter_halves(plan, here, away, slots):
    width = here.shape[-1]
    half = plan.parts // 2
    here = here.reshape(slots, half, -1, width)
    away = away.reshape(slots, half, -1, width)
    if not plan.fast:
        return (jnp.concatenate([here, away], axis=1),)
    got = swap(away, "ctx", 1)
    own = width // 2
    zero_sent = wide_sum(here[0, 1], got[0, 1]).astype(BF)
    one_sent = wide_sum(here[1, :, :, own:], got[1, :, :, own:]).astype(BF)
    return here, got, zero_sent, one_sent


def scatter_turn(plan, opened):
    if not plan.fast:
        return opened
    here, got, zero_sent, one_sent = opened
    return here, got, swap(zero_sent, "ctx", 2), swap(one_sent, "tensor", 1)


def scatter_end(plan, turned):
    if not plan.fast:
        whole = turned[0].swapaxes(0, 1)
        narrow = lax.psum_scatter(whole, "tensor", scatter_dimension=3, tiled=True)
        return lax.psum_scatter(narrow, "ctx", scatter_dimension=0, tiled=False).astype(jnp.float32)
    here, got, zero, one = turned
    own = here.shape[-1] // 2
    zero_sent = wide_sum(here[0, 0, :, own:], got[0, 0, :, own:], zero[:, own:]).astype(BF)
    one_sent = wide_sum(here[1, 1, :, :own], got[1, 1, :, :own], one[1]).astype(BF)
    zero_sent, one_sent = lax.optimization_barrier((zero_sent, one_sent))
    zero_last, one_last = lax.optimization_barrier(
        (swap(zero_sent, "tensor", 1), swap(one_sent, "ctx", 2))
    )
    zero_total = wide_sum(here[0, 0, :, :own], got[0, 0, :, :own], zero[:, :own], zero_last)
    one_total = wide_sum(here[1, 0, :, :own], got[1, 0, :, :own], one[0], one_last)
    return jnp.stack([zero_total, one_total])


def scatter_close(plan, opened, beside=None):
    turned = scatter_turn(plan, opened)
    if beside is not None:
        turned = after(turned, beside)
    return scatter_end(plan, turned)


def exchange_pieces(plan, piece):
    found = [piece(plan.place)]
    for mask in range(1, plan.parts):
        found.append(swap(piece(plan.place ^ mask), "ctx", mask))
    return found


def shared_pieces(plan, columns, rows):
    if not plan.fast:
        return exchange_pieces(plan, columns), exchange_pieces(plan, rows)
    count = plan.groups
    narrow = rows(plan.place).shape[1]

    def quarter(piece):
        size = piece.shape[0] // count
        return lax.dynamic_slice_in_dim(piece, plan.group * size, size, 0)

    got = []
    for mask in (2, 3):
        wide = quarter(columns(plan.place ^ mask))
        strips = [wide[:, i : i + narrow] for i in range(0, wide.shape[1], narrow)]
        strips.append(quarter(rows(plan.place ^ mask)))
        got.append(swap(jnp.concatenate(strips), "ctx", mask))
    return jnp.stack(got)


def core_pieces(plan, piece):
    return [piece(plan.place), swap(piece(plan.place ^ 1), "ctx", 1)]


def split_shared(plan, whole, columns, rows):
    if not plan.fast:
        return whole
    whole = lax.all_gather(whole, "dp")
    count = plan.groups
    high = columns[0].shape[0] // count
    strips = columns[0].shape[1] // rows[0].shape[1]
    for index in range(2):
        part = whole[:, index]
        wide = [part[:, i * high : (i + 1) * high].reshape(high * count, -1) for i in range(strips)]
        columns = columns + [jnp.concatenate(wide, axis=1)]
        rows = rows + [part[:, strips * high :].reshape(rows[0].shape)]
    return columns, rows


def place_rows(plan, found):
    rows, columns = found[0].shape
    whole = jnp.zeros((rows * plan.parts, columns), found[0].dtype)
    for mask, piece in enumerate(found):
        start = plan.ordered(plan.place ^ mask, plan.parts) * rows
        whole = lax.dynamic_update_slice(whole, piece, (start, 0))
    return whole


def place_columns(plan, found):
    rows, columns = found[0].shape
    whole = jnp.zeros((rows, columns * plan.parts), found[0].dtype)
    for mask, piece in enumerate(found):
        start = plan.ordered(plan.place ^ mask, plan.parts) * columns
        whole = lax.dynamic_update_slice(whole, piece, (0, start))
    return whole


def by_member(plan, found):
    bit = 1
    while bit < plan.parts:
        flip = (plan.place & bit) != 0
        found = [jnp.where(flip, found[i ^ bit], found[i]) for i in range(plan.parts)]
        bit *= 2
    return found


def column_piece(weights, parts, least=1):
    def piece(member):
        taken = []
        for weight in weights:
            share = max(1, least * parts // weight.shape[1])
            size = weight.shape[1] * share // parts
            taken.append(lax.dynamic_slice_in_dim(weight, member // share * size, size, 1))
        return jnp.concatenate(taken, axis=1)

    return piece


def row_piece(weight, parts):
    size = weight.shape[0] // parts

    def piece(member):
        return lax.dynamic_slice_in_dim(weight, member * size, size, 0)

    return piece


def forward_units_kernel(normed, weights, active, slope_gate, slope_up):
    units = weights.shape[1] // 2
    gate = matmul(normed[...], weights[:, :units])
    upward = matmul(normed[...], weights[:, units:])
    sigmoid = jax.nn.sigmoid(gate)
    swish = gate * sigmoid
    active[...] = (swish * upward).astype(BF)
    slope_gate[...] = (upward * sigmoid * (1.0 + gate * (1.0 - sigmoid))).astype(BF)
    slope_up[...] = swish.astype(BF)


def backward_units_kernel(target, slope_gate, slope_up, down, weights, grads, back):
    units = down.shape[0]
    across = (((1,), (1,)), ((), ()))
    grad = lax.dot_general(target[...], down[...], across, preferred_element_type=jnp.float32)
    grads[:, :units] = (grad * slope_gate[...]).astype(BF)
    grads[:, units:] = (grad * slope_up[...]).astype(BF)
    total = lax.dot_general(grads[...], weights[...], across, preferred_element_type=jnp.float32)
    back[...] = total.astype(BF)


def row_blocks(kernel, blocked, whole, widths):
    lines = blocked[0].shape[0]
    rows = min(512, lines)
    flops = sum(2 * lines * item.shape[0] * item.shape[1] for item in whole)
    moved = sum(2 * lines * item.shape[1] for item in blocked) + sum(2 * lines * w for w in widths)
    return pl.pallas_call(
        kernel,
        grid=(lines // rows,),
        in_specs=[pl.BlockSpec((rows, item.shape[1]), lambda i: (i, 0)) for item in blocked]
        + [pl.BlockSpec(item.shape, lambda i: (0, 0)) for item in whole],
        out_specs=[pl.BlockSpec((rows, width), lambda i: (i, 0)) for width in widths],
        out_shape=[jax.ShapeDtypeStruct((lines, width), BF) for width in widths],
        compiler_params=pltpu.CompilerParams(vmem_limit_bytes=56 * 2**20),
        cost_estimate=pl.CostEstimate(
            flops=flops,
            bytes_accessed=moved + sum(2 * item.size for item in whole),
            transcendentals=0,
        ),
    )(*blocked, *whole)


def forward_units(normed, weights):
    return row_blocks(forward_units_kernel, [normed], [weights], [weights.shape[1] // 2] * 3)


def backward_units(target, slopes, down, weights):
    return row_blocks(
        backward_units_kernel,
        [target, *slopes],
        [down, weights],
        [weights.shape[1], weights.shape[0]],
    )


def gradient_kernel(side, left_here, left_away, right_here, right_away, out):
    total = None
    for left, right in ((left_here, right_here), (left_away, right_away)):
        term = lax.dot_general(
            left[...], right[...], (((0,), (0,)), ((), ())), preferred_element_type=jnp.float32
        )
        total = term if total is None else total + term
    out[...] = total.astype(out.dtype).reshape(out.shape)


def weight_gradient(plan, lefts, rights, features_first, part=0, parts=1):
    tokens, height = lefts[0].shape
    width = rights[0].shape[1] // parts
    groups = plan.groups
    flip = groups // 2 if plan.fast else 0
    tall = height // groups if features_first else height
    broad = width if features_first else width // groups
    step = min(broad, 1024)
    lines = min(tall, 512)
    skip = part * (width // step)

    def at(i, j, side):
        group, line = (i // (tall // lines), i % (tall // lines)) if features_first else (j, i)
        column = j if features_first else 0
        return (group + flip * side[0]) % groups, line, column

    return pl.pallas_call(
        gradient_kernel,
        grid_spec=pltpu.PrefetchScalarGridSpec(
            num_scalar_prefetch=1,
            grid=(height // lines, width // step),
            in_specs=[pl.BlockSpec((tokens, lines), lambda i, j, side: (0, i))] * 2
            + [pl.BlockSpec((tokens, step), lambda i, j, side: (0, j + skip))] * 2,
            out_specs=pl.BlockSpec((1, lines, step), at),
        ),
        out_shape=jax.ShapeDtypeStruct((groups, tall, broad), BF),
        compiler_params=pltpu.CompilerParams(vmem_limit_bytes=48 * 2**20),
        cost_estimate=pl.CostEstimate(
            flops=4 * tokens * height * width,
            bytes_accessed=2 * (2 * tokens * (height + width) + height * width),
            transcendentals=0,
        ),
    )(plan.side[None].astype(jnp.int32), *lefts, *rights)


def reduce_groups(grad):
    return lax.psum_scatter(grad, "dp", scatter_dimension=0)


def finish_columns(plan, found, widths):
    found = by_member(plan, found)
    outs = []
    start = 0
    for width, share in widths:
        blocks = [piece[:, start : start + width].astype(jnp.float32) for piece in found]
        blocks = [sum(blocks[i : i + share]) for i in range(0, plan.parts, share)]
        outs.append(jnp.concatenate(blocks, axis=1))
        start += width
    return outs


def finish_rows(plan, found):
    return jnp.concatenate(by_member(plan, found), axis=0).astype(jnp.float32)


def send_rows(plan, part):
    return exchange_pieces(plan, row_piece(part, plan.parts))


def send_columns(plan, part):
    return exchange_pieces(plan, column_piece([part], plan.parts))


def total_over(values, axis):
    others = [swap(values, axis, mask) for mask in range(1, lax.axis_size(axis))]
    return sum(lax.optimization_barrier(others), values)


def feature_total(values):
    total = jnp.sum(values, axis=-1, keepdims=True)
    if lax.axis_size("tensor") == 2:
        return total + swap(total, "tensor", 1)
    return lax.psum(total, "tensor")


def per_device(
    inputs,
    cotangent,
    lengths,
    deal_order,
    query_weight,
    key_weight,
    value_weight,
    output_weight,
    gate_weight,
    up_weight,
    down_weight,
    attention_gain,
    feedforward_gain,
):
    slots, rows, half_width = inputs.shape
    plan = Plan(slots)
    width = half_width * plan.sides
    parts = plan.parts
    groups = plan.groups
    sequences = lengths.shape[0]
    ids = jnp.arange(sequences, dtype=jnp.int32)
    own_ids = plan.group * slots + jnp.arange(slots, dtype=jnp.int32)
    slot_lengths = lax.dynamic_slice_in_dim(lengths, plan.group * slots, slots)
    dealt = jnp.sum(jnp.where(deal_order[:, None] == ids[None, :], lengths[None, :], 0), axis=1)
    totals = jnp.sum(dealt.reshape(groups, -1), axis=1)
    found = jnp.where(deal_order[None, :] == own_ids[:, None], ids[None, :], 0)
    owner = jnp.sum(found, axis=1) // (sequences // groups)
    mine = owner[:, None] == jnp.arange(groups, dtype=jnp.int32)[None, :]
    own_totals = jnp.sum(jnp.where(mine, totals[None, :], 0), axis=1)
    scale = jnp.sum(lengths).astype(jnp.float32) / groups / own_totals.astype(jnp.float32)

    own_rows = plan.place * rows + jnp.arange(rows, dtype=jnp.int32)
    own_valid = own_rows[None, :] < slot_lengths[:, None]
    tables = rotation_tables(parts * rows)
    order = plan.storage()

    def scaled(away):
        starts = plan.members(away) * rows
        positions = starts[:, None] + jnp.arange(rows, dtype=jnp.int32)[None, :]
        valid = positions[None] < slot_lengths[:, None, None]
        factor = jnp.where(valid, scale[:, None, None], 0.0)
        return lambda half: (half.astype(jnp.float32) * factor[..., None]).astype(BF)

    source = inputs.astype(jnp.float32)
    inverse_one = lax.rsqrt(feature_total(source * source) / width + EPS)
    columns = column_piece([gate_weight, up_weight], parts)
    rows_piece = row_piece(down_weight, parts)
    shared = shared_pieces(plan, columns, rows_piece)
    opened = gather_open(plan, (source * inverse_one * attention_gain).astype(BF))
    qkv_w = place_rows(
        plan,
        exchange_pieces(plan, column_piece([query_weight, key_weight, value_weight], parts, HD)),
    )
    opened, shared = after((opened, shared), (tables, qkv_w))
    normed = gather_close(plan, opened)
    late = after((output_weight, gate_weight, up_weight, down_weight), normed[0])
    o_found = exchange_pieces(plan, row_piece(late[0], parts))
    normed = flat(normed)

    wide = query_weight.shape[1] // parts
    share = max(1, HD * parts // key_weight.shape[1])
    narrow = key_weight.shape[1] * share // parts
    half_shape = (slots, parts // 2, rows, -1)
    projected = [matmul(item, qkv_w).reshape(half_shape) for item in normed]
    rotated, attended, stats = attention_forward(projected, tables, order, slot_lengths)
    attended = flat(attended)
    attended, o_found = after((attended, o_found), rotated)
    o_w = place_columns(plan, o_found)
    opened = scatter_open(plan, attended, o_w, slots)
    hidden = source + scatter_close(plan, opened)
    if plan.fast:
        pair_core = core_pieces(plan, column_piece([late[1], late[2]], parts))
        down_core = core_pieces(plan, row_piece(late[3], parts))
    else:
        pair_core = down_core = None

    inverse_two = lax.rsqrt(feature_total(hidden * hidden) / width + EPS)
    opened = gather_open(plan, (hidden * inverse_two * feedforward_gain).astype(BF))
    pair_found, down_found = split_shared(plan, shared, pair_core, down_core)
    pair_w = place_rows(plan, pair_found)
    normed_two = flat(gather_close(plan, after(opened, pair_w)))
    target_open = gather_open(plan, after(cotangent, normed_two[0]))
    units = pair_w.shape[1] // 2
    active_here, *slopes_here = forward_units(normed_two[0], pair_w)
    normed_two = (normed_two[0], after(normed_two[1], active_here))
    active_away, *slopes_away = forward_units(normed_two[1], pair_w)
    active = (active_here, active_away)
    active, target_open = after((active, target_open), active_away)
    down_w = place_columns(plan, down_found)
    target_all = flat(gather_close(plan, target_open, [scaled(0), scaled(1)]))
    down_sum = weight_gradient(plan, active, target_all, False)
    down_part = reduce_groups(down_sum)

    target = cotangent.astype(jnp.float32) * own_valid[:, :, None] * scale[:, None, None]
    target_away = after(target_all[1], down_sum)
    grads_away, away = backward_units(target_away, slopes_away, down_w, pair_w)
    target_here = after(target_all[0], away)
    grads_here, here = backward_units(target_here, slopes_here, down_w, pair_w)
    grad_pair = (grads_here, grads_away)
    opened = scatter_halves(plan, here, away, slots)
    grad_late = after(grad_pair, opened[-1])
    gate_sum = weight_gradient(plan, normed_two, grad_late, True, 0, 2)
    up_sum = weight_gradient(plan, normed_two, grad_late, True, 1, 2)
    gate_part = reduce_groups(gate_sum)
    up_part = reduce_groups(up_sum)
    dn = scatter_close(plan, opened, (gate_sum, up_sum, down_part))
    weighted = dn * feedforward_gain
    total_two = feature_total(weighted * hidden)
    grad_hidden = target + inverse_two * weighted - hidden * inverse_two**3 * total_two / width
    gain_two_sum = jnp.sum(dn * hidden * inverse_two, axis=(0, 1))

    result_open = scatter_open(plan, after(active, grad_hidden), down_w, slots)
    opened = after(gather_open(plan, grad_hidden.astype(BF)), (result_open, gate_part))
    grad_hidden_all = flat(gather_close(plan, opened))
    result_open, down_part, gate_part = after((result_open, down_part, gate_part), grad_hidden_all)
    result_turned = scatter_turn(plan, result_open)
    down_sent = send_columns(plan, down_part)
    gate_sent = send_rows(plan, gate_part)
    grad_attended = [matmul(item, o_w.T).astype(BF) for item in grad_hidden_all]
    output_sum = weight_gradient(plan, attended, grad_hidden_all, False)
    grad_attended = after(grad_attended, output_sum)
    grad_attended = [item.reshape(half_shape) for item in grad_attended]
    back = attention_backward(rotated, grad_attended, stats, tables, order, slot_lengths)
    sent = (result_turned, down_sent, gate_sent, output_sum)
    back, sent = after((flat(back), sent), back)
    result_turned, down_sent, gate_sent, output_sum = sent
    output_part = reduce_groups(output_sum)
    opened = scatter_open(plan, back, qkv_w.T, slots)
    qkv_sum = weight_gradient(plan, normed, after(back, opened[-1]), True)
    result = hidden + scatter_end(plan, result_turned)
    outputs = jnp.where(own_valid[:, :, None], result, 0.0).astype(BF)
    qkv_part = reduce_groups(qkv_sum)
    dm = scatter_close(plan, opened, (qkv_sum, up_part, outputs))
    up_part = after(up_part, dm)
    up_sent = send_rows(plan, up_part)
    flip = plan.side * (width // 2) if plan.fast else 0
    halves = jnp.sum(
        jnp.roll(qkv_sum.reshape(width, -1).astype(jnp.float32), flip, 0)
        * qkv_w.astype(jnp.float32),
        axis=1,
    )
    if plan.fast:
        gain_one_sum = halves[:half_width] + after(swap(halves[half_width:], "tensor", 1), dm)
    else:
        gain_one_sum = lax.psum_scatter(halves, "tensor", scatter_dimension=0, tiled=True)
    gain_one_sum = gain_one_sum / attention_gain
    weighted = dm * attention_gain
    total_one = feature_total(weighted * source)
    input_grad = grad_hidden + inverse_one * weighted - source * inverse_one**3 * total_one / width

    gains = total_over(total_over(jnp.stack([gain_one_sum, gain_two_sum]), "ctx"), "dp")
    output_part, qkv_part = after((output_part, qkv_part), gains)
    output_sent = send_columns(plan, output_part)
    qkv_sent = send_rows(plan, qkv_part)
    down_out = finish_rows(plan, down_sent)
    (gate_out,) = finish_columns(plan, gate_sent, ((units, 1),))
    (up_out,) = finish_columns(plan, up_sent, ((units, 1),))
    output_out = finish_rows(plan, output_sent)
    query_out, key_out, value_out = finish_columns(
        plan, qkv_sent, ((wide, 1), (narrow, share), (narrow, share))
    )
    return (
        outputs,
        input_grad.astype(BF),
        query_out,
        key_out,
        value_out,
        output_out,
        gate_out,
        up_out,
        down_out,
        gains[0],
        gains[1],
    )


def solution(mesh):
    return jax.shard_map(
        per_device,
        mesh=mesh,
        in_specs=(
            P("dp", "ctx", "tensor"),
            P("dp", "ctx", "tensor"),
            P(),
            P(),
            P("ctx", "tensor"),
            P("ctx", "tensor"),
            P("ctx", "tensor"),
            P("tensor", "ctx"),
            P("ctx", "tensor"),
            P("ctx", "tensor"),
            P("tensor", "ctx"),
            P("tensor"),
            P("tensor"),
        ),
        out_specs=(
            P("dp", "ctx", "tensor"),
            P("dp", "ctx", "tensor"),
            P(("dp", "ctx"), "tensor"),
            P(("dp", "ctx"), "tensor"),
            P(("dp", "ctx"), "tensor"),
            P("tensor", ("dp", "ctx")),
            P(("dp", "ctx"), "tensor"),
            P(("dp", "ctx"), "tensor"),
            P("tensor", ("dp", "ctx")),
            P("tensor"),
            P("tensor"),
        ),
        check_vma=False,
    )
```

time: 768 us -> 689 us (0.90)
  matrix products: 110 us -> 38.6 us
  Pallas kernels: 119 us -> 177 us
  waiting for transfers between devices: 267 us -> 214 us
  other arithmetic: 113 us -> 98.6 us
  starting transfers between devices: 63 us -> 75.9 us
  local copies, waits for them, and re-layouts: 71.8 us -> 61.5 us
    ppermute x20 -> x0, waiting for transfers between devices: 181 us -> none  [turn(): return lax.ppermute(values, ('ctx', 'tensor'), pairs)]
    ppermute x53 -> x84, waiting for transfers between devices: 81.8 us -> 185 us  [swap(): return lax.ppermute(values, axis, [(i, i ^ mask) for i in range(size)])]
    pallas_call x0 -> x4, Pallas kernels: none -> 73.5 us  [row_blocks(): pl.pallas_call(kernel, grid=(lines // rows,), in_specs=[pl.BlockSpec((row...]
    dot_general x13 -> x10, matrix products: 110 us -> 38.6 us  [matmul(): return jnp.dot(left, right, preferred_element_type=jnp.float32)]
    ppermute x53 -> x84, starting transfers between devices: 36.1 us -> 75.2 us  [swap(): return lax.ppermute(values, axis, [(i, i ^ mask) for i in range(size)])]
    ppermute x20 -> x0, starting transfers between devices: 26.2 us -> none  [turn(): return lax.ppermute(values, ('ctx', 'tensor'), pairs)]
    all_gather x2 -> x1, waiting for transfers between devices: 4.36 us -> 23.7 us  [split_shared(): whole = lax.all_gather(whole, 'dp')]
    dynamic_update_slice x17 -> x0, other arithmetic: 16.5 us -> none  [the longest x8 9.67 us: finish_rows(): lax.dynamic_update_slice(whole, piece.astype(jnp.float32), (member * heig...]
  transfers between devices with their start and end apart: 79 -> 90, of which waited for: 28 -> 34; matrix products, arithmetic and copies ran while one was open for 26% -> 23% of each run, Pallas kernels for 16% -> 26%
where the time goes in v3:
time: 689 us; the launch traced here: 682 us
  waiting for transfers between devices  214 us (31%)
  Pallas kernels  177 us (26%)
  other arithmetic  98.6 us (14%)
  starting transfers between devices  75.9 us (11%)
  local copies, waits for them, and re-layouts  61.5 us (9%)
  matrix products  38.6 us (6%)
  between operations  16.5 us (2%)
    ppermute x84, waiting for transfers between devices, swap(): return lax.ppermute(values, axis, [(i, i ^ mask) for i in range(size)])  185 us
    ppermute x84, starting transfers between devices, swap(): return lax.ppermute(values, axis, [(i, i ^ mask) for i in range(size)])  75.2 us
    pallas_call x4, Pallas kernels, row_blocks(): pl.pallas_call(kernel, grid=(lines // rows,), in_specs=[pl.BlockSpec((row...  73.5 us
    pallas_call x5, Pallas kernels, weight_gradient(): pl.pallas_call(gradient_kernel, grid_spec=pltpu.PrefetchScalarGridSpec(nu...  54 us
    pallas_call x2, Pallas kernels, attention_call(): pl.pallas_call(functools.partial(kernel, heads), grid_spec=pltpu.Prefetch...  49.2 us
    dot_general x10, matrix products, matmul(): return jnp.dot(left, right, preferred_element_type=jnp.float32)  38.6 us
    all_gather x1, waiting for transfers between devices, split_shared(): whole = lax.all_gather(whole, 'dp')  23.7 us
    unnamed x163, local copies, waits for them, and re-layouts  23.2 us
  transfers between devices with their start and end apart: 90, of which 34 were waited for; matrix products, arithmetic and copies ran while one was open for 23% of the time, Pallas kernels for 26%

profile of v3, /device:TPU:0, one launch (start us, length us, event | category | flops | bytes accessed | tf_op | source)
XLA Modules:
  0.0 681.5 jit_solution(18158621821518001711)
XLA Ops:
  41.0 25.3 %collective-permute-done.11 = bf16[512,384]{1,0:T(8,128)(2,1)} collective-permute-done((bf16[512,384]{1,0:T(8,128)(2,1)}, bf16[512,384]{1,0:T(8,128)(2,1)}, u32[]{:S(2)}, u32[]{:S(2)}) %collective-permute-start.11) | collective-permute-done | bytes 393248 | tf_op jit(solution)/shard_map/ppermute | solution.py:312
  73.9 9.3 %collective-permute-done.8 = bf16[768,512]{1,0:T(8,128)(2,1)} collective-permute-done((bf16[768,512]{1,0:T(8,128)(2,1)}, bf16[768,512]{1,0:T(8,128)(2,1)}, u32[]{:S(2)}, u32[]{:S(2)}) %collective-permute-start.8) | collective-permute-done | bytes 786464 | tf_op jit(solution)/shard_map/ppermute | solution.py:312
  85.8 9.9 %collective-permute-done.2 = bf16[256,1024]{1,0:T(8,128)(2,1)S(1)} collective-permute-done((bf16[256,1024]{1,0:T(8,128)(2,1)S(1)}, bf16[256,1024]{1,0:T(8,128)(2,1)S(1)}, u32[]{:S(2)}, u32[]{:S(2)}) %collective-permute-start.2) | collective-permute-done | bytes 524320 | tf_op jit(solution)/shard_map/ppermute | solution.py:312
  95.7 10.6 %collective-permute-done.3 = bf16[256,1024]{1,0:T(8,128)(2,1)} collective-permute-done((bf16[256,1024]{1,0:T(8,128)(2,1)}, bf16[256,1024]{1,0:T(8,128)(2,1)}, u32[]{:S(2)}, u32[]{:S(2)}) %collective-permute-start.3) | collective-permute-done | bytes 524320 | tf_op jit(solution)/shard_map/ppermute | solution.py:312
  116.5 4.5 fusion.14.projected_here
  121.1 6.2 fusion.12.projected_away
  127.3 19.1 %shard_map.212 = (bf16[2,2,256,384]{3,2,1,0:T(8,128)(2,1)S(1)}, bf16[2,2,256,384]{3,2,1,0:T(8,128)(2,1)S(1)}, bf16[2,2,256,256]{3,2,1,0:T(8,128)(2,1)S(1)}, bf16...) custom-call(s32[4]{0:T(128)S(1)} %fusion.61.order, s32[2]{0:T(128)S(1)} %dynamic_slice.165.lengths, ...), custom_call_target="tpu_custom_call" | custom-call | flops 5368709120 | bytes 16777216 | tf_op jit(solution)/shard_map/pallas_call | solution.py:215
  146.7 3.3 convolution_convert_fusion.2
  163.0 21.7 %collective-permute-done.17 = bf16[256,2048]{1,0:T(8,128)(2,1)S(1)} collective-permute-done((bf16[256,2048]{1,0:T(8,128)(2,1)S(1)}, bf16[256,2048]{1,0:T(8,128)(2,1)S(1)}, u32[]{:S(2)}, u32[]{:S(2)}) %collective-permute-start.17) | collective-permute-done | bytes 1048608 | tf_op jit(solution)/shard_map/ppermute | solution.py:312
  191.5 4.5 broadcast_in_dim.132
  205.7 23.7 %all-gather.3.cloned.1.call-done = bf16[8,768,512]{2,1,0:T(8,128)(2,1)} async-done(((bf16[2,768,512]{2,1,0:T(8,128)(2,1)}), bf16[8,768,512]{2,1,0:T(8,128)(2,1)}) %all-gather.3.cloned.1.call-update) | async-done | bytes 6291472 | tf_op jit(solution)/shard_map/all_gather | solution.py:443
  229.4 3.5 slice_bitcast_fusion
  238.6 9.6 %collective-permute-done.22 = bf16[256,1024]{1,0:T(8,128)(2,1)S(1)} collective-permute-done((bf16[256,1024]{1,0:T(8,128)(2,1)S(1)}, bf16[256,1024]{1,0:T(8,128)(2,1)S(1)}, u32[]{:S(2)}, u32[]{:S(2)}) %collective-permute-start.22) | collective-permute-done | bytes 524320 | tf_op jit(solution)/shard_map/ppermute | solution.py:312
  254.4 6.5 collective-permute-done.23
  260.9 10.0 %collective-permute-done.24 = bf16[256,1024]{1,0:T(8,128)(2,1)S(1)} collective-permute-done((bf16[256,1024]{1,0:T(8,128)(2,1)S(1)}, bf16[256,1024]{1,0:T(8,128)(2,1)S(1)}, u32[]{:S(2)}, u32[]{:S(2)}) %collective-permute-start.24) | collective-permute-done | bytes 524320 | tf_op jit(solution)/shard_map/ppermute | solution.py:312
  280.1 15.2 %shard_map.213 = (bf16[1024,1024]{1,0:T(8,128)(2,1)}, bf16[1024,1024]{1,0:T(8,128)(2,1)}, bf16[1024,1024]{1,0:T(8,128)(2,1)}) custom-call(bf16[1024,2048]{1,0:T(8,128)(2,1)} %bitcast.51.normed.left_here, bf16[2048,2048]{1,0:T(8,128)(2,1)} %maximum_dynamic-update-slice_fusion.2.weights), custom_call_target="tpu_custom_call" | custom-call | flops 8589934592 | bytes 18874368 | tf_op jit(solution)/shard_map/pallas_call | solution.py:529
  296.8 5.8 collective-permute-done.34
  304.0 15.3 %shard_map.214 = (bf16[1024,1024]{1,0:T(8,128)(2,1)}, bf16[1024,1024]{1,0:T(8,128)(2,1)}, bf16[1024,1024]{1,0:T(8,128)(2,1)}) custom-call(bf16[1024,2048]{1,0:T(8,128)(2,1)} %bitcast.53.normed.left_away, bf16[2048,2048]{1,0:T(8,128)(2,1)} %maximum_dynamic-update-slice_fusion.2.weights), custom_call_target="tpu_custom_call" | custom-call | flops 8589934592 | bytes 18874368 | tf_op jit(solution)/shard_map/pallas_call | solution.py:529
  329.6 14.4 %shard_map.215 = bf16[4,1024,512]{2,1,0:T(8,128)(2,1)} custom-call(s32[1]{0:T(128)} %bitcast.63.side, bf16[1024,1024]{1,0:T(8,128)(2,1)S(1)} %copy-done.6, bf16[1024,1024]{1,0:T(8,128)(2,1)S(1)} %copy-done.7, bf16[1024,2048]{1,0:T(8,128)(2,1)} %fusion.right_here.target, bf16[1024,2048]{1,0:T(8,128)(2,1)} %bitcast.62.right_away.target), custom_call_target="tpu_custom_call" | custom-call | flops 8589934592 | bytes 16777216 | tf_op jit(solution)/shard_map/pallas_call | solution.py:584
  351.5 21.7 %shard_map.216 = (bf16[1024,2048]{1,0:T(8,128)(2,1)}, bf16[1024,2048]{1,0:T(8,128)(2,1)}) custom-call(bf16[1024,2048]{1,0:T(8,128)(2,1)} %bitcast.62.right_away.target, bf16[1024,1024]{1,0:T(8,128)(2,1)} %get-tuple-element.245.slope_gate, bf16[1024,1024]{1,0:T(8,128)(2,1)} %get-tuple-element.246.slope_up, ...), custom_call_target="tpu_custom_call" | custom-call | flops 12884901888 | bytes 29360128 | tf_op jit(solution)/shard_map/pallas_call | solution.py:529
  373.8 21.2 %shard_map.217 = (bf16[1024,2048]{1,0:T(8,128)(2,1)}, bf16[1024,2048]{1,0:T(8,128)(2,1)}) custom-call(bf16[1024,2048]{1,0:T(8,128)(2,1)} %fusion.right_here.target, bf16[1024,1024]{1,0:T(8,128)(2,1)} %get-tuple-element.250.slope_gate, bf16[1024,1024]{1,0:T(8,128)(2,1)} %get-tuple-element.251.slope_up, ...), custom_call_target="tpu_custom_call" | custom-call | flops 12884901888 | bytes 29360128 | tf_op jit(solution)/shard_map/pallas_call | solution.py:529
  395.0 3.4 fusion.19
  403.0 12.6 %shard_map.218 = bf16[4,512,1024]{2,1,0:T(8,128)(2,1)S(1)} custom-call(s32[1]{0:T(128)} %bitcast.63.side, bf16[1024,2048]{1,0:T(8,128)(2,1)} %bitcast.51.normed.left_here, bf16[1024,2048]{1,0:T(8,128)(2,1)} %bitcast.53.normed.left_away, bf16[1024,2048]{1,0:T(8,128)(2,1)} %get-tuple-element.255.right_here, bf16[1024,2048]{1,0:T(8,128)(2,1)} %get-tuple-element.256.right_away), custom_call_target="tpu_custom_call" | custom-call | flops 8589934592 | bytes 16777216 | tf_op jit(solution)/shard_map/pallas_call | solution.py:584
  417.7 12.5 %shard_map.219 = bf16[4,512,1024]{2,1,0:T(8,128)(2,1)S(1)} custom-call(s32[1]{0:T(128)} %bitcast.63.side, bf16[1024,2048]{1,0:T(8,128)(2,1)} %bitcast.51.normed.left_here, bf16[1024,2048]{1,0:T(8,128)(2,1)} %bitcast.53.normed.left_away, bf16[1024,2048]{1,0:T(8,128)(2,1)} %get-tuple-element.255.right_here, bf16[1024,2048]{1,0:T(8,128)(2,1)} %get-tuple-element.256.right_away), custom_call_target="tpu_custom_call" | custom-call | flops 8589934592 | bytes 16777216 | tf_op jit(solution)/shard_map/pallas_call | solution.py:584
  436.9 11.2 %collective-permute-done.41 = bf16[256,1024]{1,0:T(8,128)(2,1)S(1)} collective-permute-done((bf16[256,1024]{1,0:T(8,128)(2,1)S(1)}, bf16[256,1024]{1,0:T(8,128)(2,1)S(1)}, u32[]{:S(2)}, u32[]{:S(2)}) %collective-permute-start.41) | collective-permute-done | bytes 524320 | tf_op jit(solution)/shard_map/ppermute | solution.py:312
  449.3 2.7 fusion.44
  453.3 2.9 collective-permute-done.43
  459.8 4.7 convolution_convert_fusion.4
  468.8 4.7 convolution_convert_fusion.5
  473.5 5.9 collective-permute-done.44
  480.1 11.3 %collective-permute-done.48 = bf16[256,1024]{1,0:T(8,128)(2,1)S(1)} collective-permute-done((bf16[256,1024]{1,0:T(8,128)(2,1)S(1)}, bf16[256,1024]{1,0:T(8,128)(2,1)S(1)}, u32[]{:S(2)}, u32[]{:S(2)}) %collective-permute-start.48) | collective-permute-done | bytes 524320 | tf_op jit(solution)/shard_map/ppermute | solution.py:312
  496.0 5.9 collective-permute-done.46
  511.1 3.6 convolution_convert_fusion.7
  520.3 3.5 convolution_convert_fusion.6
  525.7 6.3 shard_map.220
  538.5 30.1 %shard_map.221 = (bf16[2,2,256,384]{3,2,1,0:T(8,128)(2,1)S(1)}, bf16[2,2,256,384]{3,2,1,0:T(8,128)(2,1)S(1)}) custom-call(s32[4]{0:T(128)S(1)} %copy-done.5, s32[2]{0:T(128)S(1)} %dynamic_slice.165.lengths, bf16[2,2,256,384]{3,2,1,0:T(8,128)(2,1)S(1)} %copy-done.12, bf16[2,2,256,384]{3,2,1,0:T(8,128)(2,1)S(1)} %copy-done.14, ...), custom_call_target="tpu_custom_call" | custom-call | flops 13421772800 | bytes 16777216 | tf_op jit(solution)/shard_map/pallas_call | solution.py:215
  568.7 4.5 convolution_convert_fusion
  573.3 3.4 fusion.29
  584.2 3.2 fusion.23
  594.1 2.8 fusion.41
  598.2 8.3 %shard_map.222 = bf16[4,512,384]{2,1,0:T(8,128)(2,1)} custom-call(s32[1]{0:T(128)} %bitcast.63.side, bf16[1024,2048]{1,0:T(8,128)(2,1)} %bitcast.112.left_here, bf16[1024,2048]{1,0:T(8,128)(2,1)} %bitcast.113.left_away, bf16[1024,384]{1,0:T(8,128)(2,1)S(1)} %bitcast.294, bf16[1024,384]{1,0:T(8,128)(2,1)S(1)} %bitcast.296), custom_call_target="tpu_custom_call" | custom-call | flops 3221225472 | bytes 11534336 | tf_op jit(solution)/shard_map/pallas_call | solution.py:584
  606.4 7.4 %collective-permute-done.64 = bf16[2,256,1024]{2,1,0:T(8,128)(2,1)} collective-permute-done((bf16[2,256,1024]{2,1,0:T(8,128)(2,1)}, bf16[2,256,1024]{2,1,0:T(8,128)(2,1)}, u32[]{:S(2)}, u32[]{:S(2)}) %collective-permute-start.64) | collective-permute-done | bytes 1048608 | tf_op jit(solution)/shard_map/ppermute | solution.py:312
  616.3 3.4 fusion.26
  626.4 5.8 collective-permute-done.65
  632.4 2.7 fusion.38
  643.0 3.5 collective-permute-start.74
  649.5 3.7 collective-permute-done.82
  655.0 4.6 reduce-scatter.14.cloned.1.call-done
  (473 shorter events, 229.3 us)
Async XLA Ops:
  7.2 222.2 %all-gather.3.cloned.1.call-start = ((), (), s32[]{:S(2)}) async-start(), calls=%async_computation.10 | async-start | bytes 7864320 | tf_op jit(solution)/shard_map/all_gather | solution.py:443
  11.3 25.6 %collective-permute-start.9 = (bf16[512,384]{1,0:T(8,128)(2,1)}, bf16[512,384]{1,0:T(8,128)(2,1)}, u32[]{:S(2)}, u32[]{:S(2)}) collective-permute-start(bf16[512,384]{1,0:T(8,128)(2,1)} %pad_maximum_fusion.10), channel_id=1, source_target_pairs={{0,2},{2,0},{4,6},{6,4},{1,3},{3,1},{5,7},{7,5},{8,10},{10,8},{12,... | collective-permute-start | bytes 1179656 | tf_op jit(solution)/shard_map/ppermute | solution.py:312
  12.6 24.3 %collective-permute-start.10 = (bf16[512,384]{1,0:T(8,128)(2,1)}, bf16[512,384]{1,0:T(8,128)(2,1)}, u32[]{:S(2)}, u32[]{:S(2)}) collective-permute-start(bf16[512,384]{1,0:T(8,128)(2,1)} %pad_maximum_fusion.11), channel_id=1, source_target_pairs={{0,4},{2,6},{4,0},{6,2},{1,5},{3,7},{5,1},{7,3},{8,12},{10,14},{12... | collective-permute-start | bytes 1179656 | tf_op jit(solution)/shard_map/ppermute | solution.py:312
  27.3 42.5 %collective-permute-start.7 = (bf16[768,512]{1,0:T(8,128)(2,1)}, bf16[768,512]{1,0:T(8,128)(2,1)}, u32[]{:S(2)}, u32[]{:S(2)}) collective-permute-start(bf16[768,512]{1,0:T(8,128)(2,1)} %get-tuple-element.365), channel_id=1, source_target_pairs={{0,4},{2,6},{4,0},{6,2},{1,5},{3,7},{5,1},{7,3},{8,12},{10,14},{12... | collective-permute-start | bytes 2359304 | tf_op jit(solution)/shard_map/ppermute | solution.py:312
  33.0 34.2 %collective-permute-start.1 = (bf16[256,1024]{1,0:T(8,128)(2,1)S(1)}, bf16[256,1024]{1,0:T(8,128)(2,1)}, u32[]{:S(2)}, u32[]{:S(2)}) collective-permute-start(bf16[256,1024]{1,0:T(8,128)(2,1)S(1)} %get-tuple-element.180), channel_id=1, source_target_pairs={{0,1},{1,0},{2,3},{3,2},{4,5},{5,4},{6,7},{7,6},{8,9},{9,8},{10,11... | collective-permute-start | bytes 1572872 | tf_op jit(solution)/shard_map/ppermute | solution.py:312
  34.5 34.3 %collective-permute-start.5 = (bf16[256,1024]{1,0:T(8,128)(2,1)S(1)}, bf16[256,1024]{1,0:T(8,128)(2,1)}, u32[]{:S(2)}, u32[]{:S(2)}) collective-permute-start(bf16[256,1024]{1,0:T(8,128)(2,1)S(1)} %get-tuple-element.184), channel_id=1, source_target_pairs={{0,4},{2,6},{4,0},{6,2},{1,5},{3,7},{5,1},{7,3},{8,12},{10,14},{12... | collective-permute-start | bytes 1572872 | tf_op jit(solution)/shard_map/ppermute | solution.py:312
  36.8 29.4 %collective-permute-start.11 = (bf16[512,384]{1,0:T(8,128)(2,1)}, bf16[512,384]{1,0:T(8,128)(2,1)}, u32[]{:S(2)}, u32[]{:S(2)}) collective-permute-start(bf16[512,384]{1,0:T(8,128)(2,1)} %pad_maximum_fusion.12), channel_id=1, source_target_pairs={{0,6},{2,4},{4,2},{6,0},{1,7},{3,5},{5,3},{7,1},{8,14},{10,12},{12... | collective-permute-start | bytes 1179656 | tf_op jit(solution)/shard_map/ppermute | solution.py:312
  36.9 46.3 %collective-permute-start.8 = (bf16[768,512]{1,0:T(8,128)(2,1)}, bf16[768,512]{1,0:T(8,128)(2,1)}, u32[]{:S(2)}, u32[]{:S(2)}) collective-permute-start(bf16[768,512]{1,0:T(8,128)(2,1)} %get-tuple-element.366), channel_id=1, source_target_pairs={{0,6},{2,4},{4,2},{6,0},{1,7},{3,5},{5,3},{7,1},{8,14},{10,12},{12... | collective-permute-start | bytes 2359304 | tf_op jit(solution)/shard_map/ppermute | solution.py:312
  66.3 29.4 %collective-permute-start.2 = (bf16[256,1024]{1,0:T(8,128)(2,1)S(1)}, bf16[256,1024]{1,0:T(8,128)(2,1)S(1)}, u32[]{:S(2)}, u32[]{:S(2)}) collective-permute-start(bf16[256,1024]{1,0:T(8,128)(2,1)S(1)} %get-tuple-element.180), channel_id=1, source_target_pairs={{0,4},{2,6},{4,0},{6,2},{1,5},{3,7},{5,1},{7,3},{8,12},{10,14},{12... | collective-permute-start | bytes 1572872 | tf_op jit(solution)/shard_map/ppermute | solution.py:312
  67.2 28.4 %collective-permute-start.4 = (bf16[256,1024]{1,0:T(8,128)(2,1)S(1)}, bf16[256,1024]{1,0:T(8,128)(2,1)}, u32[]{:S(2)}, u32[]{:S(2)}) collective-permute-start(bf16[256,1024]{1,0:T(8,128)(2,1)S(1)} %get-tuple-element.184), channel_id=1, source_target_pairs={{0,1},{1,0},{2,3},{3,2},{4,5},{5,4},{6,7},{7,6},{8,9},{9,8},{10,11... | collective-permute-start | bytes 1572872 | tf_op jit(solution)/shard_map/ppermute | solution.py:312
  68.8 37.5 %collective-permute-start.3 = (bf16[256,1024]{1,0:T(8,128)(2,1)}, bf16[256,1024]{1,0:T(8,128)(2,1)}, u32[]{:S(2)}, u32[]{:S(2)}) collective-permute-start(bf16[256,1024]{1,0:T(8,128)(2,1)} %collective-permute-done.1), channel_id=1, source_target_pairs={{0,4},{2,6},{4,0},{6,2},{1,5},{3,7},{5,1},{7,3},{8,12},{10,14},{12... | collective-permute-start | bytes 1572872 | tf_op jit(solution)/shard_map/ppermute | solution.py:312
  69.8 36.5 %collective-permute-start.6 = (bf16[256,1024]{1,0:T(8,128)(2,1)}, bf16[256,1024]{1,0:T(8,128)(2,1)}, u32[]{:S(2)}, u32[]{:S(2)}) collective-permute-start(bf16[256,1024]{1,0:T(8,128)(2,1)} %collective-permute-done.5), channel_id=1, source_target_pairs={{0,1},{1,0},{2,3},{3,2},{4,5},{5,4},{6,7},{7,6},{8,9},{9,8},{10,11... | collective-permute-start | bytes 1572872 | tf_op jit(solution)/shard_map/ppermute | solution.py:312
  113.4 318.8 %reduce-scatter.6.cloned.1.call-start = ((), (), s32[]{:S(2)}) async-start(), calls=%async_computation.5 | async-start | bytes 5242880 | tf_op jit(solution)/shard_map/reduce_scatter | solution.py:604
  114.6 31.8 %collective-permute-start.13 = (bf16[256,512]{1,0:T(8,128)(2,1)S(1)}, bf16[256,512]{1,0:T(8,128)(2,1)S(1)}, u32[]{:S(2)}, u32[]{:S(2)}) collective-permute-start(bf16[256,512]{1,0:T(8,128)(2,1)S(1)} %get-tuple-element.410), channel_id=1, source_target_pairs={{0,2},{2,0},{4,6},{6,4},{1,3},{3,1},{5,7},{7,5},{8,10},{10,8},{12,... | collective-permute-start | bytes 786440 | tf_op jit(solution)/shard_map/ppermute | solution.py:312
  114.7 31.7 %collective-permute-start.14 = (bf16[256,512]{1,0:T(8,128)(2,1)S(1)}, bf16[256,512]{1,0:T(8,128)(2,1)S(1)}, u32[]{:S(2)}, u32[]{:S(2)}) collective-permute-start(bf16[256,512]{1,0:T(8,128)(2,1)S(1)} %get-tuple-element.409), channel_id=1, source_target_pairs={{0,4},{2,6},{4,0},{6,2},{1,5},{3,7},{5,1},{7,3},{8,12},{10,14},{12... | collective-permute-start | bytes 786440 | tf_op jit(solution)/shard_map/ppermute | solution.py:312
  115.0 31.4 %collective-permute-start.15 = (bf16[256,512]{1,0:T(8,128)(2,1)S(1)}, bf16[256,512]{1,0:T(8,128)(2,1)S(1)}, u32[]{:S(2)}, u32[]{:S(2)}) collective-permute-start(bf16[256,512]{1,0:T(8,128)(2,1)S(1)} %get-tuple-element.408), channel_id=1, source_target_pairs={{0,6},{2,4},{4,2},{6,0},{1,7},{3,5},{5,3},{7,1},{8,14},{10,12},{12... | collective-permute-start | bytes 786440 | tf_op jit(solution)/shard_map/ppermute | solution.py:312
  153.6 43.9 %collective-permute-start.28 = (bf16[512,2048]{1,0:T(8,128)(2,1)S(1)}, bf16[512,2048]{1,0:T(8,128)(2,1)S(1)}, u32[]{:S(2)}, u32[]{:S(2)}) collective-permute-start(bf16[512,2048]{1,0:T(8,128)(2,1)S(1)} %pad_maximum_fusion.4), channel_id=1, source_target_pairs={{0,2},{2,0},{4,6},{6,4},{1,3},{3,1},{5,7},{7,5},{8,10},{10,8},{12,... | collective-permute-start | bytes 6291464 | tf_op jit(solution)/shard_map/ppermute | solution.py:312
  159.2 25.5 %collective-permute-start.17 = (bf16[256,2048]{1,0:T(8,128)(2,1)S(1)}, bf16[256,2048]{1,0:T(8,128)(2,1)S(1)}, u32[]{:S(2)}, u32[]{:S(2)}) collective-permute-start(bf16[256,2048]{1,0:T(8,128)(2,1)S(1)} %fusion.16), channel_id=1, source_target_pairs={{0,4},{2,6},{4,0},{6,2},{1,5},{3,7},{5,1},{7,3},{8,12},{10,14},{12... | collective-permute-start | bytes 3145736 | tf_op jit(solution)/shard_map/ppermute | solution.py:312
  161.1 25.2 %collective-permute-start.18 = (bf16[2,256,1024]{2,1,0:T(8,128)(2,1)S(1)}, bf16[2,256,1024]{2,1,0:T(8,128)(2,1)S(1)}, u32[]{:S(2)}, u32[]{:S(2)}) collective-permute-start(bf16[2,256,1024]{2,1,0:T(8,128)(2,1)S(1)} %fusion.17), channel_id=1, source_target_pairs={{0,1},{1,0},{2,3},{3,2},{4,5},{5,4},{6,7},{7,6},{8,9},{9,8},{10,11... | collective-permute-start | bytes 3145736 | tf_op jit(solution)/shard_map/ppermute | solution.py:312
  205.3 27.7 %collective-permute-start.21 = (f32[2,256,1]{1,0,2:T(2,128)S(1)}, f32[2,256,1]{1,0,2:T(2,128)S(1)}, u32[]{:S(2)}, u32[]{:S(2)}) collective-permute-start(f32[2,256,1]{1,0,2:T(2,128)S(1)} %bitcast.342), channel_id=1, source_target_pairs={{0,1},{1,0},{2,3},{3,2},{4,5},{5,4},{6,7},{7,6},{8,9},{9,8},{10,11... | collective-permute-start | bytes 6152 | tf_op jit(solution)/shard_map/ppermute | solution.py:312
  236.8 24.2 %collective-permute-start.23 = (bf16[256,1024]{1,0:T(8,128)(2,1)S(1)}, bf16[256,1024]{1,0:T(8,128)(2,1)S(1)}, u32[]{:S(2)}, u32[]{:S(2)}) collective-permute-start(bf16[256,1024]{1,0:T(8,128)(2,1)S(1)} %get-tuple-element.214), channel_id=1, source_target_pairs={{0,4},{2,6},{4,0},{6,2},{1,5},{3,7},{5,1},{7,3},{8,12},{10,14},{12... | collective-permute-start | bytes 1572872 | tf_op jit(solution)/shard_map/ppermute | solution.py:312
  237.4 23.5 %collective-permute-start.25 = (bf16[256,1024]{1,0:T(8,128)(2,1)S(1)}, bf16[256,1024]{1,0:T(8,128)(2,1)S(1)}, u32[]{:S(2)}, u32[]{:S(2)}) collective-permute-start(bf16[256,1024]{1,0:T(8,128)(2,1)S(1)} %get-tuple-element.218), channel_id=1, source_target_pairs={{0,1},{1,0},{2,3},{3,2},{4,5},{5,4},{6,7},{7,6},{8,9},{9,8},{10,11... | collective-permute-start | bytes 1572872 | tf_op jit(solution)/shard_map/ppermute | solution.py:312
  248.2 22.8 %collective-permute-start.24 = (bf16[256,1024]{1,0:T(8,128)(2,1)S(1)}, bf16[256,1024]{1,0:T(8,128)(2,1)S(1)}, u32[]{:S(2)}, u32[]{:S(2)}) collective-permute-start(bf16[256,1024]{1,0:T(8,128)(2,1)S(1)} %collective-permute-done.22), channel_id=1, source_target_pairs={{0,4},{2,6},{4,0},{6,2},{1,5},{3,7},{5,1},{7,3},{8,12},{10,14},{12... | collective-permute-start | bytes 1572872 | tf_op jit(solution)/shard_map/ppermute | solution.py:312
  249.7 21.3 %collective-permute-start.27 = (bf16[256,1024]{1,0:T(8,128)(2,1)S(1)}, bf16[256,1024]{1,0:T(8,128)(2,1)S(1)}, u32[]{:S(2)}, u32[]{:S(2)}) collective-permute-start(bf16[256,1024]{1,0:T(8,128)(2,1)S(1)} %collective-permute-done.26), channel_id=1, source_target_pairs={{0,1},{1,0},{2,3},{3,2},{4,5},{5,4},{6,7},{7,6},{8,9},{9,8},{10,11... | collective-permute-start | bytes 1572872 | tf_op jit(solution)/shard_map/ppermute | solution.py:312
  273.6 30.4 %collective-permute-start.29 = (bf16[2,2,256,2048]{3,2,1,0:T(8,128)(2,1)}, bf16[2,2,256,2048]{3,2,1,0:T(8,128)(2,1)}, u32[]{:S(2)}, u32[]{:S(2)}) collective-permute-start(bf16[2,2,256,2048]{3,2,1,0:T(8,128)(2,1)} %bitcast.52), channel_id=1, source_target_pairs={{0,2},{2,0},{4,6},{6,4},{1,3},{3,1},{5,7},{7,5},{8,10},{10,8},{12,... | collective-permute-start | bytes 12582920 | tf_op jit(solution)/shard_map/ppermute | solution.py:312
  276.6 42.8 %collective-permute-start.31 = (bf16[256,1024]{1,0:T(8,128)(2,1)S(1)}, bf16[256,1024]{1,0:T(8,128)(2,1)S(1)}, u32[]{:S(2)}, u32[]{:S(2)}) collective-permute-start(bf16[256,1024]{1,0:T(8,128)(2,1)S(1)} %get-tuple-element.234), channel_id=1, source_target_pairs={{0,4},{2,6},{4,0},{6,2},{1,5},{3,7},{5,1},{7,3},{8,12},{10,14},{12... | collective-permute-start | bytes 1572872 | tf_op jit(solution)/shard_map/ppermute | solution.py:312
  278.0 24.5 %collective-permute-start.34 = (bf16[256,1024]{1,0:T(8,128)(2,1)S(1)}, bf16[256,1024]{1,0:T(8,128)(2,1)S(1)}, u32[]{:S(2)}, u32[]{:S(2)}) collective-permute-start(bf16[256,1024]{1,0:T(8,128)(2,1)S(1)} %get-tuple-element.238), channel_id=1, source_target_pairs={{0,4},{2,6},{4,0},{6,2},{1,5},{3,7},{5,1},{7,3},{8,12},{10,14},{12... | collective-permute-start | bytes 1572872 | tf_op jit(solution)/shard_map/ppermute | solution.py:312
  278.6 40.8 %collective-permute-start.33 = (bf16[256,1024]{1,0:T(8,128)(2,1)S(1)}, bf16[256,1024]{1,0:T(8,128)(2,1)S(1)}, u32[]{:S(2)}, u32[]{:S(2)}) collective-permute-start(bf16[256,1024]{1,0:T(8,128)(2,1)S(1)} %get-tuple-element.238), channel_id=1, source_target_pairs={{0,1},{1,0},{2,3},{3,2},{4,5},{5,4},{6,7},{7,6},{8,9},{9,8},{10,11... | collective-permute-start | bytes 1572872 | tf_op jit(solution)/shard_map/ppermute | solution.py:312
  295.3 24.0 %collective-permute-start.32 = (bf16[256,1024]{1,0:T(8,128)(2,1)S(1)}, bf16[256,1024]{1,0:T(8,128)(2,1)S(1)}, u32[]{:S(2)}, u32[]{:S(2)}) collective-permute-start(bf16[256,1024]{1,0:T(8,128)(2,1)S(1)} %collective-permute-done.30), channel_id=1, source_target_pairs={{0,4},{2,6},{4,0},{6,2},{1,5},{3,7},{5,1},{7,3},{8,12},{10,14},{12... | collective-permute-start | bytes 1572872 | tf_op jit(solution)/shard_map/ppermute | solution.py:312
  344.0 160.0 %reduce-scatter.8.cloned.1.call-start = ((), (), s32[]{:S(2)}) async-start(), calls=%async_computation.6 | async-start | bytes 5242880 | tf_op jit(solution)/shard_map/reduce_scatter | solution.py:604
  373.2 21.9 %collective-permute-start.38 = (bf16[2,2,256,2048]{3,2,1,0:T(8,128)(2,1)}, bf16[2,2,256,2048]{3,2,1,0:T(8,128)(2,1)S(1)}, u32[]{:S(2)}, u32[]{:S(2)}) collective-permute-start(bf16[2,2,256,2048]{3,2,1,0:T(8,128)(2,1)} %bitcast.347), channel_id=1, source_target_pairs={{0,2},{2,0},{4,6},{6,4},{1,3},{3,1},{5,7},{7,5},{8,10},{10,8},{12,... | collective-permute-start | bytes 12582920 | tf_op jit(solution)/shard_map/ppermute | solution.py:312
  398.4 33.8 %collective-permute-start.40 = (bf16[2,256,1024]{2,1,0:T(8,128)(2,1)}, bf16[2,256,1024]{2,1,0:T(8,128)(2,1)}, u32[]{:S(2)}, u32[]{:S(2)}) collective-permute-start(bf16[2,256,1024]{2,1,0:T(8,128)(2,1)} %fusion.19), channel_id=1, source_target_pairs={{0,1},{1,0},{2,3},{3,2},{4,5},{5,4},{6,7},{7,6},{8,9},{9,8},{10,11... | collective-permute-start | bytes 3145736 | tf_op jit(solution)/shard_map/ppermute | solution.py:312
  401.5 30.7 %collective-permute-start.39 = (bf16[256,2048]{1,0:T(8,128)(2,1)}, bf16[256,2048]{1,0:T(8,128)(2,1)}, u32[]{:S(2)}, u32[]{:S(2)}) collective-permute-start(bf16[256,2048]{1,0:T(8,128)(2,1)} %fusion.18), channel_id=1, source_target_pairs={{0,4},{2,6},{4,0},{6,2},{1,5},{3,7},{5,1},{7,3},{8,12},{10,14},{12... | collective-permute-start | bytes 3145736 | tf_op jit(solution)/shard_map/ppermute | solution.py:312
  417.7 188.8 %reduce-scatter.10.cloned.1.call-start = ((), (), s32[]{:S(2)}) async-start(), calls=%async_computation.7 | async-start | bytes 5242880 | tf_op jit(solution)/shard_map/reduce_scatter | solution.py:604
  464.5 28.3 %collective-permute-start.50 = (bf16[2,2,256,2048]{3,2,1,0:T(8,128)(2,1)S(1)}, bf16[2,2,256,2048]{3,2,1,0:T(8,128)(2,1)S(1)}, u32[]{:S(2)}, u32[]{:S(2)}) collective-permute-start(bf16[2,2,256,2048]{3,2,1,0:T(8,128)(2,1)S(1)} %bitcast.346), channel_id=1, source_target_pairs={{0,2},{2,0},{4,6},{6,4},{1,3},{3,1},{5,7},{7,5},{8,10},{10,8},{12,... | collective-permute-start | bytes 12582920 | tf_op jit(solution)/shard_map/ppermute | solution.py:312
  465.3 30.6 %collective-permute-start.45 = (bf16[256,1024]{1,0:T(8,128)(2,1)S(1)}, bf16[256,1024]{1,0:T(8,128)(2,1)S(1)}, u32[]{:S(2)}, u32[]{:S(2)}) collective-permute-start(bf16[256,1024]{1,0:T(8,128)(2,1)S(1)} %get-tuple-element.275), channel_id=1, source_target_pairs={{0,4},{2,6},{4,0},{6,2},{1,5},{3,7},{5,1},{7,3},{8,12},{10,14},{12... | collective-permute-start | bytes 1572872 | tf_op jit(solution)/shard_map/ppermute | solution.py:312
  466.0 25.3 %collective-permute-start.48 = (bf16[256,1024]{1,0:T(8,128)(2,1)S(1)}, bf16[256,1024]{1,0:T(8,128)(2,1)S(1)}, u32[]{:S(2)}, u32[]{:S(2)}) collective-permute-start(bf16[256,1024]{1,0:T(8,128)(2,1)S(1)} %get-tuple-element.279), channel_id=1, source_target_pairs={{0,4},{2,6},{4,0},{6,2},{1,5},{3,7},{5,1},{7,3},{8,12},{10,14},{12... | collective-permute-start | bytes 1572872 | tf_op jit(solution)/shard_map/ppermute | solution.py:312
  467.4 28.6 %collective-permute-start.47 = (bf16[256,1024]{1,0:T(8,128)(2,1)S(1)}, bf16[256,1024]{1,0:T(8,128)(2,1)S(1)}, u32[]{:S(2)}, u32[]{:S(2)}) collective-permute-start(bf16[256,1024]{1,0:T(8,128)(2,1)S(1)} %get-tuple-element.279), channel_id=1, source_target_pairs={{0,1},{1,0},{2,3},{3,2},{4,5},{5,4},{6,7},{7,6},{8,9},{9,8},{10,11... | collective-permute-start | bytes 1572872 | tf_op jit(solution)/shard_map/ppermute | solution.py:312
  479.5 22.4 %collective-permute-start.46 = (bf16[256,1024]{1,0:T(8,128)(2,1)S(1)}, bf16[256,1024]{1,0:T(8,128)(2,1)S(1)}, u32[]{:S(2)}, u32[]{:S(2)}) collective-permute-start(bf16[256,1024]{1,0:T(8,128)(2,1)S(1)} %collective-permute-done.44), channel_id=1, source_target_pairs={{0,4},{2,6},{4,0},{6,2},{1,5},{3,7},{5,1},{7,3},{8,12},{10,14},{12... | collective-permute-start | bytes 1572872 | tf_op jit(solution)/shard_map/ppermute | solution.py:312
  509.9 145.1 %reduce-scatter.12.cloned.1.call-start = ((), (), s32[]{:S(2)}) async-start(), calls=%async_computation.8 | async-start | bytes 1310720 | tf_op jit(solution)/shard_map/reduce_scatter | solution.py:604
  524.6 44.0 %collective-permute-start.57 = (bf16[128,1024]{1,0:T(8,128)(2,1)}, bf16[128,1024]{1,0:T(8,128)(2,1)}, u32[]{:S(2)}, u32[]{:S(2)}) collective-permute-start(bf16[128,1024]{1,0:T(8,128)(2,1)} %get-tuple-element.396), channel_id=1, source_target_pairs={{0,2},{2,0},{4,6},{6,4},{1,3},{3,1},{5,7},{7,5},{8,10},{10,8},{12,... | collective-permute-start | bytes 786440 | tf_op jit(solution)/shard_map/ppermute | solution.py:312
  525.1 43.5 %collective-permute-start.58 = (bf16[128,1024]{1,0:T(8,128)(2,1)}, bf16[128,1024]{1,0:T(8,128)(2,1)}, u32[]{:S(2)}, u32[]{:S(2)}) collective-permute-start(bf16[128,1024]{1,0:T(8,128)(2,1)} %get-tuple-element.395), channel_id=1, source_target_pairs={{0,4},{2,6},{4,0},{6,2},{1,5},{3,7},{5,1},{7,3},{8,12},{10,14},{12... | collective-permute-start | bytes 786440 | tf_op jit(solution)/shard_map/ppermute | solution.py:312
  532.0 36.6 %collective-permute-start.59 = (bf16[128,1024]{1,0:T(8,128)(2,1)S(1)}, bf16[128,1024]{1,0:T(8,128)(2,1)S(1)}, u32[]{:S(2)}, u32[]{:S(2)}) collective-permute-start(bf16[128,1024]{1,0:T(8,128)(2,1)S(1)} %get-tuple-element.394), channel_id=1, source_target_pairs={{0,6},{2,4},{4,2},{6,0},{1,7},{3,5},{5,3},{7,1},{8,14},{10,12},{12... | collective-permute-start | bytes 786440 | tf_op jit(solution)/shard_map/ppermute | solution.py:312
  532.8 35.9 %collective-permute-start.52 = (bf16[256,2048]{1,0:T(8,128)(2,1)}, bf16[256,2048]{1,0:T(8,128)(2,1)S(1)}, u32[]{:S(2)}, u32[]{:S(2)}) collective-permute-start(bf16[256,2048]{1,0:T(8,128)(2,1)} %fusion.20), channel_id=1, source_target_pairs={{0,4},{2,6},{4,0},{6,2},{1,5},{3,7},{5,1},{7,3},{8,12},{10,14},{12... | collective-permute-start | bytes 3145736 | tf_op jit(solution)/shard_map/ppermute | solution.py:312
  533.6 35.1 %collective-permute-start.53 = (bf16[2,256,1024]{2,1,0:T(8,128)(2,1)}, bf16[2,256,1024]{2,1,0:T(8,128)(2,1)S(1)}, u32[]{:S(2)}, u32[]{:S(2)}) collective-permute-start(bf16[2,256,1024]{2,1,0:T(8,128)(2,1)} %fusion.21), channel_id=1, source_target_pairs={{0,1},{1,0},{2,3},{3,2},{4,5},{5,4},{6,7},{7,6},{8,9},{9,8},{10,11... | collective-permute-start | bytes 3145736 | tf_op jit(solution)/shard_map/ppermute | solution.py:312
  578.9 80.8 %reduce-scatter.14.cloned.1.call-start = ((), (), s32[]{:S(2)}) async-start(), calls=%async_computation.9 | async-start | bytes 1966080 | tf_op jit(solution)/shard_map/reduce_scatter | solution.py:604
  587.4 26.4 %collective-permute-start.64 = (bf16[2,256,1024]{2,1,0:T(8,128)(2,1)}, bf16[2,256,1024]{2,1,0:T(8,128)(2,1)}, u32[]{:S(2)}, u32[]{:S(2)}) collective-permute-start(bf16[2,256,1024]{2,1,0:T(8,128)(2,1)} %fusion.23), channel_id=1, source_target_pairs={{0,1},{1,0},{2,3},{3,2},{4,5},{5,4},{6,7},{7,6},{8,9},{9,8},{10,11... | collective-permute-start | bytes 3145736 | tf_op jit(solution)/shard_map/ppermute | solution.py:312
  591.4 24.8 %collective-permute-start.63 = (bf16[256,2048]{1,0:T(8,128)(2,1)}, bf16[256,2048]{1,0:T(8,128)(2,1)}, u32[]{:S(2)}, u32[]{:S(2)}) collective-permute-start(bf16[256,2048]{1,0:T(8,128)(2,1)} %fusion.22), channel_id=1, source_target_pairs={{0,4},{2,6},{4,0},{6,2},{1,5},{3,7},{5,1},{7,3},{8,12},{10,14},{12... | collective-permute-start | bytes 3145736 | tf_op jit(solution)/shard_map/ppermute | solution.py:312
  (119 other events, 939.8 us)
Sparse Core Ops, SparseCore 0:
  113.5 115.8 all-gather.2
  344.1 74.1 reduce-scatter.5
  420.7 77.2 reduce-scatter.7
  510.0 74.1 reduce-scatter.9
  586.4 27.6 reduce-scatter.11
  626.5 33.1 reduce-scatter.13

commit v4 on v3

--- a/solution.py
+++ b/solution.py
@@ -326,6 +326,16 @@
     return zero, zero_side, zero_ctx, zero_far, one, one_side, one_ctx, one_far
 
 
+def aside_open(plan, values):
+    if not plan.fast:
+        return gather_open(plan, values)
+    return values, swap(values, "tensor", 1), swap(values, "ctx", 2)
+
+
+def aside_turn(plan, opened):
+    return (*opened, swap(opened[2], "tensor", 1)) if plan.fast else opened
+
+
 def gather_close(plan, opened, finish=None):
     if finish is None:
         finish = [lambda half: half] * 2
@@ -334,6 +344,12 @@
         whole = opened[0].swapaxes(0, 1)
         return finish[0](whole[:, :half]), finish[1](whole[:, half:])
     opened = lax.optimization_barrier(opened)
+    if len(opened) == 4:
+        values, side, ctx, far = opened
+        near = jnp.concatenate([values, side], axis=2)
+        here = jnp.stack([near, jnp.concatenate([ctx, far], axis=2)], axis=1)
+        here = finish[0](here)
+        return here, swap(here, "ctx", 1)
     zero, zero_side, zero_ctx, zero_far, one, one_side, one_ctx, one_far = opened
     rows = [
         jnp.concatenate(pair, axis=1)
@@ -414,42 +430,24 @@
     return found
 
 
-def shared_pieces(plan, columns, rows):
+def shared_pieces(plan, piece, anchor):
     if not plan.fast:
-        return exchange_pieces(plan, columns), exchange_pieces(plan, rows)
-    count = plan.groups
-    narrow = rows(plan.place).shape[1]
-
-    def quarter(piece):
-        size = piece.shape[0] // count
-        return lax.dynamic_slice_in_dim(piece, plan.group * size, size, 0)
-
+        return exchange_pieces(plan, piece)
     got = []
     for mask in (2, 3):
-        wide = quarter(columns(plan.place ^ mask))
-        strips = [wide[:, i : i + narrow] for i in range(0, wide.shape[1], narrow)]
-        strips.append(quarter(rows(plan.place ^ mask)))
-        got.append(swap(jnp.concatenate(strips), "ctx", mask))
+        mine = piece(plan.place ^ mask)
+        size = mine.shape[0] // plan.groups
+        mine = lax.dynamic_slice_in_dim(mine, plan.group * size, size, 0)
+        got.append(swap(after(mine, anchor), "ctx", mask))
     return jnp.stack(got)
 
 
-def core_pieces(plan, piece):
-    return [piece(plan.place), swap(piece(plan.place ^ 1), "ctx", 1)]
-
-
-def split_shared(plan, whole, columns, rows):
+def shared_close(plan, shared, piece, anchor):
     if not plan.fast:
-        return whole
-    whole = lax.all_gather(whole, "dp")
-    count = plan.groups
-    high = columns[0].shape[0] // count
-    strips = columns[0].shape[1] // rows[0].shape[1]
-    for index in range(2):
-        part = whole[:, index]
-        wide = [part[:, i * high : (i + 1) * high].reshape(high * count, -1) for i in range(strips)]
-        columns = columns + [jnp.concatenate(wide, axis=1)]
-        rows = rows + [part[:, strips * high :].reshape(rows[0].shape)]
-    return columns, rows
+        return [(item, None) for item in shared]
+    whole = lax.all_gather(shared, "dp")
+    core = swap(after(piece(plan.place ^ 1), anchor), "ctx", 1)
+    return [(piece(plan.place), None), (core, None), (whole, 0), (whole, 1)]
 
 
 def place_rows(plan, found):
@@ -500,7 +498,23 @@
     return piece
 
 
-def forward_units_kernel(normed, weights, active, slope_gate, slope_up):
+def put_rows(places, pieces, whole):
+    rows = whole.shape[0] // len(pieces)
+    for mask, piece in enumerate(pieces):
+        start = pl.multiple_of(places[mask] * rows, rows)
+        whole[pl.ds(start, rows)] = piece[...].reshape(rows, whole.shape[1])
+
+
+def put_columns(places, pieces, whole):
+    columns = whole.shape[1] // len(pieces)
+    for mask, piece in enumerate(pieces):
+        start = pl.multiple_of(places[mask] * columns, columns)
+        whole[:, pl.ds(start, columns)] = piece[...]
+
+
+def forward_units_kernel(places, normed, *refs):
+    pieces, (active, slope_gate, slope_up, weights) = refs[:-4], refs[-4:]
+    pl.when(pl.program_id(0) == 0)(lambda: put_rows(places, pieces, weights))
     units = weights.shape[1] // 2
     gate = matmul(normed[...], weights[:, :units])
     upward = matmul(normed[...], weights[:, units:])
@@ -511,7 +525,15 @@
     slope_up[...] = swish.astype(BF)
 
 
-def backward_units_kernel(target, slope_gate, slope_up, down, weights, grads, back):
+def backward_units_kernel(places, target, slope_gate, slope_up, *refs):
+    pieces, (grads, back, weights, down) = refs[:-4], refs[-4:]
+    half = len(pieces) // 2
+
+    @pl.when(pl.program_id(0) == 0)
+    def _():
+        put_rows(places, pieces[:half], weights)
+        put_columns(places, pieces[half:], down)
+
     units = down.shape[0]
     across = (((1,), (1,)), ((), ()))
     grad = lax.dot_general(target[...], down[...], across, preferred_element_type=jnp.float32)
@@ -521,37 +543,57 @@
     back[...] = total.astype(BF)
 
 
-def row_blocks(kernel, blocked, whole, widths):
+def whole_spec(array, index):
+    once = pl.Buffered(1)
+    if index is None:
+        return pl.BlockSpec(array.shape, lambda i, _: (0, 0), pipeline_mode=once)
+    groups, _, rows, columns = array.shape
+    return pl.BlockSpec(
+        (groups, 1, rows, columns), lambda i, _: (0, index, 0, 0), pipeline_mode=once
+    )
+
+
+def row_blocks(kernel, places, blocked, pieces, widths, scratch):
     lines = blocked[0].shape[0]
     rows = min(512, lines)
-    flops = sum(2 * lines * item.shape[0] * item.shape[1] for item in whole)
+    flops = sum(2 * lines * a * b for a, b in scratch)
     moved = sum(2 * lines * item.shape[1] for item in blocked) + sum(2 * lines * w for w in widths)
     return pl.pallas_call(
         kernel,
-        grid=(lines // rows,),
-        in_specs=[pl.BlockSpec((rows, item.shape[1]), lambda i: (i, 0)) for item in blocked]
-        + [pl.BlockSpec(item.shape, lambda i: (0, 0)) for item in whole],
-        out_specs=[pl.BlockSpec((rows, width), lambda i: (i, 0)) for width in widths],
+        grid_spec=pltpu.PrefetchScalarGridSpec(
+            num_scalar_prefetch=1,
+            grid=(lines // rows,),
+            in_specs=[pl.BlockSpec((rows, item.shape[1]), lambda i, _: (i, 0)) for item in blocked]
+            + [whole_spec(*piece) for piece in pieces],
+            out_specs=[pl.BlockSpec((rows, width), lambda i, _: (i, 0)) for width in widths],
+            scratch_shapes=[pltpu.VMEM(shape, BF) for shape in scratch],
+        ),
         out_shape=[jax.ShapeDtypeStruct((lines, width), BF) for width in widths],
-        compiler_params=pltpu.CompilerParams(vmem_limit_bytes=56 * 2**20),
+        compiler_params=pltpu.CompilerParams(vmem_limit_bytes=58 * 2**20),
         cost_estimate=pl.CostEstimate(
             flops=flops,
-            bytes_accessed=moved + sum(2 * item.size for item in whole),
+            bytes_accessed=moved + sum(2 * a * b for a, b in scratch),
             transcendentals=0,
         ),
-    )(*blocked, *whole)
-
-
-def forward_units(normed, weights):
-    return row_blocks(forward_units_kernel, [normed], [weights], [weights.shape[1] // 2] * 3)
-
-
-def backward_units(target, slopes, down, weights):
+    )(places, *blocked, *[array for array, _ in pieces])
+
+
+def forward_units(places, normed, pieces):
+    both = pieces[0][0].shape[1]
+    shape = (normed.shape[1], both)
+    return row_blocks(forward_units_kernel, places, [normed], pieces, [both // 2] * 3, [shape])
+
+
+def backward_units(places, target, slopes, pieces, down):
+    both = pieces[0][0].shape[1]
+    width = target.shape[1]
     return row_blocks(
         backward_units_kernel,
+        places,
         [target, *slopes],
-        [down, weights],
-        [weights.shape[1], weights.shape[0]],
+        pieces + [(item, None) for item in down],
+        [both, width],
+        [(width, both), (both // 2, width)],
     )
 
 
@@ -602,6 +644,17 @@
 
 def reduce_groups(grad):
     return lax.psum_scatter(grad, "dp", scatter_dimension=0)
+
+
+def reduce_both(plan, left, right):
+    rows, columns = left.shape[1:]
+    if not plan.fast or 2 * rows != right.shape[1]:
+        return reduce_groups(left), reduce_groups(right)
+    half = columns // 2
+    folded = jnp.concatenate([left[:, :, :half], left[:, :, half:]], axis=1)
+    both = reduce_groups(jnp.concatenate([folded, right], axis=2))
+    left = jnp.concatenate([both[:rows, :half], both[rows:, :half]], axis=1)
+    return left, both[:, half:]
 
 
 def finish_columns(plan, found, widths):
@@ -686,18 +739,13 @@
 
     source = inputs.astype(jnp.float32)
     inverse_one = lax.rsqrt(feature_total(source * source) / width + EPS)
-    columns = column_piece([gate_weight, up_weight], parts)
-    rows_piece = row_piece(down_weight, parts)
-    shared = shared_pieces(plan, columns, rows_piece)
     opened = gather_open(plan, (source * inverse_one * attention_gain).astype(BF))
     qkv_w = place_rows(
         plan,
         exchange_pieces(plan, column_piece([query_weight, key_weight, value_weight], parts, HD)),
     )
-    opened, shared = after((opened, shared), (tables, qkv_w))
-    normed = gather_close(plan, opened)
-    late = after((output_weight, gate_weight, up_weight, down_weight), normed[0])
-    o_found = exchange_pieces(plan, row_piece(late[0], parts))
+    normed = gather_close(plan, after(opened, (tables, qkv_w)))
+    o_found = exchange_pieces(plan, row_piece(after(output_weight, normed[0]), parts))
     normed = flat(normed)
 
     wide = query_weight.shape[1] // parts
@@ -705,55 +753,59 @@
     narrow = key_weight.shape[1] * share // parts
     half_shape = (slots, parts // 2, rows, -1)
     projected = [matmul(item, qkv_w).reshape(half_shape) for item in normed]
+    pair_piece = column_piece([gate_weight, up_weight], parts)
+    shared = shared_pieces(plan, pair_piece, projected[1])
     rotated, attended, stats = attention_forward(projected, tables, order, slot_lengths)
     attended = flat(attended)
-    attended, o_found = after((attended, o_found), rotated)
+    attended, o_found, shared = after((attended, o_found, shared), rotated)
     o_w = place_columns(plan, o_found)
     opened = scatter_open(plan, attended, o_w, slots)
     hidden = source + scatter_close(plan, opened)
-    if plan.fast:
-        pair_core = core_pieces(plan, column_piece([late[1], late[2]], parts))
-        down_core = core_pieces(plan, row_piece(late[3], parts))
-    else:
-        pair_core = down_core = None
 
     inverse_two = lax.rsqrt(feature_total(hidden * hidden) / width + EPS)
     opened = gather_open(plan, (hidden * inverse_two * feedforward_gain).astype(BF))
-    pair_found, down_found = split_shared(plan, shared, pair_core, down_core)
-    pair_w = place_rows(plan, pair_found)
-    normed_two = flat(gather_close(plan, after(opened, pair_w)))
-    target_open = gather_open(plan, after(cotangent, normed_two[0]))
-    units = pair_w.shape[1] // 2
-    active_here, *slopes_here = forward_units(normed_two[0], pair_w)
-    normed_two = (normed_two[0], after(normed_two[1], active_here))
-    active_away, *slopes_away = forward_units(normed_two[1], pair_w)
+    pair_w = shared_close(plan, shared, pair_piece, hidden)
+    opened, pair_arrays = after((opened, [item for item, _ in pair_w]), hidden)
+    pair_w = [(item, index) for item, (_, index) in zip(pair_arrays, pair_w)]
+    normed_two = flat(gather_close(plan, opened))
+    down_found = exchange_pieces(plan, row_piece(after(down_weight, normed_two[0]), parts))
+    target_open = aside_open(plan, after(cotangent, normed_two[0]))
+    units = gate_weight.shape[1] // parts
+    masks = jnp.arange(parts, dtype=jnp.int32)
+    places = plan.ordered(plan.place ^ masks, parts)
+    active_here, *slopes_here = forward_units(places, normed_two[0], pair_w)
+    away, target_open = after((normed_two[1], target_open), active_here)
+    normed_two = (normed_two[0], away)
+    target_open = aside_turn(plan, target_open)
+    active_away, *slopes_away = forward_units(places, normed_two[1], pair_w)
     active = (active_here, active_away)
-    active, target_open = after((active, target_open), active_away)
-    down_w = place_columns(plan, down_found)
+    active, target_open, down_found[:3] = after((active, target_open, down_found[:3]), active_away)
     target_all = flat(gather_close(plan, target_open, [scaled(0), scaled(1)]))
+    target_all, down_found[3:] = after((target_all, down_found[3:]), active)
     down_sum = weight_gradient(plan, active, target_all, False)
     down_part = reduce_groups(down_sum)
 
     target = cotangent.astype(jnp.float32) * own_valid[:, :, None] * scale[:, None, None]
     target_away = after(target_all[1], down_sum)
-    grads_away, away = backward_units(target_away, slopes_away, down_w, pair_w)
+    grads_away, away = backward_units(places, target_away, slopes_away, pair_w, down_found)
     target_here = after(target_all[0], away)
-    grads_here, here = backward_units(target_here, slopes_here, down_w, pair_w)
+    grads_here, here = backward_units(places, target_here, slopes_here, pair_w, down_found)
     grad_pair = (grads_here, grads_away)
     opened = scatter_halves(plan, here, away, slots)
     grad_late = after(grad_pair, opened[-1])
     gate_sum = weight_gradient(plan, normed_two, grad_late, True, 0, 2)
-    up_sum = weight_gradient(plan, normed_two, grad_late, True, 1, 2)
     gate_part = reduce_groups(gate_sum)
-    up_part = reduce_groups(up_sum)
-    dn = scatter_close(plan, opened, (gate_sum, up_sum, down_part))
+    dn = scatter_close(plan, opened, (gate_sum, down_part))
     weighted = dn * feedforward_gain
     total_two = feature_total(weighted * hidden)
     grad_hidden = target + inverse_two * weighted - hidden * inverse_two**3 * total_two / width
     gain_two_sum = jnp.sum(dn * hidden * inverse_two, axis=(0, 1))
 
+    down_w = place_columns(plan, after(down_found, dn))
     result_open = scatter_open(plan, after(active, grad_hidden), down_w, slots)
-    opened = after(gather_open(plan, grad_hidden.astype(BF)), (result_open, gate_part))
+    up_sum = weight_gradient(plan, normed_two, after(grad_pair, grad_hidden), True, 1, 2)
+    up_part = reduce_groups(up_sum)
+    opened = after(gather_open(plan, grad_hidden.astype(BF)), (result_open, up_sum, gate_part))
     grad_hidden_all = flat(gather_close(plan, opened))
     result_open, down_part, gate_part = after((result_open, down_part, gate_part), grad_hidden_all)
     result_turned = scatter_turn(plan, result_open)
@@ -767,12 +819,11 @@
     sent = (result_turned, down_sent, gate_sent, output_sum)
     back, sent = after((flat(back), sent), back)
     result_turned, down_sent, gate_sent, output_sum = sent
-    output_part = reduce_groups(output_sum)
     opened = scatter_open(plan, back, qkv_w.T, slots)
     qkv_sum = weight_gradient(plan, normed, after(back, opened[-1]), True)
     result = hidden + scatter_end(plan, result_turned)
     outputs = jnp.where(own_valid[:, :, None], result, 0.0).astype(BF)
-    qkv_part = reduce_groups(qkv_sum)
+    output_part, qkv_part = reduce_both(plan, output_sum, qkv_sum)
     dm = scatter_close(plan, opened, (qkv_sum, up_part, outputs))
     up_part = after(up_part, dm)
     up_sent = send_rows(plan, up_part)

time: 689 us -> 671 us (0.974)
  local copies, waits for them, and re-layouts: 61.5 us -> 44.6 us
  waiting for transfers between devices: 214 us -> 202 us
    all_gather x1, waiting for transfers between devices: 23.7 us -> 3.59 us  [shared_close(): whole = lax.all_gather(shared, 'dp')]
    unnamed x163 -> x143, local copies, waits for them, and re-layouts: 23.2 us -> 12.4 us
    ppermute x84 -> x83, waiting for transfers between devices: 185 us -> 191 us  [swap(): return lax.ppermute(values, axis, [(i, i ^ mask) for i in range(size)])]
    another operation x19 -> x15, other arithmetic: 14.7 us -> 17.3 us  [gather_close(): here = finish[0](jnp.stack(rows).reshape(2, 2, *rows[0].shape))]
    ppermute x84 -> x83, starting transfers between devices: 75.2 us -> 73.2 us  [swap(): return lax.ppermute(values, axis, [(i, i ^ mask) for i in range(size)])]
  transfers between devices with their start and end apart: 90 -> 88, of which waited for: 34 -> 45; matrix products, arithmetic and copies ran while one was open for 23% -> 21% of each run, Pallas kernels for 26% -> 25%
where the time goes in v4:
time: 671 us; the launch traced here: 661 us
  waiting for transfers between devices  202 us (30%)
  Pallas kernels  179 us (27%)
  other arithmetic  105 us (16%)
  starting transfers between devices  73.5 us (11%)
  local copies, waits for them, and re-layouts  44.6 us (7%)
  matrix products  40.7 us (6%)
  between operations  16.1 us (2%)
    ppermute x83, waiting for transfers between devices, swap(): return lax.ppermute(values, axis, [(i, i ^ mask) for i in range(size)])  191 us
    pallas_call x4, Pallas kernels, row_blocks(): pl.pallas_call(kernel, grid_spec=pltpu.PrefetchScalarGridSpec(num_scalar_...  78.1 us
    ppermute x83, starting transfers between devices, swap(): return lax.ppermute(values, axis, [(i, i ^ mask) for i in range(size)])  73.2 us
    pallas_call x5, Pallas kernels, weight_gradient(): pl.pallas_call(gradient_kernel, grid_spec=pltpu.PrefetchScalarGridSpec(nu...  52 us
    pallas_call x2, Pallas kernels, attention_call(): pl.pallas_call(functools.partial(kernel, heads), grid_spec=pltpu.Prefetch...  49.3 us
    dot_general x10, matrix products, matmul(): return jnp.dot(left, right, preferred_element_type=jnp.float32)  40.7 us
    another operation x15, other arithmetic, gather_close(): here = finish[0](jnp.stack(rows).reshape(2, 2, *rows[0].shape))  17.3 us
  transfers between devices with their start and end apart: 88, of which 45 were waited for; matrix products, arithmetic and copies ran while one was open for 21% of the time, Pallas kernels for 25%

profile of v4, /device:TPU:0, one launch (start us, length us, event | category | flops | bytes accessed | tf_op | source)
XLA Modules:
  0.0 661.3 jit_solution(15126150235159807851)
XLA Ops:
  8.8 3.0 collective-permute-start
  28.7 6.6 collective-permute-done.1
  36.7 11.0 %collective-permute-done.5 = bf16[256,1024]{1,0:T(8,128)(2,1)} collective-permute-done((bf16[256,1024]{1,0:T(8,128)(2,1)}, bf16[256,1024]{1,0:T(8,128)(2,1)}, u32[]{:S(2)}, u32[]{:S(2)}) %collective-permute-start.5) | collective-permute-done | bytes 524320 | tf_op jit(solution)/shard_map/ppermute | solution.py:312
  52.6 6.3 collective-permute-done.2
  58.9 10.8 %collective-permute-done.3 = bf16[256,1024]{1,0:T(8,128)(2,1)S(1)} collective-permute-done((bf16[256,1024]{1,0:T(8,128)(2,1)}, bf16[256,1024]{1,0:T(8,128)(2,1)S(1)}, u32[]{:S(2)}, u32[]{:S(2)}) %collective-permute-start.3) | collective-permute-done | bytes 524320 | tf_op jit(solution)/shard_map/ppermute | solution.py:312
  75.7 4.2 constant_dynamic-slice_fusion.22
  83.1 4.5 fusion.14.projected_here
  87.6 5.7 fusion.12.projected_away
  98.2 19.2 %shard_map.212 = (bf16[2,2,256,384]{3,2,1,0:T(8,128)(2,1)S(1)}, bf16[2,2,256,384]{3,2,1,0:T(8,128)(2,1)S(1)}, bf16[2,2,256,256]{3,2,1,0:T(8,128)(2,1)S(1)}, bf16...) custom-call(s32[4]{0:T(128)S(1)} %fusion.61.order, s32[2]{0:T(128)S(1)} %dynamic_slice.157.lengths, ...), custom_call_target="tpu_custom_call" | custom-call | flops 5368709120 | bytes 16777216 | tf_op jit(solution)/shard_map/pallas_call | solution.py:215
  121.5 3.7 collective-permute-done.12
  125.1 4.3 collective-permute-done.13
  132.6 3.2 convolution_convert_fusion.2
  137.7 5.8 collective-permute-done.16
  149.0 21.7 %collective-permute-done.18 = bf16[2,256,1024]{2,1,0:T(8,128)(2,1)S(1)} collective-permute-done((bf16[2,256,1024]{2,1,0:T(8,128)(2,1)S(1)}, bf16[2,256,1024]{2,1,0:T(8,128)(2,1)S(1)}, u32[]{:S(2)}, u32[]{:S(2)}) %collective-permute-start.18) | collective-permute-done | bytes 1048608 | tf_op jit(solution)/shard_map/ppermute | solution.py:312
  179.1 8.5 %collective-permute-done.19 = bf16[256,1024]{1,0:T(8,128)(2,1)S(1)} collective-permute-done((bf16[256,1024]{1,0:T(8,128)(2,1)S(1)}, bf16[256,1024]{1,0:T(8,128)(2,1)S(1)}, u32[]{:S(2)}, u32[]{:S(2)}) %collective-permute-start.19) | collective-permute-done | bytes 524320 | tf_op jit(solution)/shard_map/ppermute | solution.py:312
  191.9 3.2 collective-permute-done.21
  199.6 10.8 %collective-permute-done.22 = bf16[256,1024]{1,0:T(8,128)(2,1)S(1)} collective-permute-done((bf16[256,1024]{1,0:T(8,128)(2,1)S(1)}, bf16[256,1024]{1,0:T(8,128)(2,1)S(1)}, u32[]{:S(2)}, u32[]{:S(2)}) %collective-permute-start.22) | collective-permute-done | bytes 524320 | tf_op jit(solution)/shard_map/ppermute | solution.py:312
  214.0 3.6 all-gather.3.cloned.1.call-done
  217.5 4.5 collective-permute-done.23
  222.0 9.7 %collective-permute-done.24 = bf16[256,1024]{1,0:T(8,128)(2,1)} collective-permute-done((bf16[256,1024]{1,0:T(8,128)(2,1)S(1)}, bf16[256,1024]{1,0:T(8,128)(2,1)}, u32[]{:S(2)}, u32[]{:S(2)}) %collective-permute-start.24) | collective-permute-done | bytes 524320 | tf_op jit(solution)/shard_map/ppermute | solution.py:312
  242.5 3.4 constant_dynamic-slice_fusion.17
  246.5 16.4 %shard_map.213 = (bf16[1024,1024]{1,0:T(8,128)(2,1)}, bf16[1024,1024]{1,0:T(8,128)(2,1)}, bf16[1024,1024]{1,0:T(8,128)(2,1)}) custom-call(s32[4]{0:T(128)} %fusion.62.places, bf16[1024,2048]{1,0:T(8,128)(2,1)} %bitcast.41.normed.left_here, bf16[512,2048]{1,0:T(8,128)(2,1)} %pad_maximum_fusion.5.refs_0_, bf16[512,2048]{1,0:T(8,128)(2,1)} %collective-permute-done.28.refs_1_, ...), custom_call_target="tpu_custom_call" | custom-call | flops 8589934592 | bytes 18874368 | tf_op jit(solution)/shard_map/pallas_call | solution.py:561
  265.8 16.4 %shard_map.214 = (bf16[1024,1024]{1,0:T(8,128)(2,1)}, bf16[1024,1024]{1,0:T(8,128)(2,1)}, bf16[1024,1024]{1,0:T(8,128)(2,1)}) custom-call(s32[4]{0:T(128)} %fusion.62.places, bf16[1024,2048]{1,0:T(8,128)(2,1)} %bitcast.43.normed.left_away, bf16[512,2048]{1,0:T(8,128)(2,1)} %pad_maximum_fusion.5.refs_0_, bf16[512,2048]{1,0:T(8,128)(2,1)} %collective-permute-done.28.refs_1_, ...), custom_call_target="tpu_custom_call" | custom-call | flops 8589934592 | bytes 18874368 | tf_op jit(solution)/shard_map/pallas_call | solution.py:561
  282.2 4.9 collective-permute-done.34.refs_6_
  302.7 4.8 copy.34
  307.5 12.7 %collective-permute-done.36.refs_7_ = bf16[1024,512]{1,0:T(8,128)(2,1)S(1)} collective-permute-done((bf16[1024,512]{1,0:T(8,128)(2,1)S(1)}, bf16[1024,512]{1,0:T(8,128)(2,1)S(1)}, u32[]{:S(2)}, u32[]{:S(2)}) %collective-permute-start.36) | collective-permute-done | bytes 1048608 | tf_op jit(solution)/shard_map/ppermute | solution.py:312
  321.2 14.5 %shard_map.215 = bf16[4,1024,512]{2,1,0:T(8,128)(2,1)} custom-call(s32[1]{0:T(128)} %bitcast.48.side, bf16[1024,1024]{1,0:T(8,128)(2,1)S(1)} %copy-done.8, bf16[1024,1024]{1,0:T(8,128)(2,1)S(1)} %copy-done.9, bf16[1024,2048]{1,0:T(8,128)(2,1)} %fusion.right_here.target, bf16[1024,2048]{1,0:T(8,128)(2,1)} %bitcast.288), custom_call_target="tpu_custom_call" | custom-call | flops 8589934592 | bytes 16777216 | tf_op jit(solution)/shard_map/pallas_call | solution.py:626
  335.7 22.4 %shard_map.216 = (bf16[1024,2048]{1,0:T(8,128)(2,1)}, bf16[1024,2048]{1,0:T(8,128)(2,1)}) custom-call(s32[4]{0:T(128)} %fusion.62.places, bf16[1024,2048]{1,0:T(8,128)(2,1)} %bitcast.289, bf16[1024,1024]{1,0:T(8,128)(2,1)} %get-tuple-element.260.slope_gate, bf16[1024,1024]{1,0:T(8,128)(2,1)} %get-tuple-element.261.slope_up, ...), custom_call_target="tpu_custom_call" | custom-call | flops 12884901888 | bytes 29360128 | tf_op jit(solution)/shard_map/pallas_call | solution.py:561
  358.5 22.8 %shard_map.217 = (bf16[1024,2048]{1,0:T(8,128)(2,1)}, bf16[1024,2048]{1,0:T(8,128)(2,1)}) custom-call(s32[4]{0:T(128)} %fusion.62.places, bf16[1024,2048]{1,0:T(8,128)(2,1)} %fusion.right_here.target, bf16[1024,1024]{1,0:T(8,128)(2,1)} %get-tuple-element.268.slope_gate, bf16[1024,1024]{1,0:T(8,128)(2,1)} %get-tuple-element.269.slope_up, ...), custom_call_target="tpu_custom_call" | custom-call | flops 12884901888 | bytes 29360128 | tf_op jit(solution)/shard_map/pallas_call | solution.py:561
  389.2 12.4 %shard_map.218 = bf16[4,512,1024]{2,1,0:T(8,128)(2,1)S(1)} custom-call(s32[1]{0:T(128)} %bitcast.48.side, bf16[1024,2048]{1,0:T(8,128)(2,1)} %bitcast.41.normed.left_here, bf16[1024,2048]{1,0:T(8,128)(2,1)} %bitcast.43.normed.left_away, bf16[1024,2048]{1,0:T(8,128)(2,1)} %get-tuple-element.289.right_here, bf16[1024,2048]{1,0:T(8,128)(2,1)} %get-tuple-element.290.right_away), custom_call_target="tpu_custom_call" | custom-call | flops 8589934592 | bytes 16777216 | tf_op jit(solution)/shard_map/pallas_call | solution.py:626
  403.7 6.1 collective-permute-done.38
  409.7 4.1 collective-permute-done.39
  422.9 6.4 collective-permute-done.40
  439.5 6.1 convolution_convert_fusion.4
  449.8 6.1 convolution_convert_fusion.5
  455.9 12.5 %shard_map.219 = bf16[4,512,1024]{2,1,0:T(8,128)(2,1)S(1)} custom-call(s32[1]{0:T(128)} %bitcast.48.side, bf16[1024,2048]{1,0:T(8,128)(2,1)} %bitcast.41.normed.left_here, bf16[1024,2048]{1,0:T(8,128)(2,1)} %bitcast.43.normed.left_away, bf16[1024,2048]{1,0:T(8,128)(2,1)} %get-tuple-element.289.right_here, bf16[1024,2048]{1,0:T(8,128)(2,1)} %get-tuple-element.290.right_away), custom_call_target="tpu_custom_call" | custom-call | flops 8589934592 | bytes 16777216 | tf_op jit(solution)/shard_map/pallas_call | solution.py:626
  479.0 4.8 collective-permute-done.45
  485.1 7.7 %reduce-scatter.7.cloned.1.call-done = bf16[1,512,1024]{2,1,0:T(8,128)(2,1)} async-done(((bf16[4,512,1024]{2,1,0:T(8,128)(2,1)}), bf16[1,512,1024]{2,1,0:T(8,128)(2,1)}) %reduce-scatter.7.cloned.1.call-update) | async-done | bytes 1048592 | tf_op jit(solution)/shard_map/reduce_scatter | solution.py:646
  500.7 3.6 convolution_convert_fusion.7
  509.1 3.5 convolution_convert_fusion.6
  512.7 5.6 shard_map.220
  523.4 30.1 %shard_map.221 = (bf16[2,2,256,384]{3,2,1,0:T(8,128)(2,1)S(1)}, bf16[2,2,256,384]{3,2,1,0:T(8,128)(2,1)S(1)}) custom-call(s32[4]{0:T(128)S(1)} %copy-done.7, s32[2]{0:T(128)S(1)} %dynamic_slice.157.lengths, bf16[2,2,256,384]{3,2,1,0:T(8,128)(2,1)S(1)} %copy-done.14, bf16[2,2,256,384]{3,2,1,0:T(8,128)(2,1)S(1)} %copy-done.16, ...), custom_call_target="tpu_custom_call" | custom-call | flops 13421772800 | bytes 16777216 | tf_op jit(solution)/shard_map/pallas_call | solution.py:215
  554.8 4.4 convolution_convert_fusion
  560.0 3.5 fusion.29
  570.8 3.0 fusion.23
  577.8 7.0 %shard_map.222 = bf16[4,512,384]{2,1,0:T(8,128)(2,1)S(1)} custom-call(s32[1]{0:T(128)} %bitcast.48.side, bf16[1024,2048]{1,0:T(8,128)(2,1)} %bitcast.95.left_here, bf16[1024,2048]{1,0:T(8,128)(2,1)} %bitcast.96.left_away, bf16[1024,384]{1,0:T(8,128)(2,1)S(1)} %bitcast.267, bf16[1024,384]{1,0:T(8,128)(2,1)S(1)} %bitcast.269), custom_call_target="tpu_custom_call" | custom-call | flops 3221225472 | bytes 11534336 | tf_op jit(solution)/shard_map/pallas_call | solution.py:626
  592.8 8.7 %collective-permute-done.62 = bf16[256,2048]{1,0:T(8,128)(2,1)} collective-permute-done((bf16[256,2048]{1,0:T(8,128)(2,1)}, bf16[256,2048]{1,0:T(8,128)(2,1)}, u32[]{:S(2)}, u32[]{:S(2)}) %collective-permute-start.62) | collective-permute-done | bytes 1048608 | tf_op jit(solution)/shard_map/ppermute | solution.py:312
  611.0 5.2 collective-permute-done.64
  (443 shorter events, 235.9 us)
Async XLA Ops:
  7.2 210.3 %all-gather.3.cloned.1.call-start = ((), (), s32[]{:S(2)}) async-start(), calls=%async_computation.8 | async-start | bytes 5242880 | tf_op jit(solution)/shard_map/all_gather | solution.py:448
  18.2 33.3 %collective-permute-start.9 = (bf16[512,384]{1,0:T(8,128)(2,1)}, bf16[512,384]{1,0:T(8,128)(2,1)}, u32[]{:S(2)}, u32[]{:S(2)}) collective-permute-start(bf16[512,384]{1,0:T(8,128)(2,1)} %pad_maximum_fusion.14), channel_id=1, source_target_pairs={{0,6},{2,4},{4,2},{6,0},{1,7},{3,5},{5,3},{7,1},{8,14},{10,12},{12... | collective-permute-start | bytes 1179656 | tf_op jit(solution)/shard_map/ppermute | solution.py:312
  20.7 27.1 %collective-permute-start.5 = (bf16[256,1024]{1,0:T(8,128)(2,1)}, bf16[256,1024]{1,0:T(8,128)(2,1)}, u32[]{:S(2)}, u32[]{:S(2)}) collective-permute-start(bf16[256,1024]{1,0:T(8,128)(2,1)} %get-tuple-element.196), channel_id=1, source_target_pairs={{0,4},{2,6},{4,0},{6,2},{1,5},{3,7},{5,1},{7,3},{8,12},{10,14},{12... | collective-permute-start | bytes 1572872 | tf_op jit(solution)/shard_map/ppermute | solution.py:312
  26.6 32.3 %collective-permute-start.2 = (bf16[256,1024]{1,0:T(8,128)(2,1)S(1)}, bf16[256,1024]{1,0:T(8,128)(2,1)S(1)}, u32[]{:S(2)}, u32[]{:S(2)}) collective-permute-start(bf16[256,1024]{1,0:T(8,128)(2,1)S(1)} %get-tuple-element.192), channel_id=1, source_target_pairs={{0,4},{2,6},{4,0},{6,2},{1,5},{3,7},{5,1},{7,3},{8,12},{10,14},{12... | collective-permute-start | bytes 1572872 | tf_op jit(solution)/shard_map/ppermute | solution.py:312
  28.1 30.8 %collective-permute-start.4 = (bf16[256,1024]{1,0:T(8,128)(2,1)}, bf16[256,1024]{1,0:T(8,128)(2,1)S(1)}, u32[]{:S(2)}, u32[]{:S(2)}) collective-permute-start(bf16[256,1024]{1,0:T(8,128)(2,1)} %get-tuple-element.196), channel_id=1, source_target_pairs={{0,1},{1,0},{2,3},{3,2},{4,5},{5,4},{6,7},{7,6},{8,9},{9,8},{10,11... | collective-permute-start | bytes 1572872 | tf_op jit(solution)/shard_map/ppermute | solution.py:312
  35.2 34.5 %collective-permute-start.3 = (bf16[256,1024]{1,0:T(8,128)(2,1)}, bf16[256,1024]{1,0:T(8,128)(2,1)S(1)}, u32[]{:S(2)}, u32[]{:S(2)}) collective-permute-start(bf16[256,1024]{1,0:T(8,128)(2,1)} %collective-permute-done.1), channel_id=1, source_target_pairs={{0,4},{2,6},{4,0},{6,2},{1,5},{3,7},{5,1},{7,3},{8,12},{10,14},{12... | collective-permute-start | bytes 1572872 | tf_op jit(solution)/shard_map/ppermute | solution.py:312
  47.8 22.0 %collective-permute-start.6 = (bf16[256,1024]{1,0:T(8,128)(2,1)}, bf16[256,1024]{1,0:T(8,128)(2,1)S(1)}, u32[]{:S(2)}, u32[]{:S(2)}) collective-permute-start(bf16[256,1024]{1,0:T(8,128)(2,1)} %collective-permute-done.5), channel_id=1, source_target_pairs={{0,1},{1,0},{2,3},{3,2},{4,5},{5,4},{6,7},{7,6},{8,9},{9,8},{10,11... | collective-permute-start | bytes 1572872 | tf_op jit(solution)/shard_map/ppermute | solution.py:312
  93.3 27.0 %collective-permute-start.15 = (bf16[128,2048]{1,0:T(8,128)(2,1)S(1)}, bf16[128,2048]{1,0:T(8,128)(2,1)S(1)}, u32[]{:S(2)}, u32[]{:S(2)}) collective-permute-start(bf16[128,2048]{1,0:T(8,128)(2,1)S(1)} %get-tuple-element.204), channel_id=1, source_target_pairs={{0,6},{2,4},{4,2},{6,0},{1,7},{3,5},{5,3},{7,1},{8,14},{10,12},{12... | collective-permute-start | bytes 1572872 | tf_op jit(solution)/shard_map/ppermute | solution.py:312
  94.9 25.4 %collective-permute-start.14 = (bf16[128,2048]{1,0:T(8,128)(2,1)S(1)}, bf16[128,2048]{1,0:T(8,128)(2,1)S(1)}, u32[]{:S(2)}, u32[]{:S(2)}) collective-permute-start(bf16[128,2048]{1,0:T(8,128)(2,1)S(1)} %get-tuple-element.203), channel_id=1, source_target_pairs={{0,4},{2,6},{4,0},{6,2},{1,5},{3,7},{5,1},{7,3},{8,12},{10,14},{12... | collective-permute-start | bytes 1572872 | tf_op jit(solution)/shard_map/ppermute | solution.py:312
  96.4 25.1 %collective-permute-start.11 = (bf16[256,512]{1,0:T(8,128)(2,1)}, bf16[256,512]{1,0:T(8,128)(2,1)}, u32[]{:S(2)}, u32[]{:S(2)}) collective-permute-start(bf16[256,512]{1,0:T(8,128)(2,1)} %get-tuple-element.424), channel_id=1, source_target_pairs={{0,2},{2,0},{4,6},{6,4},{1,3},{3,1},{5,7},{7,5},{8,10},{10,8},{12,... | collective-permute-start | bytes 786440 | tf_op jit(solution)/shard_map/ppermute | solution.py:312
  96.4 28.8 %collective-permute-start.12 = (bf16[256,512]{1,0:T(8,128)(2,1)}, bf16[256,512]{1,0:T(8,128)(2,1)}, u32[]{:S(2)}, u32[]{:S(2)}) collective-permute-start(bf16[256,512]{1,0:T(8,128)(2,1)} %get-tuple-element.423), channel_id=1, source_target_pairs={{0,4},{2,6},{4,0},{6,2},{1,5},{3,7},{5,1},{7,3},{8,12},{10,14},{12... | collective-permute-start | bytes 786440 | tf_op jit(solution)/shard_map/ppermute | solution.py:312
  97.9 31.6 %collective-permute-start.13 = (bf16[256,512]{1,0:T(8,128)(2,1)}, bf16[256,512]{1,0:T(8,128)(2,1)}, u32[]{:S(2)}, u32[]{:S(2)}) collective-permute-start(bf16[256,512]{1,0:T(8,128)(2,1)} %get-tuple-element.422), channel_id=1, source_target_pairs={{0,6},{2,4},{4,2},{6,0},{1,7},{3,5},{5,3},{7,1},{8,14},{10,12},{12... | collective-permute-start | bytes 786440 | tf_op jit(solution)/shard_map/ppermute | solution.py:312
  136.3 277.5 %reduce-scatter.5.cloned.1.call-start = ((), (), s32[]{:S(2)}) async-start(), calls=%async_computation.4 | async-start | bytes 5242880 | tf_op jit(solution)/shard_map/reduce_scatter | solution.py:646
  145.2 25.5 %collective-permute-start.18 = (bf16[2,256,1024]{2,1,0:T(8,128)(2,1)S(1)}, bf16[2,256,1024]{2,1,0:T(8,128)(2,1)S(1)}, u32[]{:S(2)}, u32[]{:S(2)}) collective-permute-start(bf16[2,256,1024]{2,1,0:T(8,128)(2,1)S(1)} %fusion.17), channel_id=1, source_target_pairs={{0,1},{1,0},{2,3},{3,2},{4,5},{5,4},{6,7},{7,6},{8,9},{9,8},{10,11... | collective-permute-start | bytes 3145736 | tf_op jit(solution)/shard_map/ppermute | solution.py:312
  147.3 25.2 %collective-permute-start.17 = (bf16[256,2048]{1,0:T(8,128)(2,1)S(1)}, bf16[256,2048]{1,0:T(8,128)(2,1)S(1)}, u32[]{:S(2)}, u32[]{:S(2)}) collective-permute-start(bf16[256,2048]{1,0:T(8,128)(2,1)S(1)} %fusion.16), channel_id=1, source_target_pairs={{0,4},{2,6},{4,0},{6,2},{1,5},{3,7},{5,1},{7,3},{8,12},{10,14},{12... | collective-permute-start | bytes 3145736 | tf_op jit(solution)/shard_map/ppermute | solution.py:312
  191.4 40.4 %collective-permute-start.28 = (bf16[512,2048]{1,0:T(8,128)(2,1)}, bf16[512,2048]{1,0:T(8,128)(2,1)}, u32[]{:S(2)}, u32[]{:S(2)}) collective-permute-start(bf16[512,2048]{1,0:T(8,128)(2,1)} %pad_maximum_fusion.6), channel_id=1, source_target_pairs={{0,2},{2,0},{4,6},{6,4},{1,3},{3,1},{5,7},{7,5},{8,10},{10,8},{12,... | collective-permute-start | bytes 6291464 | tf_op jit(solution)/shard_map/ppermute | solution.py:312
  195.9 16.0 %collective-permute-start.26 = (bf16[256,1024]{1,0:T(8,128)(2,1)S(1)}, bf16[256,1024]{1,0:T(8,128)(2,1)S(1)}, u32[]{:S(2)}, u32[]{:S(2)}) collective-permute-start(bf16[256,1024]{1,0:T(8,128)(2,1)S(1)} %get-tuple-element.231), channel_id=1, source_target_pairs={{0,4},{2,6},{4,0},{6,2},{1,5},{3,7},{5,1},{7,3},{8,12},{10,14},{12... | collective-permute-start | bytes 1572872 | tf_op jit(solution)/shard_map/ppermute | solution.py:312
  197.5 24.5 %collective-permute-start.23 = (bf16[256,1024]{1,0:T(8,128)(2,1)S(1)}, bf16[256,1024]{1,0:T(8,128)(2,1)S(1)}, u32[]{:S(2)}, u32[]{:S(2)}) collective-permute-start(bf16[256,1024]{1,0:T(8,128)(2,1)S(1)} %get-tuple-element.227), channel_id=1, source_target_pairs={{0,4},{2,6},{4,0},{6,2},{1,5},{3,7},{5,1},{7,3},{8,12},{10,14},{12... | collective-permute-start | bytes 1572872 | tf_op jit(solution)/shard_map/ppermute | solution.py:312
  197.9 24.1 %collective-permute-start.25 = (bf16[256,1024]{1,0:T(8,128)(2,1)S(1)}, bf16[256,1024]{1,0:T(8,128)(2,1)S(1)}, u32[]{:S(2)}, u32[]{:S(2)}) collective-permute-start(bf16[256,1024]{1,0:T(8,128)(2,1)S(1)} %get-tuple-element.231), channel_id=1, source_target_pairs={{0,1},{1,0},{2,3},{3,2},{4,5},{5,4},{6,7},{7,6},{8,9},{9,8},{10,11... | collective-permute-start | bytes 1572872 | tf_op jit(solution)/shard_map/ppermute | solution.py:312
  210.4 21.3 %collective-permute-start.24 = (bf16[256,1024]{1,0:T(8,128)(2,1)S(1)}, bf16[256,1024]{1,0:T(8,128)(2,1)}, u32[]{:S(2)}, u32[]{:S(2)}) collective-permute-start(bf16[256,1024]{1,0:T(8,128)(2,1)S(1)} %collective-permute-done.22), channel_id=1, source_target_pairs={{0,4},{2,6},{4,0},{6,2},{1,5},{3,7},{5,1},{7,3},{8,12},{10,14},{12... | collective-permute-start | bytes 1572872 | tf_op jit(solution)/shard_map/ppermute | solution.py:312
  211.9 19.9 %collective-permute-start.27 = (bf16[256,1024]{1,0:T(8,128)(2,1)S(1)}, bf16[256,1024]{1,0:T(8,128)(2,1)}, u32[]{:S(2)}, u32[]{:S(2)}) collective-permute-start(bf16[256,1024]{1,0:T(8,128)(2,1)S(1)} %collective-permute-done.26), channel_id=1, source_target_pairs={{0,1},{1,0},{2,3},{3,2},{4,5},{5,4},{6,7},{7,6},{8,9},{9,8},{10,11... | collective-permute-start | bytes 1572872 | tf_op jit(solution)/shard_map/ppermute | solution.py:312
  236.7 28.6 %collective-permute-start.29 = (bf16[2,2,256,2048]{3,2,1,0:T(8,128)(2,1)}, bf16[2,2,256,2048]{3,2,1,0:T(8,128)(2,1)}, u32[]{:S(2)}, u32[]{:S(2)}) collective-permute-start(bf16[2,2,256,2048]{3,2,1,0:T(8,128)(2,1)} %bitcast.42), channel_id=1, source_target_pairs={{0,2},{2,0},{4,6},{6,4},{1,3},{3,1},{5,7},{7,5},{8,10},{10,8},{12,... | collective-permute-start | bytes 12582920 | tf_op jit(solution)/shard_map/ppermute | solution.py:312
  237.5 25.7 %collective-permute-start.30 = (bf16[2,256,1024]{2,1,0:T(8,128)(2,1)S(1)}, bf16[2,256,1024]{2,1,0:T(8,128)(2,1)}, u32[]{:S(2)}, u32[]{:S(2)}) collective-permute-start(bf16[2,256,1024]{2,1,0:T(8,128)(2,1)S(1)} %copy-done.33), channel_id=1, source_target_pairs={{0,1},{1,0},{2,3},{3,2},{4,5},{5,4},{6,7},{7,6},{8,9},{9,8},{10,11... | collective-permute-start | bytes 3145736 | tf_op jit(solution)/shard_map/ppermute | solution.py:312
  239.2 26.1 %collective-permute-start.31 = (bf16[2,256,1024]{2,1,0:T(8,128)(2,1)S(1)}, bf16[2,256,1024]{2,1,0:T(8,128)(2,1)}, u32[]{:S(2)}, u32[]{:S(2)}) collective-permute-start(bf16[2,256,1024]{2,1,0:T(8,128)(2,1)S(1)} %copy-done.33), channel_id=1, source_target_pairs={{0,4},{2,6},{4,0},{6,2},{1,5},{3,7},{5,1},{7,3},{8,12},{10,14},{12... | collective-permute-start | bytes 3145736 | tf_op jit(solution)/shard_map/ppermute | solution.py:312
  245.9 36.3 %collective-permute-start.33 = (bf16[1024,512]{1,0:T(8,128)(2,1)S(1)}, bf16[1024,512]{1,0:T(8,128)(2,1)S(1)}, u32[]{:S(2)}, u32[]{:S(2)}) collective-permute-start(bf16[1024,512]{1,0:T(8,128)(2,1)S(1)} %get-tuple-element.383), channel_id=1, source_target_pairs={{0,2},{2,0},{4,6},{6,4},{1,3},{3,1},{5,7},{7,5},{8,10},{10,8},{12,... | collective-permute-start | bytes 3145736 | tf_op jit(solution)/shard_map/ppermute | solution.py:312
  245.9 41.1 %collective-permute-start.34 = (bf16[1024,512]{1,0:T(8,128)(2,1)S(1)}, bf16[1024,512]{1,0:T(8,128)(2,1)}, u32[]{:S(2)}, u32[]{:S(2)}) collective-permute-start(bf16[1024,512]{1,0:T(8,128)(2,1)S(1)} %get-tuple-element.382), channel_id=1, source_target_pairs={{0,4},{2,6},{4,0},{6,2},{1,5},{3,7},{5,1},{7,3},{8,12},{10,14},{12... | collective-permute-start | bytes 3145736 | tf_op jit(solution)/shard_map/ppermute | solution.py:312
  265.3 24.1 %collective-permute-start.32 = (bf16[2,256,1024]{2,1,0:T(8,128)(2,1)}, bf16[2,256,1024]{2,1,0:T(8,128)(2,1)}, u32[]{:S(2)}, u32[]{:S(2)}) collective-permute-start(bf16[2,256,1024]{2,1,0:T(8,128)(2,1)} %collective-permute-done.31), channel_id=1, source_target_pairs={{0,1},{1,0},{2,3},{3,2},{4,5},{5,4},{6,7},{7,6},{8,9},{9,8},{10,11... | collective-permute-start | bytes 3145736 | tf_op jit(solution)/shard_map/ppermute | solution.py:312
  295.2 25.0 %collective-permute-start.36 = (bf16[1024,512]{1,0:T(8,128)(2,1)S(1)}, bf16[1024,512]{1,0:T(8,128)(2,1)S(1)}, u32[]{:S(2)}, u32[]{:S(2)}) collective-permute-start(bf16[1024,512]{1,0:T(8,128)(2,1)S(1)} %get-tuple-element.381), channel_id=1, source_target_pairs={{0,6},{2,4},{4,2},{6,0},{1,7},{3,5},{5,3},{7,1},{8,14},{10,12},{12... | collective-permute-start | bytes 3145736 | tf_op jit(solution)/shard_map/ppermute | solution.py:312
  335.7 157.1 %reduce-scatter.7.cloned.1.call-start = ((), (), s32[]{:S(2)}) async-start(), calls=%async_computation.5 | async-start | bytes 5242880 | tf_op jit(solution)/shard_map/reduce_scatter | solution.py:646
  358.1 23.3 %collective-permute-start.37 = (bf16[2,2,256,2048]{3,2,1,0:T(8,128)(2,1)}, bf16[2,2,256,2048]{3,2,1,0:T(8,128)(2,1)}, u32[]{:S(2)}, u32[]{:S(2)}) collective-permute-start(bf16[2,2,256,2048]{3,2,1,0:T(8,128)(2,1)} %bitcast.317), channel_id=1, source_target_pairs={{0,2},{2,0},{4,6},{6,4},{1,3},{3,1},{5,7},{7,5},{8,10},{10,8},{12,... | collective-permute-start | bytes 12582920 | tf_op jit(solution)/shard_map/ppermute | solution.py:312
  384.3 25.5 %collective-permute-start.38 = (bf16[256,2048]{1,0:T(8,128)(2,1)}, bf16[256,2048]{1,0:T(8,128)(2,1)}, u32[]{:S(2)}, u32[]{:S(2)}) collective-permute-start(bf16[256,2048]{1,0:T(8,128)(2,1)} %fusion.18), channel_id=1, source_target_pairs={{0,4},{2,6},{4,0},{6,2},{1,5},{3,7},{5,1},{7,3},{8,12},{10,14},{12... | collective-permute-start | bytes 3145736 | tf_op jit(solution)/shard_map/ppermute | solution.py:312
  388.6 25.2 %collective-permute-start.39 = (bf16[2,256,1024]{2,1,0:T(8,128)(2,1)}, bf16[2,256,1024]{2,1,0:T(8,128)(2,1)}, u32[]{:S(2)}, u32[]{:S(2)}) collective-permute-start(bf16[2,256,1024]{2,1,0:T(8,128)(2,1)} %fusion.19), channel_id=1, source_target_pairs={{0,1},{1,0},{2,3},{3,2},{4,5},{5,4},{6,7},{7,6},{8,9},{9,8},{10,11... | collective-permute-start | bytes 3145736 | tf_op jit(solution)/shard_map/ppermute | solution.py:312
  403.6 189.2 %reduce-scatter.9.cloned.1.call-start = ((), (), s32[]{:S(2)}) async-start(), calls=%async_computation.6 | async-start | bytes 5242880 | tf_op jit(solution)/shard_map/reduce_scatter | solution.py:646
  445.6 27.6 %collective-permute-start.49 = (bf16[2,2,256,2048]{3,2,1,0:T(8,128)(2,1)}, bf16[2,2,256,2048]{3,2,1,0:T(8,128)(2,1)}, u32[]{:S(2)}, u32[]{:S(2)}) collective-permute-start(bf16[2,2,256,2048]{3,2,1,0:T(8,128)(2,1)} %bitcast.68), channel_id=1, source_target_pairs={{0,2},{2,0},{4,6},{6,4},{1,3},{3,1},{5,7},{7,5},{8,10},{10,8},{12,... | collective-permute-start | bytes 12582920 | tf_op jit(solution)/shard_map/ppermute | solution.py:312
  445.7 24.7 %collective-permute-start.43 = (bf16[256,1024]{1,0:T(8,128)(2,1)S(1)}, bf16[256,1024]{1,0:T(8,128)(2,1)}, u32[]{:S(2)}, u32[]{:S(2)}) collective-permute-start(bf16[256,1024]{1,0:T(8,128)(2,1)S(1)} %get-tuple-element.299), channel_id=1, source_target_pairs={{0,1},{1,0},{2,3},{3,2},{4,5},{5,4},{6,7},{7,6},{8,9},{9,8},{10,11... | collective-permute-start | bytes 1572872 | tf_op jit(solution)/shard_map/ppermute | solution.py:312
  446.2 32.8 %collective-permute-start.44 = (bf16[256,1024]{1,0:T(8,128)(2,1)S(1)}, bf16[256,1024]{1,0:T(8,128)(2,1)}, u32[]{:S(2)}, u32[]{:S(2)}) collective-permute-start(bf16[256,1024]{1,0:T(8,128)(2,1)S(1)} %get-tuple-element.299), channel_id=1, source_target_pairs={{0,4},{2,6},{4,0},{6,2},{1,5},{3,7},{5,1},{7,3},{8,12},{10,14},{12... | collective-permute-start | bytes 1572872 | tf_op jit(solution)/shard_map/ppermute | solution.py:312
  447.7 31.3 %collective-permute-start.46 = (bf16[256,1024]{1,0:T(8,128)(2,1)S(1)}, bf16[256,1024]{1,0:T(8,128)(2,1)}, u32[]{:S(2)}, u32[]{:S(2)}) collective-permute-start(bf16[256,1024]{1,0:T(8,128)(2,1)S(1)} %get-tuple-element.303), channel_id=1, source_target_pairs={{0,1},{1,0},{2,3},{3,2},{4,5},{5,4},{6,7},{7,6},{8,9},{9,8},{10,11... | collective-permute-start | bytes 1572872 | tf_op jit(solution)/shard_map/ppermute | solution.py:312
  449.3 22.6 %collective-permute-start.47 = (bf16[256,1024]{1,0:T(8,128)(2,1)S(1)}, bf16[256,1024]{1,0:T(8,128)(2,1)}, u32[]{:S(2)}, u32[]{:S(2)}) collective-permute-start(bf16[256,1024]{1,0:T(8,128)(2,1)S(1)} %get-tuple-element.303), channel_id=1, source_target_pairs={{0,4},{2,6},{4,0},{6,2},{1,5},{3,7},{5,1},{7,3},{8,12},{10,14},{12... | collective-permute-start | bytes 1572872 | tf_op jit(solution)/shard_map/ppermute | solution.py:312
  499.5 140.0 %reduce-scatter.11.cloned.1.call-start = ((), (), s32[]{:S(2)}) async-start(), calls=%async_computation.7 | async-start | bytes 3276800 | tf_op jit(solution)/shard_map/reduce_scatter | solution.py:646
  518.4 36.4 %collective-permute-start.51 = (bf16[256,2048]{1,0:T(8,128)(2,1)}, bf16[256,2048]{1,0:T(8,128)(2,1)S(1)}, u32[]{:S(2)}, u32[]{:S(2)}) collective-permute-start(bf16[256,2048]{1,0:T(8,128)(2,1)} %fusion.20), channel_id=1, source_target_pairs={{0,4},{2,6},{4,0},{6,2},{1,5},{3,7},{5,1},{7,3},{8,12},{10,14},{12... | collective-permute-start | bytes 3145736 | tf_op jit(solution)/shard_map/ppermute | solution.py:312
  519.8 34.9 %collective-permute-start.52 = (bf16[2,256,1024]{2,1,0:T(8,128)(2,1)}, bf16[2,256,1024]{2,1,0:T(8,128)(2,1)S(1)}, u32[]{:S(2)}, u32[]{:S(2)}) collective-permute-start(bf16[2,256,1024]{2,1,0:T(8,128)(2,1)} %fusion.21), channel_id=1, source_target_pairs={{0,1},{1,0},{2,3},{3,2},{4,5},{5,4},{6,7},{7,6},{8,9},{9,8},{10,11... | collective-permute-start | bytes 3145736 | tf_op jit(solution)/shard_map/ppermute | solution.py:312
  521.4 32.1 %collective-permute-start.56 = (bf16[128,1024]{1,0:T(8,128)(2,1)S(1)}, bf16[128,1024]{1,0:T(8,128)(2,1)S(1)}, u32[]{:S(2)}, u32[]{:S(2)}) collective-permute-start(bf16[128,1024]{1,0:T(8,128)(2,1)S(1)} %get-tuple-element.412), channel_id=1, source_target_pairs={{0,2},{2,0},{4,6},{6,4},{1,3},{3,1},{5,7},{7,5},{8,10},{10,8},{12,... | collective-permute-start | bytes 786440 | tf_op jit(solution)/shard_map/ppermute | solution.py:312
  521.5 32.0 %collective-permute-start.57 = (bf16[128,1024]{1,0:T(8,128)(2,1)S(1)}, bf16[128,1024]{1,0:T(8,128)(2,1)S(1)}, u32[]{:S(2)}, u32[]{:S(2)}) collective-permute-start(bf16[128,1024]{1,0:T(8,128)(2,1)S(1)} %get-tuple-element.411), channel_id=1, source_target_pairs={{0,4},{2,6},{4,0},{6,2},{1,5},{3,7},{5,1},{7,3},{8,12},{10,14},{12... | collective-permute-start | bytes 786440 | tf_op jit(solution)/shard_map/ppermute | solution.py:312
  522.2 32.5 %collective-permute-start.58 = (bf16[128,1024]{1,0:T(8,128)(2,1)S(1)}, bf16[128,1024]{1,0:T(8,128)(2,1)S(1)}, u32[]{:S(2)}, u32[]{:S(2)}) collective-permute-start(bf16[128,1024]{1,0:T(8,128)(2,1)S(1)} %get-tuple-element.410), channel_id=1, source_target_pairs={{0,6},{2,4},{4,2},{6,0},{1,7},{3,5},{5,3},{7,1},{8,14},{10,12},{12... | collective-permute-start | bytes 786440 | tf_op jit(solution)/shard_map/ppermute | solution.py:312
  563.5 25.2 %collective-permute-start.59 = (bf16[256,1024]{1,0:T(8,128)(2,1)}, bf16[256,1024]{1,0:T(8,128)(2,1)}, u32[]{:S(2)}, u32[]{:S(2)}) collective-permute-start(bf16[256,1024]{1,0:T(8,128)(2,1)} %get-tuple-element.322), channel_id=1, source_target_pairs={{0,1},{1,0},{2,3},{3,2},{4,5},{5,4},{6,7},{7,6},{8,9},{9,8},{10,11... | collective-permute-start | bytes 1572872 | tf_op jit(solution)/shard_map/ppermute | solution.py:312
  565.1 23.7 %collective-permute-start.60 = (bf16[256,1024]{1,0:T(8,128)(2,1)}, bf16[256,1024]{1,0:T(8,128)(2,1)}, u32[]{:S(2)}, u32[]{:S(2)}) collective-permute-start(bf16[256,1024]{1,0:T(8,128)(2,1)} %get-tuple-element.323), channel_id=1, source_target_pairs={{0,4},{2,6},{4,0},{6,2},{1,5},{3,7},{5,1},{7,3},{8,12},{10,14},{12... | collective-permute-start | bytes 1572872 | tf_op jit(solution)/shard_map/ppermute | solution.py:312
  573.8 27.7 %collective-permute-start.63 = (bf16[2,256,1024]{2,1,0:T(8,128)(2,1)}, bf16[2,256,1024]{2,1,0:T(8,128)(2,1)}, u32[]{:S(2)}, u32[]{:S(2)}) collective-permute-start(bf16[2,256,1024]{2,1,0:T(8,128)(2,1)} %fusion.23), channel_id=1, source_target_pairs={{0,1},{1,0},{2,3},{3,2},{4,5},{5,4},{6,7},{7,6},{8,9},{9,8},{10,11... | collective-permute-start | bytes 3145736 | tf_op jit(solution)/shard_map/ppermute | solution.py:312
  576.9 24.6 %collective-permute-start.62 = (bf16[256,2048]{1,0:T(8,128)(2,1)}, bf16[256,2048]{1,0:T(8,128)(2,1)}, u32[]{:S(2)}, u32[]{:S(2)}) collective-permute-start(bf16[256,2048]{1,0:T(8,128)(2,1)} %fusion.22), channel_id=1, source_target_pairs={{0,4},{2,6},{4,0},{6,2},{1,5},{3,7},{5,1},{7,3},{8,12},{10,14},{12... | collective-permute-start | bytes 3145736 | tf_op jit(solution)/shard_map/ppermute | solution.py:312
  (111 other events, 882.2 us)
Sparse Core Ops, SparseCore 0:
  136.4 81.0 all-gather.2
  335.8 77.2 reduce-scatter.4
  415.5 77.2 reduce-scatter.6
  499.6 77.3 reduce-scatter.8
  586.7 52.8 reduce-scatter.10

commit v5 on v4

--- a/solution.py
+++ b/solution.py
@@ -430,16 +430,13 @@
     return found
 
 
-def shared_pieces(plan, piece, anchor):
+def shared_pieces(plan, weights, anchor):
     if not plan.fast:
-        return exchange_pieces(plan, piece)
-    got = []
-    for mask in (2, 3):
-        mine = piece(plan.place ^ mask)
-        size = mine.shape[0] // plan.groups
-        mine = lax.dynamic_slice_in_dim(mine, plan.group * size, size, 0)
-        got.append(swap(after(mine, anchor), "ctx", mask))
-    return jnp.stack(got)
+        return exchange_pieces(plan, column_piece(weights, plan.parts))
+    size = weights[0].shape[0] // plan.groups
+    lines = [lax.dynamic_slice_in_dim(w, plan.group * size, size, 0) for w in weights]
+    piece = column_piece(lines, plan.parts)
+    return jnp.stack([swap(after(piece(plan.place ^ m), anchor), "ctx", m) for m in (2, 3)])
 
 
 def shared_close(plan, shared, piece, anchor):
@@ -754,7 +751,7 @@
     half_shape = (slots, parts // 2, rows, -1)
     projected = [matmul(item, qkv_w).reshape(half_shape) for item in normed]
     pair_piece = column_piece([gate_weight, up_weight], parts)
-    shared = shared_pieces(plan, pair_piece, projected[1])
+    shared = shared_pieces(plan, [gate_weight, up_weight], projected[1])
     rotated, attended, stats = attention_forward(projected, tables, order, slot_lengths)
     attended = flat(attended)
     attended, o_found, shared = after((attended, o_found, shared), rotated)

time: 671 us -> 666 us (level)
  no operation moved by 1% of the time
where the time goes in v5:
time: 666 us; the launch traced here: 659 us
  waiting for transfers between devices  201 us (30%)
  Pallas kernels  179 us (27%)
  other arithmetic  107 us (16%)
  starting transfers between devices  73.2 us (11%)
  local copies, waits for them, and re-layouts  41.9 us (6%)
  matrix products  40.8 us (6%)
  between operations  16.1 us (2%)
    ppermute x83, waiting for transfers between devices, swap(): return lax.ppermute(values, axis, [(i, i ^ mask) for i in range(size)])  191 us
    pallas_call x4, Pallas kernels, row_blocks(): pl.pallas_call(kernel, grid_spec=pltpu.PrefetchScalarGridSpec(num_scalar_...  77.9 us
    ppermute x83, starting transfers between devices, swap(): return lax.ppermute(values, axis, [(i, i ^ mask) for i in range(size)])  73 us
    pallas_call x5, Pallas kernels, weight_gradient(): pl.pallas_call(gradient_kernel, grid_spec=pltpu.PrefetchScalarGridSpec(nu...  52 us
    pallas_call x2, Pallas kernels, attention_call(): pl.pallas_call(functools.partial(kernel, heads), grid_spec=pltpu.Prefetch...  49 us
    dot_general x10, matrix products, matmul(): return jnp.dot(left, right, preferred_element_type=jnp.float32)  40.8 us
    another operation x15, other arithmetic, gather_close(): here = finish[0](jnp.stack(rows).reshape(2, 2, *rows[0].shape))  17.7 us
  transfers between devices with their start and end apart: 88, of which 45 were waited for; matrix products, arithmetic and copies ran while one was open for 21% of the time, Pallas kernels for 25%

profile of v5, /device:TPU:0, one launch (start us, length us, event | category | flops | bytes accessed | tf_op | source)
XLA Modules:
  0.0 658.8 jit_solution(11781275060114370857)
XLA Ops:
  8.8 3.0 collective-permute-start
  28.7 6.6 collective-permute-done.1
  36.7 11.0 %collective-permute-done.5 = bf16[256,1024]{1,0:T(8,128)(2,1)} collective-permute-done((bf16[256,1024]{1,0:T(8,128)(2,1)}, bf16[256,1024]{1,0:T(8,128)(2,1)}, u32[]{:S(2)}, u32[]{:S(2)}) %collective-permute-start.5) | collective-permute-done | bytes 524320 | tf_op jit(solution)/shard_map/ppermute | solution.py:312
  52.6 6.3 collective-permute-done.2
  58.9 10.8 %collective-permute-done.3 = bf16[256,1024]{1,0:T(8,128)(2,1)S(1)} collective-permute-done((bf16[256,1024]{1,0:T(8,128)(2,1)}, bf16[256,1024]{1,0:T(8,128)(2,1)S(1)}, u32[]{:S(2)}, u32[]{:S(2)}) %collective-permute-start.3) | collective-permute-done | bytes 524320 | tf_op jit(solution)/shard_map/ppermute | solution.py:312
  77.8 4.5 fusion.14.projected_here
  83.2 5.7 fusion.12.projected_away
  93.4 19.1 %shard_map.212 = (bf16[2,2,256,384]{3,2,1,0:T(8,128)(2,1)S(1)}, bf16[2,2,256,384]{3,2,1,0:T(8,128)(2,1)S(1)}, bf16[2,2,256,256]{3,2,1,0:T(8,128)(2,1)S(1)}, bf16...) custom-call(s32[4]{0:T(128)S(1)} %fusion.59.order, s32[2]{0:T(128)S(1)} %dynamic_slice.153.lengths, ...), custom_call_target="tpu_custom_call" | custom-call | flops 5368709120 | bytes 16777216 | tf_op jit(solution)/shard_map/pallas_call | solution.py:215
  116.5 3.9 collective-permute-done.12
  120.3 5.0 collective-permute-done.13
  128.4 3.4 convolution_convert_fusion.2
  133.3 6.0 collective-permute-done.16
  144.9 21.4 %collective-permute-done.18 = bf16[2,256,1024]{2,1,0:T(8,128)(2,1)S(1)} collective-permute-done((bf16[2,256,1024]{2,1,0:T(8,128)(2,1)S(1)}, bf16[2,256,1024]{2,1,0:T(8,128)(2,1)S(1)}, u32[]{:S(2)}, u32[]{:S(2)}) %collective-permute-start.18) | collective-permute-done | bytes 1048608 | tf_op jit(solution)/shard_map/ppermute | solution.py:312
  178.3 5.7 collective-permute-done.19
  189.0 3.3 collective-permute-done.21
  196.7 10.8 %collective-permute-done.22 = bf16[256,1024]{1,0:T(8,128)(2,1)S(1)} collective-permute-done((bf16[256,1024]{1,0:T(8,128)(2,1)S(1)}, bf16[256,1024]{1,0:T(8,128)(2,1)S(1)}, u32[]{:S(2)}, u32[]{:S(2)}) %collective-permute-start.22) | collective-permute-done | bytes 524320 | tf_op jit(solution)/shard_map/ppermute | solution.py:312
  213.2 5.9 collective-permute-done.23
  219.1 9.8 %collective-permute-done.24 = bf16[256,1024]{1,0:T(8,128)(2,1)} collective-permute-done((bf16[256,1024]{1,0:T(8,128)(2,1)S(1)}, bf16[256,1024]{1,0:T(8,128)(2,1)}, u32[]{:S(2)}, u32[]{:S(2)}) %collective-permute-start.24) | collective-permute-done | bytes 524320 | tf_op jit(solution)/shard_map/ppermute | solution.py:312
  239.9 3.4 constant_dynamic-slice_fusion.17
  243.9 16.4 %shard_map.213 = (bf16[1024,1024]{1,0:T(8,128)(2,1)}, bf16[1024,1024]{1,0:T(8,128)(2,1)}, bf16[1024,1024]{1,0:T(8,128)(2,1)}) custom-call(s32[4]{0:T(128)} %fusion.60.places, bf16[1024,2048]{1,0:T(8,128)(2,1)} %bitcast.41.normed.left_here, bf16[512,2048]{1,0:T(8,128)(2,1)} %pad_maximum_fusion.5.refs_0_, bf16[512,2048]{1,0:T(8,128)(2,1)} %collective-permute-done.28.refs_1_, ...), custom_call_target="tpu_custom_call" | custom-call | flops 8589934592 | bytes 18874368 | tf_op jit(solution)/shard_map/pallas_call | solution.py:558
  263.2 16.5 %shard_map.214 = (bf16[1024,1024]{1,0:T(8,128)(2,1)}, bf16[1024,1024]{1,0:T(8,128)(2,1)}, bf16[1024,1024]{1,0:T(8,128)(2,1)}) custom-call(s32[4]{0:T(128)} %fusion.60.places, bf16[1024,2048]{1,0:T(8,128)(2,1)} %bitcast.43.normed.left_away, bf16[512,2048]{1,0:T(8,128)(2,1)} %pad_maximum_fusion.5.refs_0_, bf16[512,2048]{1,0:T(8,128)(2,1)} %collective-permute-done.28.refs_1_, ...), custom_call_target="tpu_custom_call" | custom-call | flops 8589934592 | bytes 18874368 | tf_op jit(solution)/shard_map/pallas_call | solution.py:558
  279.7 4.8 collective-permute-done.34.refs_6_
  300.1 4.8 copy.34
  304.8 12.7 %collective-permute-done.36.refs_7_ = bf16[1024,512]{1,0:T(8,128)(2,1)S(1)} collective-permute-done((bf16[1024,512]{1,0:T(8,128)(2,1)S(1)}, bf16[1024,512]{1,0:T(8,128)(2,1)S(1)}, u32[]{:S(2)}, u32[]{:S(2)}) %collective-permute-start.36) | collective-permute-done | bytes 1048608 | tf_op jit(solution)/shard_map/ppermute | solution.py:312
  318.5 14.5 %shard_map.215 = bf16[4,1024,512]{2,1,0:T(8,128)(2,1)} custom-call(s32[1]{0:T(128)} %bitcast.48.side, bf16[1024,1024]{1,0:T(8,128)(2,1)S(1)} %copy-done.8, bf16[1024,1024]{1,0:T(8,128)(2,1)S(1)} %copy-done.9, bf16[1024,2048]{1,0:T(8,128)(2,1)} %fusion.right_here.target, bf16[1024,2048]{1,0:T(8,128)(2,1)} %bitcast.288), custom_call_target="tpu_custom_call" | custom-call | flops 8589934592 | bytes 16777216 | tf_op jit(solution)/shard_map/pallas_call | solution.py:623
  333.1 22.3 %shard_map.216 = (bf16[1024,2048]{1,0:T(8,128)(2,1)}, bf16[1024,2048]{1,0:T(8,128)(2,1)}) custom-call(s32[4]{0:T(128)} %fusion.60.places, bf16[1024,2048]{1,0:T(8,128)(2,1)} %bitcast.289, bf16[1024,1024]{1,0:T(8,128)(2,1)} %get-tuple-element.260.slope_gate, bf16[1024,1024]{1,0:T(8,128)(2,1)} %get-tuple-element.261.slope_up, ...), custom_call_target="tpu_custom_call" | custom-call | flops 12884901888 | bytes 29360128 | tf_op jit(solution)/shard_map/pallas_call | solution.py:558
  355.8 22.6 %shard_map.217 = (bf16[1024,2048]{1,0:T(8,128)(2,1)}, bf16[1024,2048]{1,0:T(8,128)(2,1)}) custom-call(s32[4]{0:T(128)} %fusion.60.places, bf16[1024,2048]{1,0:T(8,128)(2,1)} %fusion.right_here.target, bf16[1024,1024]{1,0:T(8,128)(2,1)} %get-tuple-element.268.slope_gate, bf16[1024,1024]{1,0:T(8,128)(2,1)} %get-tuple-element.269.slope_up, ...), custom_call_target="tpu_custom_call" | custom-call | flops 12884901888 | bytes 29360128 | tf_op jit(solution)/shard_map/pallas_call | solution.py:558
  382.8 2.9 fusion.19
  386.4 12.4 %shard_map.218 = bf16[4,512,1024]{2,1,0:T(8,128)(2,1)S(1)} custom-call(s32[1]{0:T(128)} %bitcast.48.side, bf16[1024,2048]{1,0:T(8,128)(2,1)} %bitcast.41.normed.left_here, bf16[1024,2048]{1,0:T(8,128)(2,1)} %bitcast.43.normed.left_away, bf16[1024,2048]{1,0:T(8,128)(2,1)} %get-tuple-element.289.right_here, bf16[1024,2048]{1,0:T(8,128)(2,1)} %get-tuple-element.290.right_away), custom_call_target="tpu_custom_call" | custom-call | flops 8589934592 | bytes 16777216 | tf_op jit(solution)/shard_map/pallas_call | solution.py:623
  400.9 6.0 collective-permute-done.38
  406.8 4.1 collective-permute-done.39
  420.4 6.4 collective-permute-done.40
  437.3 6.1 convolution_convert_fusion.4
  447.6 6.1 convolution_convert_fusion.5
  453.7 12.4 %shard_map.219 = bf16[4,512,1024]{2,1,0:T(8,128)(2,1)S(1)} custom-call(s32[1]{0:T(128)} %bitcast.48.side, bf16[1024,2048]{1,0:T(8,128)(2,1)} %bitcast.41.normed.left_here, bf16[1024,2048]{1,0:T(8,128)(2,1)} %bitcast.43.normed.left_away, bf16[1024,2048]{1,0:T(8,128)(2,1)} %get-tuple-element.289.right_here, bf16[1024,2048]{1,0:T(8,128)(2,1)} %get-tuple-element.290.right_away), custom_call_target="tpu_custom_call" | custom-call | flops 8589934592 | bytes 16777216 | tf_op jit(solution)/shard_map/pallas_call | solution.py:623
  471.0 2.9 fusion.21
  476.8 4.9 collective-permute-done.45
  482.9 7.3 %reduce-scatter.7.cloned.1.call-done = bf16[1,512,1024]{2,1,0:T(8,128)(2,1)} async-done(((bf16[4,512,1024]{2,1,0:T(8,128)(2,1)}), bf16[1,512,1024]{2,1,0:T(8,128)(2,1)}) %reduce-scatter.7.cloned.1.call-update) | async-done | bytes 1048592 | tf_op jit(solution)/shard_map/reduce_scatter | solution.py:643
  498.2 3.6 convolution_convert_fusion.7
  506.6 3.5 convolution_convert_fusion.6
  510.2 5.6 shard_map.220
  520.9 29.9 %shard_map.221 = (bf16[2,2,256,384]{3,2,1,0:T(8,128)(2,1)S(1)}, bf16[2,2,256,384]{3,2,1,0:T(8,128)(2,1)S(1)}) custom-call(s32[4]{0:T(128)S(1)} %copy-done.7, s32[2]{0:T(128)S(1)} %dynamic_slice.153.lengths, bf16[2,2,256,384]{3,2,1,0:T(8,128)(2,1)S(1)} %copy-done.14, bf16[2,2,256,384]{3,2,1,0:T(8,128)(2,1)S(1)} %copy-done.16, ...), custom_call_target="tpu_custom_call" | custom-call | flops 13421772800 | bytes 16777216 | tf_op jit(solution)/shard_map/pallas_call | solution.py:215
  552.3 4.4 convolution_convert_fusion
  557.5 3.5 fusion.29
  568.3 3.0 fusion.23
  575.2 7.0 %shard_map.222 = bf16[4,512,384]{2,1,0:T(8,128)(2,1)S(1)} custom-call(s32[1]{0:T(128)} %bitcast.48.side, bf16[1024,2048]{1,0:T(8,128)(2,1)} %bitcast.95.left_here, bf16[1024,2048]{1,0:T(8,128)(2,1)} %bitcast.96.left_away, bf16[1024,384]{1,0:T(8,128)(2,1)S(1)} %bitcast.267, bf16[1024,384]{1,0:T(8,128)(2,1)S(1)} %bitcast.269), custom_call_target="tpu_custom_call" | custom-call | flops 3221225472 | bytes 11534336 | tf_op jit(solution)/shard_map/pallas_call | solution.py:623
  590.3 8.7 %collective-permute-done.62 = bf16[256,2048]{1,0:T(8,128)(2,1)} collective-permute-done((bf16[256,2048]{1,0:T(8,128)(2,1)}, bf16[256,2048]{1,0:T(8,128)(2,1)}, u32[]{:S(2)}, u32[]{:S(2)}) %collective-permute-start.62) | collective-permute-done | bytes 1048608 | tf_op jit(solution)/shard_map/ppermute | solution.py:312
  608.5 5.2 collective-permute-done.64
  (436 shorter events, 236.6 us)
Async XLA Ops:
  7.2 206.0 %all-gather.3.cloned.1.call-start = ((), (), s32[]{:S(2)}) async-start(), calls=%async_computation.8 | async-start | bytes 5242880 | tf_op jit(solution)/shard_map/all_gather | solution.py:445
  18.2 33.3 %collective-permute-start.9 = (bf16[512,384]{1,0:T(8,128)(2,1)}, bf16[512,384]{1,0:T(8,128)(2,1)}, u32[]{:S(2)}, u32[]{:S(2)}) collective-permute-start(bf16[512,384]{1,0:T(8,128)(2,1)} %pad_maximum_fusion.16), channel_id=1, source_target_pairs={{0,6},{2,4},{4,2},{6,0},{1,7},{3,5},{5,3},{7,1},{8,14},{10,12},{12... | collective-permute-start | bytes 1179656 | tf_op jit(solution)/shard_map/ppermute | solution.py:312
  20.7 27.1 %collective-permute-start.5 = (bf16[256,1024]{1,0:T(8,128)(2,1)}, bf16[256,1024]{1,0:T(8,128)(2,1)}, u32[]{:S(2)}, u32[]{:S(2)}) collective-permute-start(bf16[256,1024]{1,0:T(8,128)(2,1)} %get-tuple-element.196), channel_id=1, source_target_pairs={{0,4},{2,6},{4,0},{6,2},{1,5},{3,7},{5,1},{7,3},{8,12},{10,14},{12... | collective-permute-start | bytes 1572872 | tf_op jit(solution)/shard_map/ppermute | solution.py:312
  26.6 32.3 %collective-permute-start.2 = (bf16[256,1024]{1,0:T(8,128)(2,1)S(1)}, bf16[256,1024]{1,0:T(8,128)(2,1)S(1)}, u32[]{:S(2)}, u32[]{:S(2)}) collective-permute-start(bf16[256,1024]{1,0:T(8,128)(2,1)S(1)} %get-tuple-element.192), channel_id=1, source_target_pairs={{0,4},{2,6},{4,0},{6,2},{1,5},{3,7},{5,1},{7,3},{8,12},{10,14},{12... | collective-permute-start | bytes 1572872 | tf_op jit(solution)/shard_map/ppermute | solution.py:312
  28.1 30.8 %collective-permute-start.4 = (bf16[256,1024]{1,0:T(8,128)(2,1)}, bf16[256,1024]{1,0:T(8,128)(2,1)S(1)}, u32[]{:S(2)}, u32[]{:S(2)}) collective-permute-start(bf16[256,1024]{1,0:T(8,128)(2,1)} %get-tuple-element.196), channel_id=1, source_target_pairs={{0,1},{1,0},{2,3},{3,2},{4,5},{5,4},{6,7},{7,6},{8,9},{9,8},{10,11... | collective-permute-start | bytes 1572872 | tf_op jit(solution)/shard_map/ppermute | solution.py:312
  35.2 34.5 %collective-permute-start.3 = (bf16[256,1024]{1,0:T(8,128)(2,1)}, bf16[256,1024]{1,0:T(8,128)(2,1)S(1)}, u32[]{:S(2)}, u32[]{:S(2)}) collective-permute-start(bf16[256,1024]{1,0:T(8,128)(2,1)} %collective-permute-done.1), channel_id=1, source_target_pairs={{0,4},{2,6},{4,0},{6,2},{1,5},{3,7},{5,1},{7,3},{8,12},{10,14},{12... | collective-permute-start | bytes 1572872 | tf_op jit(solution)/shard_map/ppermute | solution.py:312
  47.8 22.0 %collective-permute-start.6 = (bf16[256,1024]{1,0:T(8,128)(2,1)}, bf16[256,1024]{1,0:T(8,128)(2,1)S(1)}, u32[]{:S(2)}, u32[]{:S(2)}) collective-permute-start(bf16[256,1024]{1,0:T(8,128)(2,1)} %collective-permute-done.5), channel_id=1, source_target_pairs={{0,1},{1,0},{2,3},{3,2},{4,5},{5,4},{6,7},{7,6},{8,9},{9,8},{10,11... | collective-permute-start | bytes 1572872 | tf_op jit(solution)/shard_map/ppermute | solution.py:312
  88.8 26.5 %collective-permute-start.15 = (bf16[128,2048]{1,0:T(8,128)(2,1)S(1)}, bf16[128,2048]{1,0:T(8,128)(2,1)S(1)}, u32[]{:S(2)}, u32[]{:S(2)}) collective-permute-start(bf16[128,2048]{1,0:T(8,128)(2,1)S(1)} %pad_maximum_fusion.13), channel_id=1, source_target_pairs={{0,6},{2,4},{4,2},{6,0},{1,7},{3,5},{5,3},{7,1},{8,14},{10,12},{12... | collective-permute-start | bytes 1572872 | tf_op jit(solution)/shard_map/ppermute | solution.py:312
  90.1 25.2 %collective-permute-start.14 = (bf16[128,2048]{1,0:T(8,128)(2,1)S(1)}, bf16[128,2048]{1,0:T(8,128)(2,1)S(1)}, u32[]{:S(2)}, u32[]{:S(2)}) collective-permute-start(bf16[128,2048]{1,0:T(8,128)(2,1)S(1)} %pad_maximum_fusion.12), channel_id=1, source_target_pairs={{0,4},{2,6},{4,0},{6,2},{1,5},{3,7},{5,1},{7,3},{8,12},{10,14},{12... | collective-permute-start | bytes 1572872 | tf_op jit(solution)/shard_map/ppermute | solution.py:312
  91.5 24.9 %collective-permute-start.11 = (bf16[256,512]{1,0:T(8,128)(2,1)}, bf16[256,512]{1,0:T(8,128)(2,1)}, u32[]{:S(2)}, u32[]{:S(2)}) collective-permute-start(bf16[256,512]{1,0:T(8,128)(2,1)} %get-tuple-element.424), channel_id=1, source_target_pairs={{0,2},{2,0},{4,6},{6,4},{1,3},{3,1},{5,7},{7,5},{8,10},{10,8},{12,... | collective-permute-start | bytes 786440 | tf_op jit(solution)/shard_map/ppermute | solution.py:312
  91.6 28.7 %collective-permute-start.12 = (bf16[256,512]{1,0:T(8,128)(2,1)}, bf16[256,512]{1,0:T(8,128)(2,1)}, u32[]{:S(2)}, u32[]{:S(2)}) collective-permute-start(bf16[256,512]{1,0:T(8,128)(2,1)} %get-tuple-element.423), channel_id=1, source_target_pairs={{0,4},{2,6},{4,0},{6,2},{1,5},{3,7},{5,1},{7,3},{8,12},{10,14},{12... | collective-permute-start | bytes 786440 | tf_op jit(solution)/shard_map/ppermute | solution.py:312
  93.1 32.2 %collective-permute-start.13 = (bf16[256,512]{1,0:T(8,128)(2,1)}, bf16[256,512]{1,0:T(8,128)(2,1)}, u32[]{:S(2)}, u32[]{:S(2)}) collective-permute-start(bf16[256,512]{1,0:T(8,128)(2,1)} %get-tuple-element.422), channel_id=1, source_target_pairs={{0,6},{2,4},{4,2},{6,0},{1,7},{3,5},{5,3},{7,1},{8,14},{10,12},{12... | collective-permute-start | bytes 786440 | tf_op jit(solution)/shard_map/ppermute | solution.py:312
  132.0 279.0 %reduce-scatter.5.cloned.1.call-start = ((), (), s32[]{:S(2)}) async-start(), calls=%async_computation.4 | async-start | bytes 5242880 | tf_op jit(solution)/shard_map/reduce_scatter | solution.py:643
  141.0 25.3 %collective-permute-start.18 = (bf16[2,256,1024]{2,1,0:T(8,128)(2,1)S(1)}, bf16[2,256,1024]{2,1,0:T(8,128)(2,1)S(1)}, u32[]{:S(2)}, u32[]{:S(2)}) collective-permute-start(bf16[2,256,1024]{2,1,0:T(8,128)(2,1)S(1)} %fusion.17), channel_id=1, source_target_pairs={{0,1},{1,0},{2,3},{3,2},{4,5},{5,4},{6,7},{7,6},{8,9},{9,8},{10,11... | collective-permute-start | bytes 3145736 | tf_op jit(solution)/shard_map/ppermute | solution.py:312
  143.0 25.0 %collective-permute-start.17 = (bf16[256,2048]{1,0:T(8,128)(2,1)S(1)}, bf16[256,2048]{1,0:T(8,128)(2,1)S(1)}, u32[]{:S(2)}, u32[]{:S(2)}) collective-permute-start(bf16[256,2048]{1,0:T(8,128)(2,1)S(1)} %fusion.16), channel_id=1, source_target_pairs={{0,4},{2,6},{4,0},{6,2},{1,5},{3,7},{5,1},{7,3},{8,12},{10,14},{12... | collective-permute-start | bytes 3145736 | tf_op jit(solution)/shard_map/ppermute | solution.py:312
  188.5 40.3 %collective-permute-start.28 = (bf16[512,2048]{1,0:T(8,128)(2,1)}, bf16[512,2048]{1,0:T(8,128)(2,1)}, u32[]{:S(2)}, u32[]{:S(2)}) collective-permute-start(bf16[512,2048]{1,0:T(8,128)(2,1)} %pad_maximum_fusion.6), channel_id=1, source_target_pairs={{0,2},{2,0},{4,6},{6,4},{1,3},{3,1},{5,7},{7,5},{8,10},{10,8},{12,... | collective-permute-start | bytes 6291464 | tf_op jit(solution)/shard_map/ppermute | solution.py:312
  193.0 16.0 %collective-permute-start.26 = (bf16[256,1024]{1,0:T(8,128)(2,1)S(1)}, bf16[256,1024]{1,0:T(8,128)(2,1)S(1)}, u32[]{:S(2)}, u32[]{:S(2)}) collective-permute-start(bf16[256,1024]{1,0:T(8,128)(2,1)S(1)} %get-tuple-element.231), channel_id=1, source_target_pairs={{0,4},{2,6},{4,0},{6,2},{1,5},{3,7},{5,1},{7,3},{8,12},{10,14},{12... | collective-permute-start | bytes 1572872 | tf_op jit(solution)/shard_map/ppermute | solution.py:312
  194.6 24.5 %collective-permute-start.23 = (bf16[256,1024]{1,0:T(8,128)(2,1)S(1)}, bf16[256,1024]{1,0:T(8,128)(2,1)S(1)}, u32[]{:S(2)}, u32[]{:S(2)}) collective-permute-start(bf16[256,1024]{1,0:T(8,128)(2,1)S(1)} %get-tuple-element.227), channel_id=1, source_target_pairs={{0,4},{2,6},{4,0},{6,2},{1,5},{3,7},{5,1},{7,3},{8,12},{10,14},{12... | collective-permute-start | bytes 1572872 | tf_op jit(solution)/shard_map/ppermute | solution.py:312
  195.0 24.1 %collective-permute-start.25 = (bf16[256,1024]{1,0:T(8,128)(2,1)S(1)}, bf16[256,1024]{1,0:T(8,128)(2,1)S(1)}, u32[]{:S(2)}, u32[]{:S(2)}) collective-permute-start(bf16[256,1024]{1,0:T(8,128)(2,1)S(1)} %get-tuple-element.231), channel_id=1, source_target_pairs={{0,1},{1,0},{2,3},{3,2},{4,5},{5,4},{6,7},{7,6},{8,9},{9,8},{10,11... | collective-permute-start | bytes 1572872 | tf_op jit(solution)/shard_map/ppermute | solution.py:312
  207.5 21.3 %collective-permute-start.24 = (bf16[256,1024]{1,0:T(8,128)(2,1)S(1)}, bf16[256,1024]{1,0:T(8,128)(2,1)}, u32[]{:S(2)}, u32[]{:S(2)}) collective-permute-start(bf16[256,1024]{1,0:T(8,128)(2,1)S(1)} %collective-permute-done.22), channel_id=1, source_target_pairs={{0,4},{2,6},{4,0},{6,2},{1,5},{3,7},{5,1},{7,3},{8,12},{10,14},{12... | collective-permute-start | bytes 1572872 | tf_op jit(solution)/shard_map/ppermute | solution.py:312
  209.0 19.8 %collective-permute-start.27 = (bf16[256,1024]{1,0:T(8,128)(2,1)S(1)}, bf16[256,1024]{1,0:T(8,128)(2,1)}, u32[]{:S(2)}, u32[]{:S(2)}) collective-permute-start(bf16[256,1024]{1,0:T(8,128)(2,1)S(1)} %collective-permute-done.26), channel_id=1, source_target_pairs={{0,1},{1,0},{2,3},{3,2},{4,5},{5,4},{6,7},{7,6},{8,9},{9,8},{10,11... | collective-permute-start | bytes 1572872 | tf_op jit(solution)/shard_map/ppermute | solution.py:312
  234.1 28.6 %collective-permute-start.29 = (bf16[2,2,256,2048]{3,2,1,0:T(8,128)(2,1)}, bf16[2,2,256,2048]{3,2,1,0:T(8,128)(2,1)}, u32[]{:S(2)}, u32[]{:S(2)}) collective-permute-start(bf16[2,2,256,2048]{3,2,1,0:T(8,128)(2,1)} %bitcast.42), channel_id=1, source_target_pairs={{0,2},{2,0},{4,6},{6,4},{1,3},{3,1},{5,7},{7,5},{8,10},{10,8},{12,... | collective-permute-start | bytes 12582920 | tf_op jit(solution)/shard_map/ppermute | solution.py:312
  234.9 25.7 %collective-permute-start.30 = (bf16[2,256,1024]{2,1,0:T(8,128)(2,1)S(1)}, bf16[2,256,1024]{2,1,0:T(8,128)(2,1)}, u32[]{:S(2)}, u32[]{:S(2)}) collective-permute-start(bf16[2,256,1024]{2,1,0:T(8,128)(2,1)S(1)} %copy-done.33), channel_id=1, source_target_pairs={{0,1},{1,0},{2,3},{3,2},{4,5},{5,4},{6,7},{7,6},{8,9},{9,8},{10,11... | collective-permute-start | bytes 3145736 | tf_op jit(solution)/shard_map/ppermute | solution.py:312
  236.6 26.1 %collective-permute-start.31 = (bf16[2,256,1024]{2,1,0:T(8,128)(2,1)S(1)}, bf16[2,256,1024]{2,1,0:T(8,128)(2,1)}, u32[]{:S(2)}, u32[]{:S(2)}) collective-permute-start(bf16[2,256,1024]{2,1,0:T(8,128)(2,1)S(1)} %copy-done.33), channel_id=1, source_target_pairs={{0,4},{2,6},{4,0},{6,2},{1,5},{3,7},{5,1},{7,3},{8,12},{10,14},{12... | collective-permute-start | bytes 3145736 | tf_op jit(solution)/shard_map/ppermute | solution.py:312
  243.3 36.3 %collective-permute-start.33 = (bf16[1024,512]{1,0:T(8,128)(2,1)S(1)}, bf16[1024,512]{1,0:T(8,128)(2,1)S(1)}, u32[]{:S(2)}, u32[]{:S(2)}) collective-permute-start(bf16[1024,512]{1,0:T(8,128)(2,1)S(1)} %get-tuple-element.383), channel_id=1, source_target_pairs={{0,2},{2,0},{4,6},{6,4},{1,3},{3,1},{5,7},{7,5},{8,10},{10,8},{12,... | collective-permute-start | bytes 3145736 | tf_op jit(solution)/shard_map/ppermute | solution.py:312
  243.3 41.1 %collective-permute-start.34 = (bf16[1024,512]{1,0:T(8,128)(2,1)S(1)}, bf16[1024,512]{1,0:T(8,128)(2,1)}, u32[]{:S(2)}, u32[]{:S(2)}) collective-permute-start(bf16[1024,512]{1,0:T(8,128)(2,1)S(1)} %get-tuple-element.382), channel_id=1, source_target_pairs={{0,4},{2,6},{4,0},{6,2},{1,5},{3,7},{5,1},{7,3},{8,12},{10,14},{12... | collective-permute-start | bytes 3145736 | tf_op jit(solution)/shard_map/ppermute | solution.py:312
  262.7 24.1 %collective-permute-start.32 = (bf16[2,256,1024]{2,1,0:T(8,128)(2,1)}, bf16[2,256,1024]{2,1,0:T(8,128)(2,1)}, u32[]{:S(2)}, u32[]{:S(2)}) collective-permute-start(bf16[2,256,1024]{2,1,0:T(8,128)(2,1)} %collective-permute-done.31), channel_id=1, source_target_pairs={{0,1},{1,0},{2,3},{3,2},{4,5},{5,4},{6,7},{7,6},{8,9},{9,8},{10,11... | collective-permute-start | bytes 3145736 | tf_op jit(solution)/shard_map/ppermute | solution.py:312
  292.6 25.0 %collective-permute-start.36 = (bf16[1024,512]{1,0:T(8,128)(2,1)S(1)}, bf16[1024,512]{1,0:T(8,128)(2,1)S(1)}, u32[]{:S(2)}, u32[]{:S(2)}) collective-permute-start(bf16[1024,512]{1,0:T(8,128)(2,1)S(1)} %get-tuple-element.381), channel_id=1, source_target_pairs={{0,6},{2,4},{4,2},{6,0},{1,7},{3,5},{5,3},{7,1},{8,14},{10,12},{12... | collective-permute-start | bytes 3145736 | tf_op jit(solution)/shard_map/ppermute | solution.py:312
  333.0 157.2 %reduce-scatter.7.cloned.1.call-start = ((), (), s32[]{:S(2)}) async-start(), calls=%async_computation.5 | async-start | bytes 5242880 | tf_op jit(solution)/shard_map/reduce_scatter | solution.py:643
  355.4 23.1 %collective-permute-start.37 = (bf16[2,2,256,2048]{3,2,1,0:T(8,128)(2,1)}, bf16[2,2,256,2048]{3,2,1,0:T(8,128)(2,1)}, u32[]{:S(2)}, u32[]{:S(2)}) collective-permute-start(bf16[2,2,256,2048]{3,2,1,0:T(8,128)(2,1)} %bitcast.317), channel_id=1, source_target_pairs={{0,2},{2,0},{4,6},{6,4},{1,3},{3,1},{5,7},{7,5},{8,10},{10,8},{12,... | collective-permute-start | bytes 12582920 | tf_op jit(solution)/shard_map/ppermute | solution.py:312
  381.4 25.5 %collective-permute-start.38 = (bf16[256,2048]{1,0:T(8,128)(2,1)}, bf16[256,2048]{1,0:T(8,128)(2,1)}, u32[]{:S(2)}, u32[]{:S(2)}) collective-permute-start(bf16[256,2048]{1,0:T(8,128)(2,1)} %fusion.18), channel_id=1, source_target_pairs={{0,4},{2,6},{4,0},{6,2},{1,5},{3,7},{5,1},{7,3},{8,12},{10,14},{12... | collective-permute-start | bytes 3145736 | tf_op jit(solution)/shard_map/ppermute | solution.py:312
  385.8 25.2 %collective-permute-start.39 = (bf16[2,256,1024]{2,1,0:T(8,128)(2,1)}, bf16[2,256,1024]{2,1,0:T(8,128)(2,1)}, u32[]{:S(2)}, u32[]{:S(2)}) collective-permute-start(bf16[2,256,1024]{2,1,0:T(8,128)(2,1)} %fusion.19), channel_id=1, source_target_pairs={{0,1},{1,0},{2,3},{3,2},{4,5},{5,4},{6,7},{7,6},{8,9},{9,8},{10,11... | collective-permute-start | bytes 3145736 | tf_op jit(solution)/shard_map/ppermute | solution.py:312
  400.8 189.5 %reduce-scatter.9.cloned.1.call-start = ((), (), s32[]{:S(2)}) async-start(), calls=%async_computation.6 | async-start | bytes 5242880 | tf_op jit(solution)/shard_map/reduce_scatter | solution.py:643
  443.4 27.6 %collective-permute-start.49 = (bf16[2,2,256,2048]{3,2,1,0:T(8,128)(2,1)}, bf16[2,2,256,2048]{3,2,1,0:T(8,128)(2,1)}, u32[]{:S(2)}, u32[]{:S(2)}) collective-permute-start(bf16[2,2,256,2048]{3,2,1,0:T(8,128)(2,1)} %bitcast.68), channel_id=1, source_target_pairs={{0,2},{2,0},{4,6},{6,4},{1,3},{3,1},{5,7},{7,5},{8,10},{10,8},{12,... | collective-permute-start | bytes 12582920 | tf_op jit(solution)/shard_map/ppermute | solution.py:312
  443.5 24.8 %collective-permute-start.43 = (bf16[256,1024]{1,0:T(8,128)(2,1)S(1)}, bf16[256,1024]{1,0:T(8,128)(2,1)}, u32[]{:S(2)}, u32[]{:S(2)}) collective-permute-start(bf16[256,1024]{1,0:T(8,128)(2,1)S(1)} %get-tuple-element.299), channel_id=1, source_target_pairs={{0,1},{1,0},{2,3},{3,2},{4,5},{5,4},{6,7},{7,6},{8,9},{9,8},{10,11... | collective-permute-start | bytes 1572872 | tf_op jit(solution)/shard_map/ppermute | solution.py:312
  444.0 32.8 %collective-permute-start.44 = (bf16[256,1024]{1,0:T(8,128)(2,1)S(1)}, bf16[256,1024]{1,0:T(8,128)(2,1)}, u32[]{:S(2)}, u32[]{:S(2)}) collective-permute-start(bf16[256,1024]{1,0:T(8,128)(2,1)S(1)} %get-tuple-element.299), channel_id=1, source_target_pairs={{0,4},{2,6},{4,0},{6,2},{1,5},{3,7},{5,1},{7,3},{8,12},{10,14},{12... | collective-permute-start | bytes 1572872 | tf_op jit(solution)/shard_map/ppermute | solution.py:312
  445.5 31.3 %collective-permute-start.46 = (bf16[256,1024]{1,0:T(8,128)(2,1)S(1)}, bf16[256,1024]{1,0:T(8,128)(2,1)}, u32[]{:S(2)}, u32[]{:S(2)}) collective-permute-start(bf16[256,1024]{1,0:T(8,128)(2,1)S(1)} %get-tuple-element.303), channel_id=1, source_target_pairs={{0,1},{1,0},{2,3},{3,2},{4,5},{5,4},{6,7},{7,6},{8,9},{9,8},{10,11... | collective-permute-start | bytes 1572872 | tf_op jit(solution)/shard_map/ppermute | solution.py:312
  447.0 22.7 %collective-permute-start.47 = (bf16[256,1024]{1,0:T(8,128)(2,1)S(1)}, bf16[256,1024]{1,0:T(8,128)(2,1)}, u32[]{:S(2)}, u32[]{:S(2)}) collective-permute-start(bf16[256,1024]{1,0:T(8,128)(2,1)S(1)} %get-tuple-element.303), channel_id=1, source_target_pairs={{0,4},{2,6},{4,0},{6,2},{1,5},{3,7},{5,1},{7,3},{8,12},{10,14},{12... | collective-permute-start | bytes 1572872 | tf_op jit(solution)/shard_map/ppermute | solution.py:312
  497.0 140.0 %reduce-scatter.11.cloned.1.call-start = ((), (), s32[]{:S(2)}) async-start(), calls=%async_computation.7 | async-start | bytes 3276800 | tf_op jit(solution)/shard_map/reduce_scatter | solution.py:643
  515.9 36.4 %collective-permute-start.51 = (bf16[256,2048]{1,0:T(8,128)(2,1)}, bf16[256,2048]{1,0:T(8,128)(2,1)S(1)}, u32[]{:S(2)}, u32[]{:S(2)}) collective-permute-start(bf16[256,2048]{1,0:T(8,128)(2,1)} %fusion.20), channel_id=1, source_target_pairs={{0,4},{2,6},{4,0},{6,2},{1,5},{3,7},{5,1},{7,3},{8,12},{10,14},{12... | collective-permute-start | bytes 3145736 | tf_op jit(solution)/shard_map/ppermute | solution.py:312
  517.3 34.9 %collective-permute-start.52 = (bf16[2,256,1024]{2,1,0:T(8,128)(2,1)}, bf16[2,256,1024]{2,1,0:T(8,128)(2,1)S(1)}, u32[]{:S(2)}, u32[]{:S(2)}) collective-permute-start(bf16[2,256,1024]{2,1,0:T(8,128)(2,1)} %fusion.21), channel_id=1, source_target_pairs={{0,1},{1,0},{2,3},{3,2},{4,5},{5,4},{6,7},{7,6},{8,9},{9,8},{10,11... | collective-permute-start | bytes 3145736 | tf_op jit(solution)/shard_map/ppermute | solution.py:312
  518.9 31.9 %collective-permute-start.56 = (bf16[128,1024]{1,0:T(8,128)(2,1)S(1)}, bf16[128,1024]{1,0:T(8,128)(2,1)S(1)}, u32[]{:S(2)}, u32[]{:S(2)}) collective-permute-start(bf16[128,1024]{1,0:T(8,128)(2,1)S(1)} %get-tuple-element.412), channel_id=1, source_target_pairs={{0,2},{2,0},{4,6},{6,4},{1,3},{3,1},{5,7},{7,5},{8,10},{10,8},{12,... | collective-permute-start | bytes 786440 | tf_op jit(solution)/shard_map/ppermute | solution.py:312
  519.0 31.8 %collective-permute-start.57 = (bf16[128,1024]{1,0:T(8,128)(2,1)S(1)}, bf16[128,1024]{1,0:T(8,128)(2,1)S(1)}, u32[]{:S(2)}, u32[]{:S(2)}) collective-permute-start(bf16[128,1024]{1,0:T(8,128)(2,1)S(1)} %get-tuple-element.411), channel_id=1, source_target_pairs={{0,4},{2,6},{4,0},{6,2},{1,5},{3,7},{5,1},{7,3},{8,12},{10,14},{12... | collective-permute-start | bytes 786440 | tf_op jit(solution)/shard_map/ppermute | solution.py:312
  519.7 32.5 %collective-permute-start.58 = (bf16[128,1024]{1,0:T(8,128)(2,1)S(1)}, bf16[128,1024]{1,0:T(8,128)(2,1)S(1)}, u32[]{:S(2)}, u32[]{:S(2)}) collective-permute-start(bf16[128,1024]{1,0:T(8,128)(2,1)S(1)} %get-tuple-element.410), channel_id=1, source_target_pairs={{0,6},{2,4},{4,2},{6,0},{1,7},{3,5},{5,3},{7,1},{8,14},{10,12},{12... | collective-permute-start | bytes 786440 | tf_op jit(solution)/shard_map/ppermute | solution.py:312
  561.0 25.2 %collective-permute-start.59 = (bf16[256,1024]{1,0:T(8,128)(2,1)}, bf16[256,1024]{1,0:T(8,128)(2,1)}, u32[]{:S(2)}, u32[]{:S(2)}) collective-permute-start(bf16[256,1024]{1,0:T(8,128)(2,1)} %get-tuple-element.322), channel_id=1, source_target_pairs={{0,1},{1,0},{2,3},{3,2},{4,5},{5,4},{6,7},{7,6},{8,9},{9,8},{10,11... | collective-permute-start | bytes 1572872 | tf_op jit(solution)/shard_map/ppermute | solution.py:312
  562.5 23.7 %collective-permute-start.60 = (bf16[256,1024]{1,0:T(8,128)(2,1)}, bf16[256,1024]{1,0:T(8,128)(2,1)}, u32[]{:S(2)}, u32[]{:S(2)}) collective-permute-start(bf16[256,1024]{1,0:T(8,128)(2,1)} %get-tuple-element.323), channel_id=1, source_target_pairs={{0,4},{2,6},{4,0},{6,2},{1,5},{3,7},{5,1},{7,3},{8,12},{10,14},{12... | collective-permute-start | bytes 1572872 | tf_op jit(solution)/shard_map/ppermute | solution.py:312
  571.3 27.6 %collective-permute-start.63 = (bf16[2,256,1024]{2,1,0:T(8,128)(2,1)}, bf16[2,256,1024]{2,1,0:T(8,128)(2,1)}, u32[]{:S(2)}, u32[]{:S(2)}) collective-permute-start(bf16[2,256,1024]{2,1,0:T(8,128)(2,1)} %fusion.23), channel_id=1, source_target_pairs={{0,1},{1,0},{2,3},{3,2},{4,5},{5,4},{6,7},{7,6},{8,9},{9,8},{10,11... | collective-permute-start | bytes 3145736 | tf_op jit(solution)/shard_map/ppermute | solution.py:312
  574.4 24.6 %collective-permute-start.62 = (bf16[256,2048]{1,0:T(8,128)(2,1)}, bf16[256,2048]{1,0:T(8,128)(2,1)}, u32[]{:S(2)}, u32[]{:S(2)}) collective-permute-start(bf16[256,2048]{1,0:T(8,128)(2,1)} %fusion.22), channel_id=1, source_target_pairs={{0,4},{2,6},{4,0},{6,2},{1,5},{3,7},{5,1},{7,3},{8,12},{10,14},{12... | collective-permute-start | bytes 3145736 | tf_op jit(solution)/shard_map/ppermute | solution.py:312
  (107 other events, 812.0 us)
Sparse Core Ops, SparseCore 0:
  132.1 81.0 all-gather.2
  333.1 77.3 reduce-scatter.4
  412.9 77.2 reduce-scatter.6
  497.1 77.3 reduce-scatter.8
  584.2 52.7 reduce-scatter.10
